TPU v7x, 256 devices: a whole 4x4x8 slice. The times are simulated.
256 devices in a mesh: ta: 8 (over z_hi, core), gy: 4 (over x), gx: 8 (over y, z_lo).
Axes of the slice: x: 4, y: 4, z: 8 (z_hi: 4, z_lo: 2; z = z_hi * 2 + z_lo), core: 2. Of those that a mesh axis runs over, the one named last changes fastest.
Arguments:
- residual: bfloat16 [524288], P(('ta', 'gy', 'gx')), may hold values from -6 to 6
- footprint: bfloat16 [524288, 1024], P(('ta', 'gy', 'gx')), may hold values from 0.0099487305 to 1
- tile_id: int32 [524288, 1], P(('ta', 'gy', 'gx')), may hold values from 0 to 31; in each aligned block of 2048 rows (0 to 2047, 2048 to 4095, ...) at most 128 rows name the same one
- step_id: int32 [524288], P(('ta', 'gy', 'gx')), may hold values from 0 to 3
- block_id: int32 [524288], P(('ta', 'gy', 'gx')), may hold values from 0 to 15
- sigma: float32 [4, 256, 2048], P(None, 'gy', 'gx'), may hold values from 0.3 to 3
- taps: float32 [4, 5], replicated, may hold values from 0.05 to 0.4
- diffusivity: float32 [256, 2048], P('gy', 'gx'), may hold values from 0.03 to 0.24
Outputs:
- increment: float32 [4, 32, 256, 2048], P(None, 'ta', 'gy', 'gx')
Inputs may be any that keep to these rules, and one draw needn't show every extreme that they name: `tile_id`: among the rows of one device at most 128 soundings name the same tile; some device reaches 128 in every draw. `block_id`: blocks are numbered row-major over 8 x 2 blocks of a tile.
All inputs are finite; a program needn't handle non-finite values.
Results may differ from a plain program's by a relative error of at most 0.006.
Values may be sent and summed in bfloat16 or wider, within the bound.
No kernel may reach another device: no remote copies, remote signals or barrier semaphores. Data moves between devices by JAX's collectives and lax.ppermute only.
A program may use at most 64 MiB of HBM per device.

v0:
```python
import jax
import jax.numpy as jnp
from jax import lax
from jax.sharding import PartitionSpec as P

TS_DEV = 4
TRACERS = 4
BLK_LAT = 8
BLK_LON = 128
HB = 2
KSTEPS = 4
CAP = 128


def padded_2(block, sides, width, periodic):
    for axis, dim in sides:
        count = lax.axis_size(axis)
        forward = [(i, i + 1) for i in range(count - 1)]
        if periodic:
            forward.append((count - 1, 0))
        backward = [(target, source) for source, target in forward]
        low = lax.ppermute(
            lax.slice_in_dim(block, block.shape[dim] - width, None, axis=dim), axis, forward
        )
        high = lax.ppermute(lax.slice_in_dim(block, 0, width, axis=dim), axis, backward)
        block = jnp.concatenate([low, block, high], axis=dim)
    return block


def per_device(residual, footprint, tile_id, step_id, block_id, sigma, taps, diffusivity):
    lat_dev = sigma.shape[1]
    lon_dev = sigma.shape[2]
    fp_cells = footprint.shape[1]
    block_rows = lat_dev // BLK_LAT
    block_cols = lon_dev // BLK_LON
    bins_dev = TS_DEV * block_rows * block_cols
    tiles = lax.axis_size("gy") * lax.axis_size("gx")
    contrib = (residual.astype(jnp.float32)[:, None] * footprint.astype(jnp.float32)).astype(
        jnp.bfloat16
    )
    dest = tile_id[:, 0]
    local_bin = step_id * (block_rows * block_cols) + block_id
    hits = (dest[:, None] == jnp.arange(tiles, dtype=jnp.int32)[None, :]).astype(jnp.int32)
    rank = jnp.sum((jnp.cumsum(hits, axis=0) - 1) * hits, axis=1)
    target = dest * CAP + rank
    send_rows = jnp.zeros((tiles * CAP, fp_cells), jnp.bfloat16).at[target].set(contrib)
    send_bins = jnp.full((tiles * CAP,), -1, jnp.int32).at[target].set(local_bin)
    got_rows, got_bins = (
        lax.all_to_all(
            send_rows.reshape(tiles, CAP, fp_cells),
            ("gy", "gx"),
            split_axis=0,
            concat_axis=0,
            tiled=True,
        ),
        lax.all_to_all(
            send_bins.reshape(tiles, CAP), ("gy", "gx"), split_axis=0, concat_axis=0, tiled=True
        ),
    )
    selector = (
        jnp.arange(bins_dev, dtype=jnp.int32)[None, :, None] == got_bins[:, None, :]
    ).astype(jnp.bfloat16)
    partial_value = jnp.einsum(
        "sbc,scf->sbf", selector, got_rows, preferred_element_type=jnp.float32
    )
    rounded = lax.optimization_barrier(partial_value.astype(jnp.bfloat16))
    summed = jnp.sum(rounded.astype(jnp.float32), axis=0)
    adjoint = summed.reshape(TS_DEV, block_rows, block_cols, BLK_LAT, BLK_LON)
    adjoint = adjoint.transpose(0, 1, 3, 2, 4).reshape(TS_DEV, lat_dev, lon_dev)
    padded = padded_2(adjoint.astype(jnp.bfloat16), (("ta", 0),), HB, False).astype(adjoint.dtype)
    banded = jnp.zeros((TRACERS, TS_DEV, lat_dev, lon_dev), jnp.float32)
    for offset in range(2 * HB + 1):
        banded = (
            banded + taps[:, offset][:, None, None, None] * padded[None, offset : offset + TS_DEV]
        )
    field = sigma[:, None] * banded
    for sweep in range(KSTEPS):
        wide_lon = padded_2(field.astype(jnp.bfloat16), (("gx", 3),), 1, True).astype(field.dtype)
        wide_lat = padded_2(field.astype(jnp.bfloat16), (("gy", 2),), 1, False).astype(field.dtype)
        beside_all = (
            wide_lon[:, :, :, 2:]
            + wide_lon[:, :, :, :-2]
            + wide_lat[:, :, 2:]
            + wide_lat[:, :, :-2]
        )
        field = field + diffusivity * (beside_all - 4.0 * field)
    return sigma[:, None] * field


def solution(mesh):
    return jax.shard_map(
        per_device,
        mesh=mesh,
        in_specs=(
            P(("ta", "gy", "gx")),
            P(("ta", "gy", "gx"), None),
            P(("ta", "gy", "gx"), None),
            P(("ta", "gy", "gx")),
            P(("ta", "gy", "gx")),
            P(None, "gy", "gx"),
            P(),
            P("gy", "gx"),
        ),
        out_specs=P(None, "ta", "gy", "gx"),
        check_vma=False,
    )
```

profile of v0, /device:TPU:128, one launch (start us, length us, event | category | flops | bytes accessed | tf_op | source)
XLA Modules:
  0.0 227.4 jit_solution(11564460564867087882)
XLA Ops:
  0.8 9.1 %reduce-window.6 = s32[32,16,128]{2,1,0:T(8,128)S(1)} reduce-window(s32[32,16,128]{2,1,0:T(8,128)S(1)} %fusion.20, s32[]{:T(128)} %constant.9.clone.1), window={size=1x1x128 pad=0_0x0_0x127_0}, to_apply=%region_0.0 | reduce-window | flops 8323072 | bytes 524292 | tf_op jit(solution)/shard_map/reduce-window
  10.8 8.6 %scatter_custom_fusion = s32[4096]{0:T(1024)} fusion(s32[2048]{0:T(1024)S(1)} %bitcast.47, s32[2048]{0:T(1024)S(1)} %multiply_add_fusion, s32[]{:T(128)} %constant.7.clone.1), kind=kCustom, calls=%fused_computation.56 | custom fusion | bytes 16388 | tf_op jit(solution)/shard_map/scatter | solution.py:47
  19.4 7.8 %all-to-all-start = ((s32[32,1,128]{2,1,0:T(1,128)}), s32[32,1,128]{2,1,0:T(1,128)S(1)}, u32[]{:S(2)}, u32[]{:S(2)}) async-start(s32[32,1,128]{2,1,0:T(1,128)} %bitcast.7), calls=%async_computation | async-start | bytes 32768 | tf_op jit(solution)/shard_map/all_to_all | solution.py:56
  27.2 15.8 %scatter_custom_fusion.1 = bf16[4096,1024]{1,0:T(8,128)(2,1)} fusion(s32[2048]{0:T(1024)S(1)} %bitcast.48, bf16[2048,1024]{1,0:T(8,128)(2,1)} %param.9, f32[2048]{0:T(1024)S(1)} %convert_element_type.73, bf16[]{:T(256)} %constant.6.clone.1), kind=kCustom, calls=%fused_computation.3 | custom fusion | flops 6291456 | bytes 12591106 | tf_op jit(solution)/shard_map/scatter | solution.py:46
  43.0 104.2 %all_to_all.14 = bf16[32,128,1024]{2,1,0:T(8,128)(2,1)S(1)} all-to-all(bf16[32,128,1024]{2,1,0:T(8,128)(2,1)} %bitcast.36), channel_id=1, replica_groups=mesh['ta'=8,'gy'=4,'gx'=8] {'gy','gx'}, dimensions={0} | all-to-all | bytes 16777216 | tf_op jit(solution)/shard_map/all_to_all | solution.py:49
  147.2 3.2 %convolution_convert_fusion = bf16[32,64,1024]{2,1,0:T(8,128)(2,1)} fusion(bf16[32,128,1024]{2,1,0:T(8,128)(2,1)S(1)} %all_to_all.14, s32[32,128]{1,0:T(8,128)S(1)} %bitcast.43), kind=kOutput, calls=%fused_computation.6 | convolution fusion | flops 539230208 | bytes 12599296 | tf_op jit(solution)/shard_map/sbc,scf->sbf/dot_general | solution.py:63
  150.4 3.1 %reduce_sum.25 = bf16[64,1024]{1,0:T(8,128)(2,1)S(1)} reduce(bf16[32,64,1024]{2,1,0:T(8,128)(2,1)} %convolution_convert_fusion, bf16[]{:T(256)} %constant.6.clone.1), dimensions={0}, to_apply=%region_5.6 | reduce | flops 2031616 | bytes 4325378 | tf_op jit(solution)/shard_map/reduce_sum | solution.py:67
  153.6 1.9 collective-permute-start
  155.5 5.9 %collective-permute-start.1 = (bf16[2,64,256]{2,1,0:T(8,128)(2,1)S(1)}, bf16[2,64,256]{2,1,0:T(8,128)(2,1)S(1)}, u32[]{:S(2)}, u32[]{:S(2)}) collective-permute-start(bf16[2,64,256]{2,1,0:T(8,128)(2,1)S(1)} %get-tuple-element.38), channel_id=1, source_target_pairs={{32,0},{64,32},{96,64},{128,96},{160,128},{192,160},{224,192},{33,... | collective-permute-start | bytes 196616 | tf_op jit(solution)/shard_map/ppermute | solution.py:25
  161.7 2.0 collective-permute-done.1
  165.4 4.0 %collective-permute-start.3 = (bf16[4,4,64,1]{3,2,1,0:T(8,128)(2,1)S(1)}, bf16[4,4,64,1]{3,2,1,0:T(8,128)(2,1)S(1)}, u32[]{:S(2)}, u32[]{:S(2)}) collective-permute-start(bf16[4,4,64,1]{3,2,1,0:T(8,128)(2,1)S(1)} %get-tuple-element.29), channel_id=1, source_target_pairs={{1,0},{2,1},{3,2},{4,3},{5,4},{6,5},{7,6},{0,7},{9,8},{10,9},{11,1... | collective-permute-start | bytes 6152 | tf_op jit(solution)/shard_map/ppermute | solution.py:25
  169.5 1.3 collective-permute-start.4
  170.8 1.4 collective-permute-start.5
  172.2 4.4 %collective-permute-done.2 = bf16[4,4,64,1]{3,2,1,0:T(8,128)(2,1)S(1)} collective-permute-done((bf16[4,4,64,1]{3,2,1,0:T(8,128)(2,1)S(1)}, bf16[4,4,64,1]{3,2,1,0:T(8,128)(2,1)S(1)}, u32[]{:S(2)}, u32[]{:S(2)}) %collective-permute-start.2) | collective-permute-done | bytes 2080 | tf_op jit(solution)/shard_map/ppermute | solution.py:22
  176.6 2.8 %collective-permute-done.3 = bf16[4,4,64,1]{3,2,1,0:T(8,128)(2,1)S(1)} collective-permute-done((bf16[4,4,64,1]{3,2,1,0:T(8,128)(2,1)S(1)}, bf16[4,4,64,1]{3,2,1,0:T(8,128)(2,1)S(1)}, u32[]{:S(2)}, u32[]{:S(2)}) %collective-permute-start.3) | collective-permute-done | bytes 2080 | tf_op jit(solution)/shard_map/ppermute | solution.py:25
  180.1 0.8 fusion.27
  181.4 3.9 %collective-permute-start.7 = (bf16[4,4,64,1]{3,2,1,0:T(8,128)(2,1)S(1)}, bf16[4,4,64,1]{3,2,1,0:T(8,128)(2,1)S(1)}, u32[]{:S(2)}, u32[]{:S(2)}) collective-permute-start(bf16[4,4,64,1]{3,2,1,0:T(8,128)(2,1)S(1)} %get-tuple-element.25), channel_id=1, source_target_pairs={{1,0},{2,1},{3,2},{4,3},{5,4},{6,5},{7,6},{0,7},{9,8},{10,9},{11,1... | collective-permute-start | bytes 6152 | tf_op jit(solution)/shard_map/ppermute | solution.py:25
  185.3 2.3 %collective-permute-start.8 = (bf16[4,4,1,256]{3,2,1,0:T(2,128)(2,1)S(1)}, bf16[4,4,1,256]{3,2,1,0:T(2,128)(2,1)S(1)}, u32[]{:S(2)}, u32[]{:S(2)}) collective-permute-start(bf16[4,4,1,256]{3,2,1,0:T(2,128)(2,1)S(1)} %get-tuple-element.26), channel_id=1, source_target_pairs={{0,8},{8,16},{16,24},{1,9},{9,17},{17,25},{2,10},{10,18},{18,26},{... | collective-permute-start | bytes 24584 | tf_op jit(solution)/shard_map/ppermute | solution.py:22
  187.6 1.3 collective-permute-start.9
  188.9 3.5 %collective-permute-done.6 = bf16[4,4,64,1]{3,2,1,0:T(8,128)(2,1)S(1)} collective-permute-done((bf16[4,4,64,1]{3,2,1,0:T(8,128)(2,1)S(1)}, bf16[4,4,64,1]{3,2,1,0:T(8,128)(2,1)S(1)}, u32[]{:S(2)}, u32[]{:S(2)}) %collective-permute-start.6) | collective-permute-done | bytes 2080 | tf_op jit(solution)/shard_map/ppermute | solution.py:22
  192.4 2.4 %collective-permute-done.7 = bf16[4,4,64,1]{3,2,1,0:T(8,128)(2,1)S(1)} collective-permute-done((bf16[4,4,64,1]{3,2,1,0:T(8,128)(2,1)S(1)}, bf16[4,4,64,1]{3,2,1,0:T(8,128)(2,1)S(1)}, u32[]{:S(2)}, u32[]{:S(2)}) %collective-permute-start.7) | collective-permute-done | bytes 2080 | tf_op jit(solution)/shard_map/ppermute | solution.py:25
  196.7 3.7 %collective-permute-start.11 = (bf16[4,4,64,1]{3,2,1,0:T(8,128)(2,1)S(1)}, bf16[4,4,64,1]{3,2,1,0:T(8,128)(2,1)S(1)}, u32[]{:S(2)}, u32[]{:S(2)}) collective-permute-start(bf16[4,4,64,1]{3,2,1,0:T(8,128)(2,1)S(1)} %get-tuple-element.21), channel_id=1, source_target_pairs={{1,0},{2,1},{3,2},{4,3},{5,4},{6,5},{7,6},{0,7},{9,8},{10,9},{11,1... | collective-permute-start | bytes 6152 | tf_op jit(solution)/shard_map/ppermute | solution.py:25
  200.4 2.6 %collective-permute-start.12 = (bf16[4,4,1,256]{3,2,1,0:T(2,128)(2,1)S(1)}, bf16[4,4,1,256]{3,2,1,0:T(2,128)(2,1)S(1)}, u32[]{:S(2)}, u32[]{:S(2)}) collective-permute-start(bf16[4,4,1,256]{3,2,1,0:T(2,128)(2,1)S(1)} %get-tuple-element.22), channel_id=1, source_target_pairs={{0,8},{8,16},{16,24},{1,9},{9,17},{17,25},{2,10},{10,18},{18,26},{... | collective-permute-start | bytes 24584 | tf_op jit(solution)/shard_map/ppermute | solution.py:22
  203.0 1.3 collective-permute-start.13
  204.3 3.3 %collective-permute-done.10 = bf16[4,4,64,1]{3,2,1,0:T(8,128)(2,1)S(1)} collective-permute-done((bf16[4,4,64,1]{3,2,1,0:T(8,128)(2,1)S(1)}, bf16[4,4,64,1]{3,2,1,0:T(8,128)(2,1)S(1)}, u32[]{:S(2)}, u32[]{:S(2)}) %collective-permute-start.10) | collective-permute-done | bytes 2080 | tf_op jit(solution)/shard_map/ppermute | solution.py:22
  209.5 1.6 collective-permute-start.14
  211.2 2.6 %collective-permute-start.15 = (bf16[4,4,64,1]{3,2,1,0:T(8,128)(2,1)S(1)}, bf16[4,4,64,1]{3,2,1,0:T(8,128)(2,1)S(1)}, u32[]{:S(2)}, u32[]{:S(2)}) collective-permute-start(bf16[4,4,64,1]{3,2,1,0:T(8,128)(2,1)S(1)} %get-tuple-element.17), channel_id=1, source_target_pairs={{1,0},{2,1},{3,2},{4,3},{5,4},{6,5},{7,6},{0,7},{9,8},{10,9},{11,1... | collective-permute-start | bytes 6152 | tf_op jit(solution)/shard_map/ppermute | solution.py:25
  213.8 2.6 %collective-permute-start.16 = (bf16[4,4,1,256]{3,2,1,0:T(2,128)(2,1)S(1)}, bf16[4,4,1,256]{3,2,1,0:T(2,128)(2,1)S(1)}, u32[]{:S(2)}, u32[]{:S(2)}) collective-permute-start(bf16[4,4,1,256]{3,2,1,0:T(2,128)(2,1)S(1)} %get-tuple-element.18), channel_id=1, source_target_pairs={{0,8},{8,16},{16,24},{1,9},{9,17},{17,25},{2,10},{10,18},{18,26},{... | collective-permute-start | bytes 24584 | tf_op jit(solution)/shard_map/ppermute | solution.py:22
  216.4 1.3 collective-permute-start.17
  217.7 3.0 %collective-permute-done.14 = bf16[4,4,64,1]{3,2,1,0:T(8,128)(2,1)S(1)} collective-permute-done((bf16[4,4,64,1]{3,2,1,0:T(8,128)(2,1)S(1)}, bf16[4,4,64,1]{3,2,1,0:T(8,128)(2,1)S(1)}, u32[]{:S(2)}, u32[]{:S(2)}) %collective-permute-start.14) | collective-permute-done | bytes 2080 | tf_op jit(solution)/shard_map/ppermute | solution.py:22
  220.8 4.5 %collective-permute-done.15 = bf16[4,4,64,1]{3,2,1,0:T(8,128)(2,1)S(1)} collective-permute-done((bf16[4,4,64,1]{3,2,1,0:T(8,128)(2,1)S(1)}, bf16[4,4,64,1]{3,2,1,0:T(8,128)(2,1)S(1)}, u32[]{:S(2)}, u32[]{:S(2)}) %collective-permute-start.15) | collective-permute-done | bytes 2080 | tf_op jit(solution)/shard_map/ppermute | solution.py:25
  225.9 1.5 fusion.6
  (61 shorter events, 9.2 us)
Async XLA Ops:
  0.0 10.6 %copy-start.2 = (s32[2048,1]{0,1:T(1,128)S(1)}, s32[2048,1]{0,1:T(1,128)}, u32[]{:S(2)}) copy-start(s32[2048,1]{0,1:T(1,128)} %param.10) | copy-start | bytes 24580
  0.0 10.7 %copy-start.5 = (s32[2048]{0:T(1024)S(1)}, s32[2048]{0:T(1024)}, u32[]{:S(2)}) copy-start(s32[2048]{0:T(1024)} %param.11) | copy-start | bytes 24580
  0.0 10.7 %copy-start.4 = (s32[2048]{0:T(1024)S(1)}, s32[2048]{0:T(1024)}, u32[]{:S(2)}) copy-start(s32[2048]{0:T(1024)} %param.12) | copy-start | bytes 24580
  0.0 27.2 %copy-start.6 = (bf16[2048]{0:T(1024)(128)(2,1)S(1)}, bf16[2048]{0:T(1024)(128)(2,1)}, u32[]{:S(2)}) copy-start(bf16[2048]{0:T(1024)(128)(2,1)} %param.8) | copy-start | bytes 12292
  19.4 23.6 %all-to-all-start = ((s32[32,1,128]{2,1,0:T(1,128)}), s32[32,1,128]{2,1,0:T(1,128)S(1)}, u32[]{:S(2)}, u32[]{:S(2)}) async-start(s32[32,1,128]{2,1,0:T(1,128)} %bitcast.7), calls=%async_computation | async-start | bytes 32768 | tf_op jit(solution)/shard_map/all_to_all | solution.py:56
  150.4 11.1 %copy-start.3 = (f32[4,5]{1,0:T(4,128)S(1)}, f32[4,5]{1,0:T(4,128)}, u32[]{:S(2)}) copy-start(f32[4,5]{1,0:T(4,128)} %param.14) | copy-start | bytes 244
  153.6 8.1 %collective-permute-start = (bf16[2,64,256]{2,1,0:T(8,128)(2,1)S(1)}, bf16[2,64,256]{2,1,0:T(8,128)(2,1)S(1)}, u32[]{:S(2)}, u32[]{:S(2)}) collective-permute-start(bf16[2,64,256]{2,1,0:T(8,128)(2,1)S(1)} %get-tuple-element.37), channel_id=1, source_target_pairs={{0,32},{32,64},{64,96},{96,128},{128,160},{160,192},{192,224},{1,3... | collective-permute-start | bytes 196616 | tf_op jit(solution)/shard_map/ppermute | solution.py:22
  155.5 8.2 %collective-permute-start.1 = (bf16[2,64,256]{2,1,0:T(8,128)(2,1)S(1)}, bf16[2,64,256]{2,1,0:T(8,128)(2,1)S(1)}, u32[]{:S(2)}, u32[]{:S(2)}) collective-permute-start(bf16[2,64,256]{2,1,0:T(8,128)(2,1)S(1)} %get-tuple-element.38), channel_id=1, source_target_pairs={{32,0},{64,32},{96,64},{128,96},{160,128},{192,160},{224,192},{33,... | collective-permute-start | bytes 196616 | tf_op jit(solution)/shard_map/ppermute | solution.py:25
  163.7 0.9 copy-start
  165.2 11.4 %collective-permute-start.2 = (bf16[4,4,64,1]{3,2,1,0:T(8,128)(2,1)S(1)}, bf16[4,4,64,1]{3,2,1,0:T(8,128)(2,1)S(1)}, u32[]{:S(2)}, u32[]{:S(2)}) collective-permute-start(bf16[4,4,64,1]{3,2,1,0:T(8,128)(2,1)S(1)} %get-tuple-element.28), channel_id=1, source_target_pairs={{0,1},{1,2},{2,3},{3,4},{4,5},{5,6},{6,7},{7,0},{8,9},{9,10},{10,1... | collective-permute-start | bytes 6152 | tf_op jit(solution)/shard_map/ppermute | solution.py:22
  165.4 14.0 %collective-permute-start.3 = (bf16[4,4,64,1]{3,2,1,0:T(8,128)(2,1)S(1)}, bf16[4,4,64,1]{3,2,1,0:T(8,128)(2,1)S(1)}, u32[]{:S(2)}, u32[]{:S(2)}) collective-permute-start(bf16[4,4,64,1]{3,2,1,0:T(8,128)(2,1)S(1)} %get-tuple-element.29), channel_id=1, source_target_pairs={{1,0},{2,1},{3,2},{4,3},{5,4},{6,5},{7,6},{0,7},{9,8},{10,9},{11,1... | collective-permute-start | bytes 6152 | tf_op jit(solution)/shard_map/ppermute | solution.py:25
  169.5 10.4 %collective-permute-start.4 = (bf16[4,4,1,256]{3,2,1,0:T(2,128)(2,1)S(1)}, bf16[4,4,1,256]{3,2,1,0:T(2,128)(2,1)S(1)}, u32[]{:S(2)}, u32[]{:S(2)}) collective-permute-start(bf16[4,4,1,256]{3,2,1,0:T(2,128)(2,1)S(1)} %get-tuple-element.30), channel_id=1, source_target_pairs={{0,8},{8,16},{16,24},{1,9},{9,17},{17,25},{2,10},{10,18},{18,26},{... | collective-permute-start | bytes 24584 | tf_op jit(solution)/shard_map/ppermute | solution.py:22
  170.8 9.3 %copy-start.1 = (f32[64,256]{1,0:T(8,128)S(1)}, f32[64,256]{1,0:T(8,128)}, u32[]{:S(2)}) copy-start(f32[64,256]{1,0:T(8,128)} %param.15) | copy-start | bytes 196612
  170.8 9.1 %collective-permute-start.5 = (bf16[4,4,1,256]{3,2,1,0:T(2,128)(2,1)S(1)}, bf16[4,4,1,256]{3,2,1,0:T(2,128)(2,1)S(1)}, u32[]{:S(2)}, u32[]{:S(2)}) collective-permute-start(bf16[4,4,1,256]{3,2,1,0:T(2,128)(2,1)S(1)} %get-tuple-element.31), channel_id=1, source_target_pairs={{8,0},{16,8},{24,16},{9,1},{17,9},{25,17},{10,2},{18,10},{26,18},{... | collective-permute-start | bytes 24584 | tf_op jit(solution)/shard_map/ppermute | solution.py:25
  181.0 11.4 %collective-permute-start.6 = (bf16[4,4,64,1]{3,2,1,0:T(8,128)(2,1)S(1)}, bf16[4,4,64,1]{3,2,1,0:T(8,128)(2,1)S(1)}, u32[]{:S(2)}, u32[]{:S(2)}) collective-permute-start(bf16[4,4,64,1]{3,2,1,0:T(8,128)(2,1)S(1)} %get-tuple-element.24), channel_id=1, source_target_pairs={{0,1},{1,2},{2,3},{3,4},{4,5},{5,6},{6,7},{7,0},{8,9},{9,10},{10,1... | collective-permute-start | bytes 6152 | tf_op jit(solution)/shard_map/ppermute | solution.py:22
  181.4 13.4 %collective-permute-start.7 = (bf16[4,4,64,1]{3,2,1,0:T(8,128)(2,1)S(1)}, bf16[4,4,64,1]{3,2,1,0:T(8,128)(2,1)S(1)}, u32[]{:S(2)}, u32[]{:S(2)}) collective-permute-start(bf16[4,4,64,1]{3,2,1,0:T(8,128)(2,1)S(1)} %get-tuple-element.25), channel_id=1, source_target_pairs={{1,0},{2,1},{3,2},{4,3},{5,4},{6,5},{7,6},{0,7},{9,8},{10,9},{11,1... | collective-permute-start | bytes 6152 | tf_op jit(solution)/shard_map/ppermute | solution.py:25
  185.3 10.0 %collective-permute-start.8 = (bf16[4,4,1,256]{3,2,1,0:T(2,128)(2,1)S(1)}, bf16[4,4,1,256]{3,2,1,0:T(2,128)(2,1)S(1)}, u32[]{:S(2)}, u32[]{:S(2)}) collective-permute-start(bf16[4,4,1,256]{3,2,1,0:T(2,128)(2,1)S(1)} %get-tuple-element.26), channel_id=1, source_target_pairs={{0,8},{8,16},{16,24},{1,9},{9,17},{17,25},{2,10},{10,18},{18,26},{... | collective-permute-start | bytes 24584 | tf_op jit(solution)/shard_map/ppermute | solution.py:22
  187.6 7.7 %collective-permute-start.9 = (bf16[4,4,1,256]{3,2,1,0:T(2,128)(2,1)S(1)}, bf16[4,4,1,256]{3,2,1,0:T(2,128)(2,1)S(1)}, u32[]{:S(2)}, u32[]{:S(2)}) collective-permute-start(bf16[4,4,1,256]{3,2,1,0:T(2,128)(2,1)S(1)} %get-tuple-element.27), channel_id=1, source_target_pairs={{8,0},{16,8},{24,16},{9,1},{17,9},{25,17},{10,2},{18,10},{26,18},{... | collective-permute-start | bytes 24584 | tf_op jit(solution)/shard_map/ppermute | solution.py:25
  196.2 11.4 %collective-permute-start.10 = (bf16[4,4,64,1]{3,2,1,0:T(8,128)(2,1)S(1)}, bf16[4,4,64,1]{3,2,1,0:T(8,128)(2,1)S(1)}, u32[]{:S(2)}, u32[]{:S(2)}) collective-permute-start(bf16[4,4,64,1]{3,2,1,0:T(8,128)(2,1)S(1)} %get-tuple-element.20), channel_id=1, source_target_pairs={{0,1},{1,2},{2,3},{3,4},{4,5},{5,6},{6,7},{7,0},{8,9},{9,10},{10,1... | collective-permute-start | bytes 6152 | tf_op jit(solution)/shard_map/ppermute | solution.py:22
  196.7 11.5 %collective-permute-start.11 = (bf16[4,4,64,1]{3,2,1,0:T(8,128)(2,1)S(1)}, bf16[4,4,64,1]{3,2,1,0:T(8,128)(2,1)S(1)}, u32[]{:S(2)}, u32[]{:S(2)}) collective-permute-start(bf16[4,4,64,1]{3,2,1,0:T(8,128)(2,1)S(1)} %get-tuple-element.21), channel_id=1, source_target_pairs={{1,0},{2,1},{3,2},{4,3},{5,4},{6,5},{7,6},{0,7},{9,8},{10,9},{11,1... | collective-permute-start | bytes 6152 | tf_op jit(solution)/shard_map/ppermute | solution.py:25
  200.4 8.2 %collective-permute-start.12 = (bf16[4,4,1,256]{3,2,1,0:T(2,128)(2,1)S(1)}, bf16[4,4,1,256]{3,2,1,0:T(2,128)(2,1)S(1)}, u32[]{:S(2)}, u32[]{:S(2)}) collective-permute-start(bf16[4,4,1,256]{3,2,1,0:T(2,128)(2,1)S(1)} %get-tuple-element.22), channel_id=1, source_target_pairs={{0,8},{8,16},{16,24},{1,9},{9,17},{17,25},{2,10},{10,18},{18,26},{... | collective-permute-start | bytes 24584 | tf_op jit(solution)/shard_map/ppermute | solution.py:22
  203.0 5.6 %collective-permute-start.13 = (bf16[4,4,1,256]{3,2,1,0:T(2,128)(2,1)S(1)}, bf16[4,4,1,256]{3,2,1,0:T(2,128)(2,1)S(1)}, u32[]{:S(2)}, u32[]{:S(2)}) collective-permute-start(bf16[4,4,1,256]{3,2,1,0:T(2,128)(2,1)S(1)} %get-tuple-element.23), channel_id=1, source_target_pairs={{8,0},{16,8},{24,16},{9,1},{17,9},{25,17},{10,2},{18,10},{26,18},{... | collective-permute-start | bytes 24584 | tf_op jit(solution)/shard_map/ppermute | solution.py:25
  209.5 11.2 %collective-permute-start.14 = (bf16[4,4,64,1]{3,2,1,0:T(8,128)(2,1)S(1)}, bf16[4,4,64,1]{3,2,1,0:T(8,128)(2,1)S(1)}, u32[]{:S(2)}, u32[]{:S(2)}) collective-permute-start(bf16[4,4,64,1]{3,2,1,0:T(8,128)(2,1)S(1)} %get-tuple-element.16), channel_id=1, source_target_pairs={{0,1},{1,2},{2,3},{3,4},{4,5},{5,6},{6,7},{7,0},{8,9},{9,10},{10,1... | collective-permute-start | bytes 6152 | tf_op jit(solution)/shard_map/ppermute | solution.py:22
  211.2 14.1 %collective-permute-start.15 = (bf16[4,4,64,1]{3,2,1,0:T(8,128)(2,1)S(1)}, bf16[4,4,64,1]{3,2,1,0:T(8,128)(2,1)S(1)}, u32[]{:S(2)}, u32[]{:S(2)}) collective-permute-start(bf16[4,4,64,1]{3,2,1,0:T(8,128)(2,1)S(1)} %get-tuple-element.17), channel_id=1, source_target_pairs={{1,0},{2,1},{3,2},{4,3},{5,4},{6,5},{7,6},{0,7},{9,8},{10,9},{11,1... | collective-permute-start | bytes 6152 | tf_op jit(solution)/shard_map/ppermute | solution.py:25
  213.8 11.9 %collective-permute-start.16 = (bf16[4,4,1,256]{3,2,1,0:T(2,128)(2,1)S(1)}, bf16[4,4,1,256]{3,2,1,0:T(2,128)(2,1)S(1)}, u32[]{:S(2)}, u32[]{:S(2)}) collective-permute-start(bf16[4,4,1,256]{3,2,1,0:T(2,128)(2,1)S(1)} %get-tuple-element.18), channel_id=1, source_target_pairs={{0,8},{8,16},{16,24},{1,9},{9,17},{17,25},{2,10},{10,18},{18,26},{... | collective-permute-start | bytes 24584 | tf_op jit(solution)/shard_map/ppermute | solution.py:22
  216.4 9.3 %collective-permute-start.17 = (bf16[4,4,1,256]{3,2,1,0:T(2,128)(2,1)S(1)}, bf16[4,4,1,256]{3,2,1,0:T(2,128)(2,1)S(1)}, u32[]{:S(2)}, u32[]{:S(2)}) collective-permute-start(bf16[4,4,1,256]{3,2,1,0:T(2,128)(2,1)S(1)} %get-tuple-element.19), channel_id=1, source_target_pairs={{8,0},{16,8},{24,16},{9,1},{17,9},{25,17},{10,2},{18,10},{26,18},{... | collective-permute-start | bytes 24584 | tf_op jit(solution)/shard_map/ppermute | solution.py:25
where the time goes:
time: 228 us; the launch traced here: 227 us
  blocking collectives  104 us (46%)
  starting transfers between devices  46.5 us (20%)
  other arithmetic  35.7 us (16%)
  waiting for transfers between devices  26.5 us (12%)
  local copies, waits for them, and re-layouts  10.9 us (5%)
  matrix products  3.2 us (1%)
    all_to_all x1, blocking collectives, per_device(): lax.all_to_all(send_rows.reshape(tiles, CAP, fp_cells), ('gy', 'gx'), spl...  104 us
    ppermute x9, starting transfers between devices, padded_2(): lax.ppermute(lax.slice_in_dim(block, 0, width, axis=dim), axis, backward)  25.4 us
    scatter x1, other arithmetic, per_device(): jnp.zeros((tiles * CAP, fp_cells), jnp.bfloat16).at[target].set(contrib)  15.8 us
    ppermute x9, waiting for transfers between devices, padded_2(): lax.ppermute(lax.slice_in_dim(block, block.shape[dim] - width, None, axis...  14.3 us
    ppermute x9, starting transfers between devices, padded_2(): lax.ppermute(lax.slice_in_dim(block, block.shape[dim] - width, None, axis...  13.4 us
    ppermute x9, waiting for transfers between devices, padded_2(): lax.ppermute(lax.slice_in_dim(block, 0, width, axis=dim), axis, backward)  12.2 us
    another operation x2, other arithmetic  9.27 us
    scatter x1, local copies, waits for them, and re-layouts, per_device(): jnp.full((tiles * CAP,), -1, jnp.int32).at[target].set(local_bin)  8.62 us
  transfers between devices with their start and end apart: 19, of which 9 were waited for; matrix products, arithmetic and copies ran while one was open for 8% of the time, Pallas kernels for 0%

commit v1 on v0

v1 whole, which is shorter than its diff:
```python
import jax
import jax.numpy as jnp
from jax import lax
from jax.experimental import pallas as pl
from jax.experimental.pallas import tpu as pltpu
from jax.sharding import PartitionSpec as P

TS_DEV = 4
TRACERS = 4
HB = 2
KSTEPS = 4
LAT = 64
LON = 256
FP = 1024
BINS = 64
SND = 2048
TILES = 32
PAD_LAT = LAT + 16
PAD_LON = LON + 128
HALO = KSTEPS
F32 = jnp.float32
BF16 = jnp.bfloat16
MIB = 1 << 20


def vmem(*refs):
    return [pl.BlockSpec(memory_space=pltpu.VMEM)] * len(refs)


def bin_sums(bins, residual, footprint, col_blocks):
    cols = FP // col_blocks
    rows = 512

    def body(bins_ref, res_ref, fp_ref, out_ref, sel_ref):
        @pl.when(pl.program_id(0) == 0)
        def _():
            @pl.loop(0, TILES * BINS // 128)
            def _(m):
                first = m * 128
                number = lax.broadcasted_iota(jnp.int32, (128, SND), 0) + first
                hit = bins_ref[...] == number
                sel_ref[pl.ds(pl.multiple_of(first, 128), 128), :] = jnp.where(
                    hit, res_ref[...], 0.0
                ).astype(BF16)

        @pl.loop(0, TILES * BINS // rows)
        def _(m):
            at = pl.ds(pl.multiple_of(m * rows, rows), rows)
            out_ref[at, :] = jnp.dot(
                sel_ref[at, :], fp_ref[...], preferred_element_type=F32
            ).astype(BF16)

    return pl.pallas_call(
        body,
        grid=(col_blocks,),
        in_specs=[
            pl.BlockSpec((1, SND), lambda c: (0, 0)),
            pl.BlockSpec((1, SND), lambda c: (0, 0)),
            pl.BlockSpec((SND, cols), lambda c: (0, c)),
        ],
        out_specs=pl.BlockSpec((TILES * BINS, cols), lambda c: (0, c)),
        out_shape=jax.ShapeDtypeStruct((TILES * BINS, FP), BF16),
        scratch_shapes=[pltpu.VMEM((TILES * BINS, SND), BF16)],
        compiler_params=pltpu.CompilerParams(vmem_limit_bytes=40 * MIB),
        cost_estimate=pl.CostEstimate(
            flops=2 * TILES * BINS * SND * FP, bytes_accessed=8 * MIB, transcendentals=0
        ),
        name="bin_sums",
    )(bins, residual, footprint)


def tile_sum(got):
    def body(got_ref, adj_ref, send_ref, half_ref):
        total = got_ref[0].astype(F32)
        for s in range(1, TILES):
            total = total + got_ref[s].astype(F32)
        for bc in range(2):
            for i in range(8):
                half_ref[bc, pl.ds(i, 8, stride=8), :] = total[
                    bc * 8 : bc * 8 + 8, i * 128 : i * 128 + 128
                ]
            adj_ref[0, :, bc * 128 : bc * 128 + 128] = half_ref[bc]
        send_ref[...] = adj_ref[...].astype(BF16)

    return pl.pallas_call(
        body,
        grid=(TS_DEV,),
        in_specs=[pl.BlockSpec((TILES, BINS // TS_DEV, FP), lambda t: (0, t, 0))],
        out_specs=[pl.BlockSpec((1, LAT, LON), lambda t: (t, 0, 0))] * 2,
        out_shape=[
            jax.ShapeDtypeStruct((TS_DEV, LAT, LON), F32),
            jax.ShapeDtypeStruct((TS_DEV, LAT, LON), BF16),
        ],
        scratch_shapes=[pltpu.VMEM((2, LAT, 128), F32)],
        compiler_params=pltpu.CompilerParams(vmem_limit_bytes=20 * MIB),
        name="tile_sum",
    )(got)


def put_strips(strip, dtype):
    lane = lax.broadcasted_iota(jnp.int32, (LAT, 128), 1)

    def packed(planes, side):
        out = jnp.zeros((LAT, 128), F32)
        for k, plane in enumerate(planes):
            if side == 0:
                part = plane[:, :128]
                shift = HALO * k
            else:
                part = plane[:, LON - 128 :]
                shift = HALO * k + HALO
            moved = pltpu.roll(part, shift % 128, 1) if shift % 128 else part
            out = jnp.where((lane >= HALO * k) & (lane < HALO * k + HALO), moved, out)
        return out.astype(dtype)

    return packed(strip, 0), packed(strip, 1)


def pack_lon(arrays, dtype, name):
    counts = [a.shape[0] for a in arrays]

    def body(*refs):
        planes = [
            ref[k].astype(F32) for ref, count in zip(refs, counts) for k in range(count)
        ]
        refs[-2][...], refs[-1][...] = put_strips(planes, dtype)

    return pl.pallas_call(
        body,
        in_specs=vmem(*arrays),
        out_specs=vmem(0, 0),
        out_shape=[jax.ShapeDtypeStruct((LAT, 128), dtype)] * 2,
        name=name,
    )(*arrays)


def pack_lat(arrays, from_left, from_right, dtype, name):
    counts = [a.shape[0] for a in arrays]
    n = sum(counts)

    def body(*refs):
        up_ref, down_ref = refs[-2:]
        strips = jnp.concatenate(
            [refs[-4][...].astype(F32), refs[-3][...].astype(F32)], axis=1
        )
        planes = [
            ref[k].astype(F32) for ref, count in zip(refs, counts) for k in range(count)
        ] + [strips]
        up = jnp.concatenate([p[:HALO] for p in planes], axis=0)
        down = jnp.concatenate([p[LAT - HALO :] for p in planes], axis=0)
        up_ref[...] = up.astype(dtype)
        down_ref[...] = down.astype(dtype)

    return pl.pallas_call(
        body,
        in_specs=vmem(*arrays, 0, 0),
        out_specs=vmem(0, 0),
        out_shape=[jax.ShapeDtypeStruct(((n + 1) * HALO, LON), dtype)] * 2,
        name=name,
    )(*arrays, from_left, from_right)


def padded_plane(k, n, plane, left, right, up, down):
    lane = lax.broadcasted_iota(jnp.int32, (PAD_LAT, 128), 1)

    def rows(mid, top, low):
        zero = jnp.zeros((8 - HALO, mid.shape[1]), F32)
        return jnp.concatenate([zero, top, mid, low, zero], axis=0)

    def from_end(strips, side):
        return strips[n * HALO : (n + 1) * HALO, side * 128 : side * 128 + 128]

    main = rows(plane, up[k * HALO : (k + 1) * HALO], down[k * HALO : (k + 1) * HALO])
    lefts = rows(left, from_end(up, 0), from_end(down, 0))
    rights = rows(right, from_end(up, 1), from_end(down, 1))
    to_right = (-HALO * k) % 128
    to_left = (128 - HALO - HALO * k) % 128
    rights = pltpu.roll(rights, to_right, 1) if to_right else rights
    lefts = pltpu.roll(lefts, to_left, 1) if to_left else lefts
    side = jnp.where(lane < HALO, rights, jnp.where(lane >= 128 - HALO, lefts, 0.0))
    return jnp.concatenate([main, side], axis=1)


def pad_static(sigma, diffusivity, left, right, up, down):
    n = TRACERS + 1

    def body(s_ref, d_ref, l_ref, r_ref, u_ref, w_ref, out_ref):
        for k in range(n):
            plane = s_ref[k] if k < TRACERS else d_ref[0]
            out_ref[k] = padded_plane(
                k, n, plane, l_ref[...], r_ref[...], u_ref[...], w_ref[...]
            )

    return pl.pallas_call(
        body,
        in_specs=vmem(*range(6)),
        out_specs=pl.BlockSpec(memory_space=pltpu.VMEM),
        out_shape=jax.ShapeDtypeStruct((n, PAD_LAT, PAD_LON), F32),
        name="pad_static",
    )(sigma, diffusivity, left, right, up, down)


def diffuse(adj, before, after, left, right, up, down, static, taps):
    n = TS_DEV + 2 * HB

    def body(
        taps_ref, a_ref, b_ref, f_ref, l_ref, r_ref, u_ref, w_ref, st_ref, out_ref, pad_ref
    ):
        c = pl.program_id(0)

        @pl.when(c == 0)
        def _():
            left_, right_ = l_ref[...].astype(F32), r_ref[...].astype(F32)
            up_, down_ = u_ref[...].astype(F32), w_ref[...].astype(F32)
            for k in range(n):
                if k < HB:
                    plane = b_ref[k].astype(F32)
                elif k < HB + TS_DEV:
                    plane = a_ref[k - HB]
                else:
                    plane = f_ref[k - HB - TS_DEV].astype(F32)
                pad_ref[k] = padded_plane(k, n, plane, left_, right_, up_, down_)

        for t in range(TS_DEV):
            banded = taps_ref[c, 0] * pad_ref[t]
            for k in range(1, 2 * HB + 1):
                banded = banded + taps_ref[c, k] * pad_ref[t + k]
            field = st_ref[c] * banded
            for _ in range(KSTEPS):
                beside = (
                    pltpu.roll(field, 1, 1)
                    + pltpu.roll(field, PAD_LON - 1, 1)
                    + pltpu.roll(field, 1, 0)
                    + pltpu.roll(field, PAD_LAT - 1, 0)
                )
                field = field + st_ref[TRACERS] * (beside - 4.0 * field)
            out_ref[0, t] = st_ref[c, 8 : 8 + LAT, :LON] * field[8 : 8 + LAT, :LON]

    whole = [pl.BlockSpec(memory_space=pltpu.VMEM)] * 8
    return pl.pallas_call(
        body,
        grid=(TRACERS,),
        in_specs=[pl.BlockSpec(memory_space=pltpu.SMEM)] + whole,
        out_specs=pl.BlockSpec((1, TS_DEV, LAT, LON), lambda c: (c, 0, 0, 0)),
        out_shape=jax.ShapeDtypeStruct((TRACERS, TS_DEV, LAT, LON), F32),
        scratch_shapes=[pltpu.VMEM((n, PAD_LAT, PAD_LON), F32)],
        compiler_params=pltpu.CompilerParams(vmem_limit_bytes=20 * MIB),
        name="diffuse",
    )(taps, adj, before, after, left, right, up, down, static)


def steps(axis, periodic):
    count = lax.axis_size(axis)
    forward = [(i, i + 1) for i in range(count - 1)]
    if periodic:
        forward.append((count - 1, 0))
    return forward, [(b, a) for a, b in forward]


def halos(arrays, dtype, name):
    east, west = steps("gx", True)
    south, north = steps("gy", False)
    to_left, to_right = pack_lon(arrays, dtype, name + "_lon")
    left = lax.ppermute(to_right, "gx", east)
    right = lax.ppermute(to_left, "gx", west)
    to_up, to_down = pack_lat(arrays, left, right, dtype, name + "_lat")
    up = lax.ppermute(to_down, "gy", south)
    down = lax.ppermute(to_up, "gy", north)
    return left, right, up, down


def per_device(residual, footprint, tile_id, step_id, block_id, sigma, taps, diffusivity):
    bins = tile_id[:, 0] * BINS + step_id * 16 + (block_id % 2) * 8 + block_id // 2
    plane = diffusivity[None]
    static = pad_static(sigma, plane, *halos((sigma, plane), F32, "static"))
    partial_sums = bin_sums(
        bins[None, :], residual.astype(F32)[None, :], footprint, 4
    )
    got = lax.all_to_all(
        partial_sums.reshape(TILES, BINS, FP), ("gy", "gx"), 0, 0, tiled=True
    )
    adj, adj16 = tile_sum(got)
    later, sooner = steps("ta", False)
    before = lax.ppermute(adj16[TS_DEV - HB :], "ta", later)
    after = lax.ppermute(adj16[:HB], "ta", sooner)
    sides = halos((before, adj, after), BF16, "adjoint")
    return diffuse(adj, before, after, *sides, static, taps)


def solution(mesh):
    return jax.shard_map(
        per_device,
        mesh=mesh,
        in_specs=(
            P(("ta", "gy", "gx")),
            P(("ta", "gy", "gx"), None),
            P(("ta", "gy", "gx"), None),
            P(("ta", "gy", "gx")),
            P(("ta", "gy", "gx")),
            P(None, "gy", "gx"),
            P(),
            P("gy", "gx"),
        ),
        out_specs=P(None, "ta", "gy", "gx"),
        check_vma=False,
    )
```

time: 228 us -> 133 us (0.58)
  the two profiles are of different devices: /device:TPU:128 before, /device:TPU:67 now
where the time goes in v1:
time: 133 us; the launch traced here: 132 us
  blocking collectives  56.5 us (42%)
  Pallas kernels  32.6 us (25%)
  starting transfers between devices  27.8 us (21%)
  local copies, waits for them, and re-layouts  12.2 us (9%)
  other arithmetic  2.12 us (2%)
    all_to_all x1, blocking collectives, per_device(): lax.all_to_all(partial_sums.reshape(TILES, BINS, FP), ('gy', 'gx'), 0, 0,...  56.5 us
    pallas_call x1, Pallas kernels, bin_sums(): pl.pallas_call(body, grid=(col_blocks,), in_specs=[pl.BlockSpec((1, SND),...  14.1 us
    unnamed x34, local copies, waits for them, and re-layouts  12.2 us
    pallas_call x1, Pallas kernels, diffuse(): pl.pallas_call(body, grid=(TRACERS,), in_specs=[pl.BlockSpec(memory_space...  8.92 us
    ppermute x1, starting transfers between devices, per_device(): before = lax.ppermute(adj16[TS_DEV - HB:], 'ta', later)  7.03 us
    ppermute x2, starting transfers between devices, halos(): down = lax.ppermute(to_up, 'gy', north)  6.12 us
    ppermute x2, starting transfers between devices, halos(): up = lax.ppermute(to_down, 'gy', south)  5.62 us
    ppermute x2, starting transfers between devices, halos(): right = lax.ppermute(to_left, 'gx', west)  3.65 us
  transfers between devices with their start and end apart: 10, of which 1 were waited for; matrix products, arithmetic and copies ran while one was open for 0% of the time, Pallas kernels for 7%

profile of v1, /device:TPU:67, one launch (start us, length us, event | category | flops | bytes accessed | tf_op | source)
XLA Modules:
  0.0 132.1 jit_solution(1917528917923472410)
XLA Ops:
  0.0 0.7 broadcast_multiply_fusion
  0.7 0.7 broadcast_in_dim.15
  1.4 0.7 fusion.2
  2.1 2.2 %copy-done.12 = bf16[2048,1024]{1,0:T(8,128)(2,1)S(1)} copy-done((bf16[2048,1024]{1,0:T(8,128)(2,1)S(1)}, bf16[2048,1024]{1,0:T(8,128)(2,1)}, u32[]{:S(2)}) %copy-start.12) | copy-done | bytes 4194328
  4.3 14.1 %bin_sums.1 = bf16[2048,1024]{1,0:T(8,128)(2,1)S(1)} custom-call(s32[1,2048]{1,0:T(1,128)S(1)} %bitcast.7, f32[1,2048]{1,0:T(1,128)S(1)} %bitcast.6, bf16[2048,1024]{1,0:T(8,128)(2,1)S(1)} %copy-done.12), custom_call_target="tpu_custom_call" | custom-call | flops 8589934592 | bytes 8388608 | tf_op jit(solution)/shard_map/bin_sums/pallas_call | solution.py:53
  18.4 56.5 %all_to_all.5.got_ref = bf16[32,64,1024]{2,1,0:T(8,128)(2,1)S(1)} all-to-all(bf16[32,64,1024]{2,1,0:T(8,128)(2,1)S(1)} %bitcast.5), channel_id=1, replica_groups=mesh['ta'=8,'gy'=4,'gx'=8] {'gy','gx'}, dimensions={0} | all-to-all | bytes 8388608 | tf_op jit(solution)/shard_map/all_to_all | solution.py:279
  75.0 0.9 tile_sum.1
  75.9 0.7 copy-done.1
  76.6 7.0 %collective-permute-start = (bf16[2,64,256]{2,1,0:T(8,128)(2,1)S(1)}, bf16[2,64,256]{2,1,0:T(8,128)(2,1)S(1)}, u32[]{:S(2)}, u32[]{:S(2)}) collective-permute-start(bf16[2,64,256]{2,1,0:T(8,128)(2,1)S(1)} %get-tuple-element.26), channel_id=1, source_target_pairs={{0,32},{32,64},{64,96},{96,128},{128,160},{160,192},{192,224},{1,3... | collective-permute-start | bytes 196616 | tf_op jit(solution)/shard_map/ppermute | solution.py:284
  83.7 1.9 %collective-permute-start.1 = (bf16[2,64,256]{2,1,0:T(8,128)(2,1)S(1)}, bf16[2,64,256]{2,1,0:T(8,128)(2,1)S(1)}, u32[]{:S(2)}, u32[]{:S(2)}) collective-permute-start(bf16[2,64,256]{2,1,0:T(8,128)(2,1)S(1)} %get-tuple-element.25), channel_id=1, source_target_pairs={{32,0},{64,32},{96,64},{128,96},{160,128},{192,160},{224,192},{33,... | collective-permute-start | bytes 196616 | tf_op jit(solution)/shard_map/ppermute | solution.py:285
  85.6 1.7 %static_lon.1 = (f32[64,128]{1,0:T(8,128)}, f32[64,128]{1,0:T(8,128)}) custom-call(f32[4,64,256]{2,1,0:T(8,128)} %s_ref.1, f32[1,64,256]{2,1,0:T(8,128)} %bitcast.8), custom_call_target="tpu_custom_call" | custom-call | tf_op jit(solution)/shard_map/static_lon/pallas_call | solution.py:128
  87.3 1.6 %collective-permute-start.6 = (f32[64,128]{1,0:T(8,128)}, f32[64,128]{1,0:T(8,128)S(1)}, u32[]{:S(2)}, u32[]{:S(2)}) collective-permute-start(f32[64,128]{1,0:T(8,128)} %get-tuple-element.21), channel_id=1, source_target_pairs={{0,1},{1,2},{2,3},{3,4},{4,5},{5,6},{6,7},{7,0},{8,9},{9,10},{10,1... | collective-permute-start | bytes 98312 | tf_op jit(solution)/shard_map/ppermute | solution.py:264
  88.9 1.9 %collective-permute-start.7 = (f32[64,128]{1,0:T(8,128)}, f32[64,128]{1,0:T(8,128)S(1)}, u32[]{:S(2)}, u32[]{:S(2)}) collective-permute-start(f32[64,128]{1,0:T(8,128)} %get-tuple-element.22), channel_id=1, source_target_pairs={{1,0},{2,1},{3,2},{4,3},{5,4},{6,5},{7,6},{0,7},{9,8},{10,9},{11,1... | collective-permute-start | bytes 98312 | tf_op jit(solution)/shard_map/ppermute | solution.py:265
  92.1 1.7 %adjoint_lon.1 = (bf16[64,128]{1,0:T(8,128)(2,1)}, bf16[64,128]{1,0:T(8,128)(2,1)}) custom-call(bf16[2,64,256]{2,1,0:T(8,128)(2,1)} %copy-done.3, f32[4,64,256]{2,1,0:T(8,128)} %copy-done.1, bf16[2,64,256]{2,1,0:T(8,128)(2,1)} %copy-done.5), custom_call_target="tpu_custom_call" | custom-call | tf_op jit(solution)/shard_map/adjoint_lon/pallas_call | solution.py:128
  93.8 1.9 %collective-permute-start.2 = (bf16[64,128]{1,0:T(8,128)(2,1)}, bf16[64,128]{1,0:T(8,128)(2,1)S(1)}, u32[]{:S(2)}, u32[]{:S(2)}) collective-permute-start(bf16[64,128]{1,0:T(8,128)(2,1)} %get-tuple-element.17), channel_id=1, source_target_pairs={{0,1},{1,2},{2,3},{3,4},{4,5},{5,6},{6,7},{7,0},{8,9},{9,10},{10,1... | collective-permute-start | bytes 49160 | tf_op jit(solution)/shard_map/ppermute | solution.py:264
  95.6 1.7 %collective-permute-start.3 = (bf16[64,128]{1,0:T(8,128)(2,1)}, bf16[64,128]{1,0:T(8,128)(2,1)S(1)}, u32[]{:S(2)}, u32[]{:S(2)}) collective-permute-start(bf16[64,128]{1,0:T(8,128)(2,1)} %get-tuple-element.18), channel_id=1, source_target_pairs={{1,0},{2,1},{3,2},{4,3},{5,4},{6,5},{7,6},{0,7},{9,8},{10,9},{11,1... | collective-permute-start | bytes 49160 | tf_op jit(solution)/shard_map/ppermute | solution.py:265
  97.4 0.6 copy-done.13
  98.0 0.6 copy-done.14
  98.6 1.6 %static_lat.1 = (f32[24,256]{1,0:T(8,128)}, f32[24,256]{1,0:T(8,128)}) custom-call(f32[4,64,256]{2,1,0:T(8,128)} %s_ref.1, f32[1,64,256]{2,1,0:T(8,128)} %bitcast.9, f32[64,128]{1,0:T(8,128)} %copy-done.13, f32[64,128]{1,0:T(8,128)} %copy-done.14), custom_call_target="tpu_custom_call" | custom-call | tf_op jit(solution)/shard_map/static_lat/pallas_call | solution.py:154
  100.2 3.4 %collective-permute-start.8 = (f32[24,256]{1,0:T(8,128)}, f32[24,256]{1,0:T(8,128)S(1)}, u32[]{:S(2)}, u32[]{:S(2)}) collective-permute-start(f32[24,256]{1,0:T(8,128)} %get-tuple-element.23), channel_id=1, source_target_pairs={{0,8},{8,16},{16,24},{1,9},{9,17},{17,25},{2,10},{10,18},{18,26},{... | collective-permute-start | bytes 73736 | tf_op jit(solution)/shard_map/ppermute | solution.py:267
  103.6 3.0 %collective-permute-start.9 = (f32[24,256]{1,0:T(8,128)}, f32[24,256]{1,0:T(8,128)S(1)}, u32[]{:S(2)}, u32[]{:S(2)}) collective-permute-start(f32[24,256]{1,0:T(8,128)} %get-tuple-element.24), channel_id=1, source_target_pairs={{8,0},{16,8},{24,16},{9,1},{17,9},{25,17},{10,2},{18,10},{26,18},{... | collective-permute-start | bytes 73736 | tf_op jit(solution)/shard_map/ppermute | solution.py:268
  107.9 1.6 %adjoint_lat.1 = (bf16[36,256]{1,0:T(8,128)(2,1)}, bf16[36,256]{1,0:T(8,128)(2,1)}) custom-call(bf16[2,64,256]{2,1,0:T(8,128)(2,1)} %copy-done.3, f32[4,64,256]{2,1,0:T(8,128)} %copy-done.1, bf16[2,64,256]{2,1,0:T(8,128)(2,1)} %copy-done.5, bf16[64,128]{1,0:T(8,128)(2,1)} %copy-done.7, bf16[64,128]{1,0:T(8,128)(2,1)} %copy-done.9), custom_call_target="tpu_custom_call" | custom-call | tf_op jit(solution)/shard_map/adjoint_lat/pallas_call | solution.py:154
  109.5 2.2 %collective-permute-start.4 = (bf16[36,256]{1,0:T(8,128)(2,1)}, bf16[36,256]{1,0:T(8,128)(2,1)S(1)}, u32[]{:S(2)}, u32[]{:S(2)}) collective-permute-start(bf16[36,256]{1,0:T(8,128)(2,1)} %get-tuple-element.19), channel_id=1, source_target_pairs={{0,8},{8,16},{16,24},{1,9},{9,17},{17,25},{2,10},{10,18},{18,26},{... | collective-permute-start | bytes 55304 | tf_op jit(solution)/shard_map/ppermute | solution.py:267
  111.7 3.1 %collective-permute-start.5 = (bf16[36,256]{1,0:T(8,128)(2,1)}, bf16[36,256]{1,0:T(8,128)(2,1)S(1)}, u32[]{:S(2)}, u32[]{:S(2)}) collective-permute-start(bf16[36,256]{1,0:T(8,128)(2,1)} %get-tuple-element.20), channel_id=1, source_target_pairs={{8,0},{16,8},{24,16},{9,1},{17,9},{25,17},{10,2},{18,10},{26,18},{... | collective-permute-start | bytes 55304 | tf_op jit(solution)/shard_map/ppermute | solution.py:268
  116.0 2.0 %pad_static.1.st_ref = f32[5,80,384]{2,1,0:T(8,128)} custom-call(f32[4,64,256]{2,1,0:T(8,128)} %s_ref.1, f32[1,64,256]{2,1,0:T(8,128)} %bitcast.10, f32[64,128]{1,0:T(8,128)} %copy-done.13, f32[64,128]{1,0:T(8,128)} %copy-done.14, f32[24,256]{1,0:T(8,128)} %copy-done.15, f32[24,256]{1,0:T(8,128)} %copy-done.16), custom_call_target="tpu_custom_call" | custom-call | tf_op jit(solution)/shard_map/pad_static/pallas_call | solution.py:194
  118.0 1.1 copy-done
  119.1 0.9 copy-done.2
  120.0 0.8 copy-done.4
  120.9 0.8 copy-done.6
  121.7 0.7 copy-done.8
  122.4 0.7 copy-done.10
  123.2 8.9 %diffuse.1 = f32[4,4,64,256]{3,2,1,0:T(8,128)} custom-call(f32[4,5]{1,0:T(4,128)S(1)} %copy-done.11, f32[4,64,256]{2,1,0:T(8,128)S(1)} %copy-done.2, bf16[2,64,256]{2,1,0:T(8,128)(2,1)S(1)} %copy-done.4, bf16[2,64,256]{2,1,0:T(8,128)(2,1)S(1)} %copy-done.6, bf16[64,128]{1,0:T(8,128)(2,1)S(1)} %copy-done.8, bf16[64,128]{1,0:T(8,128)(2,1)S(1)} %copy-done.10, ...), custom_call_target="tpu_custom_call" | custom-call | tf_op jit(solution)/shard_map/diffuse/pallas_call | solution.py:240
  (35 shorter events, 3.6 us)
Async XLA Ops:
  2.1 2.2 %copy-start.12 = (bf16[2048,1024]{1,0:T(8,128)(2,1)S(1)}, bf16[2048,1024]{1,0:T(8,128)(2,1)}, u32[]{:S(2)}) copy-start(bf16[2048,1024]{1,0:T(8,128)(2,1)} %fp_ref.1) | copy-start | bytes 12582916
  75.0 43.0 %copy-start.11 = (f32[4,5]{1,0:T(4,128)S(1)}, f32[4,5]{1,0:T(4,128)}, u32[]{:S(2)}) copy-start(f32[4,5]{1,0:T(4,128)} %taps_ref.1) | copy-start | bytes 244
  75.9 0.7 copy-start.1
  76.6 14.3 %collective-permute-start = (bf16[2,64,256]{2,1,0:T(8,128)(2,1)S(1)}, bf16[2,64,256]{2,1,0:T(8,128)(2,1)S(1)}, u32[]{:S(2)}, u32[]{:S(2)}) collective-permute-start(bf16[2,64,256]{2,1,0:T(8,128)(2,1)S(1)} %get-tuple-element.26), channel_id=1, source_target_pairs={{0,32},{32,64},{64,96},{96,128},{128,160},{160,192},{192,224},{1,3... | collective-permute-start | bytes 196616 | tf_op jit(solution)/shard_map/ppermute | solution.py:284
  83.7 7.8 %collective-permute-start.1 = (bf16[2,64,256]{2,1,0:T(8,128)(2,1)S(1)}, bf16[2,64,256]{2,1,0:T(8,128)(2,1)S(1)}, u32[]{:S(2)}, u32[]{:S(2)}) collective-permute-start(bf16[2,64,256]{2,1,0:T(8,128)(2,1)S(1)} %get-tuple-element.25), channel_id=1, source_target_pairs={{32,0},{64,32},{96,64},{128,96},{160,128},{192,160},{224,192},{33,... | collective-permute-start | bytes 196616 | tf_op jit(solution)/shard_map/ppermute | solution.py:285
  87.3 10.1 %collective-permute-start.6 = (f32[64,128]{1,0:T(8,128)}, f32[64,128]{1,0:T(8,128)S(1)}, u32[]{:S(2)}, u32[]{:S(2)}) collective-permute-start(f32[64,128]{1,0:T(8,128)} %get-tuple-element.21), channel_id=1, source_target_pairs={{0,1},{1,2},{2,3},{3,4},{4,5},{5,6},{6,7},{7,0},{8,9},{9,10},{10,1... | collective-permute-start | bytes 98312 | tf_op jit(solution)/shard_map/ppermute | solution.py:264
  88.9 8.4 %collective-permute-start.7 = (f32[64,128]{1,0:T(8,128)}, f32[64,128]{1,0:T(8,128)S(1)}, u32[]{:S(2)}, u32[]{:S(2)}) collective-permute-start(f32[64,128]{1,0:T(8,128)} %get-tuple-element.22), channel_id=1, source_target_pairs={{1,0},{2,1},{3,2},{4,3},{5,4},{6,5},{7,6},{0,7},{9,8},{10,9},{11,1... | collective-permute-start | bytes 98312 | tf_op jit(solution)/shard_map/ppermute | solution.py:265
  90.9 0.6 copy-start.3
  91.5 0.6 copy-start.5
  93.8 12.9 %collective-permute-start.2 = (bf16[64,128]{1,0:T(8,128)(2,1)}, bf16[64,128]{1,0:T(8,128)(2,1)S(1)}, u32[]{:S(2)}, u32[]{:S(2)}) collective-permute-start(bf16[64,128]{1,0:T(8,128)(2,1)} %get-tuple-element.17), channel_id=1, source_target_pairs={{0,1},{1,2},{2,3},{3,4},{4,5},{5,6},{6,7},{7,0},{8,9},{9,10},{10,1... | collective-permute-start | bytes 49160 | tf_op jit(solution)/shard_map/ppermute | solution.py:264
  95.6 11.0 %collective-permute-start.3 = (bf16[64,128]{1,0:T(8,128)(2,1)}, bf16[64,128]{1,0:T(8,128)(2,1)S(1)}, u32[]{:S(2)}, u32[]{:S(2)}) collective-permute-start(bf16[64,128]{1,0:T(8,128)(2,1)} %get-tuple-element.18), channel_id=1, source_target_pairs={{1,0},{2,1},{3,2},{4,3},{5,4},{6,5},{7,6},{0,7},{9,8},{10,9},{11,1... | collective-permute-start | bytes 49160 | tf_op jit(solution)/shard_map/ppermute | solution.py:265
  97.4 0.6 copy-start.13
  98.0 0.6 copy-start.14
  100.2 14.6 %collective-permute-start.8 = (f32[24,256]{1,0:T(8,128)}, f32[24,256]{1,0:T(8,128)S(1)}, u32[]{:S(2)}, u32[]{:S(2)}) collective-permute-start(f32[24,256]{1,0:T(8,128)} %get-tuple-element.23), channel_id=1, source_target_pairs={{0,8},{8,16},{16,24},{1,9},{9,17},{17,25},{2,10},{10,18},{18,26},{... | collective-permute-start | bytes 73736 | tf_op jit(solution)/shard_map/ppermute | solution.py:267
  103.6 11.2 %collective-permute-start.9 = (f32[24,256]{1,0:T(8,128)}, f32[24,256]{1,0:T(8,128)S(1)}, u32[]{:S(2)}, u32[]{:S(2)}) collective-permute-start(f32[24,256]{1,0:T(8,128)} %get-tuple-element.24), channel_id=1, source_target_pairs={{8,0},{16,8},{24,16},{9,1},{17,9},{25,17},{10,2},{18,10},{26,18},{... | collective-permute-start | bytes 73736 | tf_op jit(solution)/shard_map/ppermute | solution.py:268
  106.7 0.6 copy-start.7
  107.3 0.6 copy-start.9
  109.5 8.5 %collective-permute-start.4 = (bf16[36,256]{1,0:T(8,128)(2,1)}, bf16[36,256]{1,0:T(8,128)(2,1)S(1)}, u32[]{:S(2)}, u32[]{:S(2)}) collective-permute-start(bf16[36,256]{1,0:T(8,128)(2,1)} %get-tuple-element.19), channel_id=1, source_target_pairs={{0,8},{8,16},{16,24},{1,9},{9,17},{17,25},{2,10},{10,18},{18,26},{... | collective-permute-start | bytes 55304 | tf_op jit(solution)/shard_map/ppermute | solution.py:267
  111.7 6.3 %collective-permute-start.5 = (bf16[36,256]{1,0:T(8,128)(2,1)}, bf16[36,256]{1,0:T(8,128)(2,1)S(1)}, u32[]{:S(2)}, u32[]{:S(2)}) collective-permute-start(bf16[36,256]{1,0:T(8,128)(2,1)} %get-tuple-element.20), channel_id=1, source_target_pairs={{8,0},{16,8},{24,16},{9,1},{17,9},{25,17},{10,2},{18,10},{26,18},{... | collective-permute-start | bytes 55304 | tf_op jit(solution)/shard_map/ppermute | solution.py:268
  114.8 0.6 copy-start.15
  115.4 0.6 copy-start.16
  118.0 1.1 copy-start
  119.1 0.9 copy-start.2
  120.0 0.8 copy-start.4
  120.9 0.8 copy-start.6
  121.7 0.7 copy-start.8
  122.4 0.7 copy-start.10

commit v2 on v1

--- a/solution.py
+++ b/solution.py
@@ -12,6 +12,7 @@
 LAT = 64
 LON = 256
 FP = 1024
+HALF = FP // 2
 BINS = 64
 SND = 2048
 TILES = 32
@@ -23,23 +24,20 @@
 MIB = 1 << 20
 
 
-def vmem(*refs):
-    return [pl.BlockSpec(memory_space=pltpu.VMEM)] * len(refs)
-
-
-def bin_sums(bins, residual, footprint, col_blocks):
-    cols = FP // col_blocks
+def bin_sums(bins, residual, footprint, half, col_blocks):
+    cols = HALF // col_blocks
     rows = 512
 
     def body(bins_ref, res_ref, fp_ref, out_ref, sel_ref):
         @pl.when(pl.program_id(0) == 0)
         def _():
-            @pl.loop(0, TILES * BINS // 128)
+            number = lax.broadcasted_iota(jnp.int32, (16, SND), 0)
+
+            @pl.loop(0, TILES * BINS // 16, unroll=4)
             def _(m):
-                first = m * 128
-                number = lax.broadcasted_iota(jnp.int32, (128, SND), 0) + first
-                hit = bins_ref[...] == number
-                sel_ref[pl.ds(pl.multiple_of(first, 128), 128), :] = jnp.where(
+                first = m * 16
+                hit = (bins_ref[...] - first) == number
+                sel_ref[pl.ds(pl.multiple_of(first, 16), 16), :] = jnp.where(
                     hit, res_ref[...], 0.0
                 ).astype(BF16)
 
@@ -56,28 +54,53 @@
         in_specs=[
             pl.BlockSpec((1, SND), lambda c: (0, 0)),
             pl.BlockSpec((1, SND), lambda c: (0, 0)),
-            pl.BlockSpec((SND, cols), lambda c: (0, c)),
+            pl.BlockSpec((SND, cols), lambda c: (0, half * col_blocks + c)),
         ],
         out_specs=pl.BlockSpec((TILES * BINS, cols), lambda c: (0, c)),
-        out_shape=jax.ShapeDtypeStruct((TILES * BINS, FP), BF16),
+        out_shape=jax.ShapeDtypeStruct((TILES * BINS, HALF), BF16),
         scratch_shapes=[pltpu.VMEM((TILES * BINS, SND), BF16)],
-        compiler_params=pltpu.CompilerParams(vmem_limit_bytes=40 * MIB),
+        compiler_params=pltpu.CompilerParams(vmem_limit_bytes=58 * MIB),
         cost_estimate=pl.CostEstimate(
-            flops=2 * TILES * BINS * SND * FP, bytes_accessed=8 * MIB, transcendentals=0
+            flops=2 * TILES * BINS * SND * HALF, bytes_accessed=4 * MIB, transcendentals=0
         ),
         name="bin_sums",
     )(bins, residual, footprint)
 
 
-def tile_sum(got):
-    def body(got_ref, adj_ref, send_ref, half_ref):
+def sum_first(got, blocks):
+    count, rows, cols = got.shape
+
+    def body(got_ref, out_ref):
         total = got_ref[0].astype(F32)
-        for s in range(1, TILES):
+        for s in range(1, count):
             total = total + got_ref[s].astype(F32)
+        out_ref[...] = total.astype(BF16)
+
+    return pl.pallas_call(
+        body,
+        grid=(blocks,),
+        in_specs=[pl.BlockSpec((count, rows // blocks, cols), lambda t: (0, t, 0))],
+        out_specs=pl.BlockSpec((rows // blocks, cols), lambda t: (t, 0)),
+        out_shape=jax.ShapeDtypeStruct((rows, cols), BF16),
+        compiler_params=pltpu.CompilerParams(vmem_limit_bytes=8 * MIB),
+        name="sum_first",
+    )(got)
+
+
+def tile_sum(summed, got):
+    count = got.shape[0]
+    half_i = HALF // 128
+
+    def body(sum_ref, got_ref, adj_ref, send_ref, half_ref):
+        low = sum_ref[...].astype(F32)
+        high = got_ref[0].astype(F32)
+        for s in range(1, count):
+            high = high + got_ref[s].astype(F32)
         for bc in range(2):
             for i in range(8):
-                half_ref[bc, pl.ds(i, 8, stride=8), :] = total[
-                    bc * 8 : bc * 8 + 8, i * 128 : i * 128 + 128
+                part, k = (low, i) if i < half_i else (high, i - half_i)
+                half_ref[bc, pl.ds(i, 8, stride=8), :] = part[
+                    bc * 8 : bc * 8 + 8, k * 128 : k * 128 + 128
                 ]
             adj_ref[0, :, bc * 128 : bc * 128 + 128] = half_ref[bc]
         send_ref[...] = adj_ref[...].astype(BF16)
@@ -85,16 +108,19 @@
     return pl.pallas_call(
         body,
         grid=(TS_DEV,),
-        in_specs=[pl.BlockSpec((TILES, BINS // TS_DEV, FP), lambda t: (0, t, 0))],
+        in_specs=[
+            pl.BlockSpec((BINS // TS_DEV, HALF), lambda t: (t, 0)),
+            pl.BlockSpec((count, BINS // TS_DEV, HALF), lambda t: (0, t, 0)),
+        ],
         out_specs=[pl.BlockSpec((1, LAT, LON), lambda t: (t, 0, 0))] * 2,
         out_shape=[
             jax.ShapeDtypeStruct((TS_DEV, LAT, LON), F32),
             jax.ShapeDtypeStruct((TS_DEV, LAT, LON), BF16),
         ],
         scratch_shapes=[pltpu.VMEM((2, LAT, 128), F32)],
-        compiler_params=pltpu.CompilerParams(vmem_limit_bytes=20 * MIB),
+        compiler_params=pltpu.CompilerParams(vmem_limit_bytes=8 * MIB),
         name="tile_sum",
-    )(got)
+    )(summed, got)
 
 
 def put_strips(strip, dtype):
@@ -127,9 +153,8 @@
 
     return pl.pallas_call(
         body,
-        in_specs=vmem(*arrays),
-        out_specs=vmem(0, 0),
         out_shape=[jax.ShapeDtypeStruct((LAT, 128), dtype)] * 2,
+        compiler_params=pltpu.CompilerParams(vmem_limit_bytes=8 * MIB),
         name=name,
     )(*arrays)
 
@@ -153,9 +178,8 @@
 
     return pl.pallas_call(
         body,
-        in_specs=vmem(*arrays, 0, 0),
-        out_specs=vmem(0, 0),
         out_shape=[jax.ShapeDtypeStruct(((n + 1) * HALO, LON), dtype)] * 2,
+        compiler_params=pltpu.CompilerParams(vmem_limit_bytes=8 * MIB),
         name=name,
     )(*arrays, from_left, from_right)
 
@@ -181,51 +205,31 @@
     return jnp.concatenate([main, side], axis=1)
 
 
-def pad_static(sigma, diffusivity, left, right, up, down):
-    n = TRACERS + 1
-
-    def body(s_ref, d_ref, l_ref, r_ref, u_ref, w_ref, out_ref):
-        for k in range(n):
-            plane = s_ref[k] if k < TRACERS else d_ref[0]
-            out_ref[k] = padded_plane(
-                k, n, plane, l_ref[...], r_ref[...], u_ref[...], w_ref[...]
-            )
-
-    return pl.pallas_call(
-        body,
-        in_specs=vmem(*range(6)),
-        out_specs=pl.BlockSpec(memory_space=pltpu.VMEM),
-        out_shape=jax.ShapeDtypeStruct((n, PAD_LAT, PAD_LON), F32),
-        name="pad_static",
-    )(sigma, diffusivity, left, right, up, down)
-
-
-def diffuse(adj, before, after, left, right, up, down, static, taps):
+def diffuse(adj, before, after, sigma, diffusivity, left, right, up, down, taps):
     n = TS_DEV + 2 * HB
+    count = n + TRACERS + 1
 
     def body(
-        taps_ref, a_ref, b_ref, f_ref, l_ref, r_ref, u_ref, w_ref, st_ref, out_ref, pad_ref
+        taps_ref, a_ref, b_ref, f_ref, s_ref, d_ref, l_ref, r_ref, u_ref, w_ref, out_ref, pad_ref
     ):
         c = pl.program_id(0)
 
         @pl.when(c == 0)
         def _():
-            left_, right_ = l_ref[...].astype(F32), r_ref[...].astype(F32)
-            up_, down_ = u_ref[...].astype(F32), w_ref[...].astype(F32)
-            for k in range(n):
-                if k < HB:
-                    plane = b_ref[k].astype(F32)
-                elif k < HB + TS_DEV:
-                    plane = a_ref[k - HB]
-                else:
-                    plane = f_ref[k - HB - TS_DEV].astype(F32)
-                pad_ref[k] = padded_plane(k, n, plane, left_, right_, up_, down_)
+            planes = [b_ref[k].astype(F32) for k in range(HB)]
+            planes += [a_ref[k] for k in range(TS_DEV)]
+            planes += [f_ref[k].astype(F32) for k in range(HB)]
+            planes += [s_ref[k] for k in range(TRACERS)] + [d_ref[0]]
+            for k in range(count):
+                pad_ref[k] = padded_plane(
+                    k, count, planes[k], l_ref[...], r_ref[...], u_ref[...], w_ref[...]
+                )
 
         for t in range(TS_DEV):
             banded = taps_ref[c, 0] * pad_ref[t]
             for k in range(1, 2 * HB + 1):
                 banded = banded + taps_ref[c, k] * pad_ref[t + k]
-            field = st_ref[c] * banded
+            field = pad_ref[n + c] * banded
             for _ in range(KSTEPS):
                 beside = (
                     pltpu.roll(field, 1, 1)
@@ -233,20 +237,23 @@
                     + pltpu.roll(field, 1, 0)
                     + pltpu.roll(field, PAD_LAT - 1, 0)
                 )
-                field = field + st_ref[TRACERS] * (beside - 4.0 * field)
-            out_ref[0, t] = st_ref[c, 8 : 8 + LAT, :LON] * field[8 : 8 + LAT, :LON]
-
-    whole = [pl.BlockSpec(memory_space=pltpu.VMEM)] * 8
+                field = field + pad_ref[count - 1] * (beside - 4.0 * field)
+            out_ref[0, t] = s_ref[c] * field[8 : 8 + LAT, :LON]
+
+    def whole(a):
+        return pl.BlockSpec(a.shape, lambda c: (0,) * a.ndim)
+
+    arrays = (adj, before, after, sigma, diffusivity, left, right, up, down)
     return pl.pallas_call(
         body,
         grid=(TRACERS,),
-        in_specs=[pl.BlockSpec(memory_space=pltpu.SMEM)] + whole,
+        in_specs=[pl.BlockSpec(memory_space=pltpu.SMEM)] + [whole(a) for a in arrays],
         out_specs=pl.BlockSpec((1, TS_DEV, LAT, LON), lambda c: (c, 0, 0, 0)),
         out_shape=jax.ShapeDtypeStruct((TRACERS, TS_DEV, LAT, LON), F32),
-        scratch_shapes=[pltpu.VMEM((n, PAD_LAT, PAD_LON), F32)],
-        compiler_params=pltpu.CompilerParams(vmem_limit_bytes=20 * MIB),
+        scratch_shapes=[pltpu.VMEM((count, PAD_LAT, PAD_LON), F32)],
+        compiler_params=pltpu.CompilerParams(vmem_limit_bytes=24 * MIB),
         name="diffuse",
-    )(taps, adj, before, after, left, right, up, down, static)
+    )(taps, *arrays)
 
 
 def steps(axis, periodic):
@@ -270,21 +277,30 @@
 
 
 def per_device(residual, footprint, tile_id, step_id, block_id, sigma, taps, diffusivity):
-    bins = tile_id[:, 0] * BINS + step_id * 16 + (block_id % 2) * 8 + block_id // 2
-    plane = diffusivity[None]
-    static = pad_static(sigma, plane, *halos((sigma, plane), F32, "static"))
-    partial_sums = bin_sums(
-        bins[None, :], residual.astype(F32)[None, :], footprint, 4
+    rows_gy, cols_gx = lax.axis_size("gy"), lax.axis_size("gx")
+    local = step_id * 16 + (block_id % 2) * 8 + block_id // 2
+    tile = tile_id[:, 0]
+    gy_first = tile * BINS + local
+    gx_first = ((tile % cols_gx) * rows_gy + tile // cols_gx) * BINS + local
+    weight = residual.astype(F32)[None, :]
+    by_gy = bin_sums(gy_first[None, :], weight, footprint, 1, 2)
+    by_gx = bin_sums(gx_first[None, :], weight, footprint, 0, 2)
+    some_gy = lax.psum_scatter(by_gy, "gy", scatter_dimension=0, tiled=True)
+    got_gx = lax.all_to_all(
+        by_gx.reshape(cols_gx, rows_gy * BINS, HALF), "gx", 0, 0, tiled=True
     )
-    got = lax.all_to_all(
-        partial_sums.reshape(TILES, BINS, FP), ("gy", "gx"), 0, 0, tiled=True
+    some_gx = sum_first(got_gx, rows_gy)
+    all_gx = lax.psum_scatter(some_gx, "gy", scatter_dimension=0, tiled=True)
+    got_gy = lax.all_to_all(
+        some_gy.reshape(cols_gx, BINS, HALF), "gx", 0, 0, tiled=True
     )
-    adj, adj16 = tile_sum(got)
+    adj, adj16 = tile_sum(all_gx, got_gy)
     later, sooner = steps("ta", False)
     before = lax.ppermute(adj16[TS_DEV - HB :], "ta", later)
     after = lax.ppermute(adj16[:HB], "ta", sooner)
-    sides = halos((before, adj, after), BF16, "adjoint")
-    return diffuse(adj, before, after, *sides, static, taps)
+    plane = diffusivity[None]
+    sides = halos((before, adj, after, sigma, plane), F32, "halo")
+    return diffuse(adj, before, after, sigma, plane, *sides, taps)
 
 
 def solution(mesh):

time: 133 us -> 138 us (1.038)
  the two profiles are of different devices: /device:TPU:67 before, /device:TPU:162 now
where the time goes in v2:
time: 138 us; the launch traced here: 137 us
  waiting for transfers between devices  37.7 us (27%)
  Pallas kernels  33.2 us (24%)
  blocking collectives  31.7 us (23%)
  starting transfers between devices  17.5 us (13%)
  between operations  13.5 us (10%)
  other arithmetic  2.64 us (2%)
    all_to_all x1, blocking collectives, per_device(): lax.all_to_all(by_gx.reshape(cols_gx, rows_gy * BINS, HALF), 'gx', 0, 0,...  31.7 us
    reduce_scatter x1, waiting for transfers between devices, per_device(): all_gx = lax.psum_scatter(some_gx, 'gy', scatter_dimension=0, tiled=True)  23.6 us
    pallas_call x2, Pallas kernels, bin_sums(): pl.pallas_call(body, grid=(col_blocks,), in_specs=[pl.BlockSpec((1, SND),...  22 us
    pallas_call x1, Pallas kernels, diffuse(): pl.pallas_call(body, grid=(TRACERS,), in_specs=[pl.BlockSpec(memory_space...  9.09 us
    ppermute x1, waiting for transfers between devices, per_device(): before = lax.ppermute(adj16[TS_DEV - HB:], 'ta', later)  5.34 us
    all_to_all x1, starting transfers between devices, per_device(): lax.all_to_all(some_gy.reshape(cols_gx, BINS, HALF), 'gx', 0, 0, tiled=True)  5 us
    ppermute x1, waiting for transfers between devices, halos(): down = lax.ppermute(to_up, 'gy', north)  3.7 us
    ppermute x1, starting transfers between devices, halos(): up = lax.ppermute(to_down, 'gy', south)  3.69 us
  transfers between devices with their start and end apart: 9, of which 6 were waited for; matrix products, arithmetic and copies ran while one was open for 0% of the time, Pallas kernels for 9%

profile of v2, /device:TPU:162, one launch (start us, length us, event | category | flops | bytes accessed | tf_op | source)
XLA Modules:
  0.0 137.2 jit_solution(15009363062440814264)
XLA Ops:
  6.5 0.0 reduce-scatter.5.cloned.1.call-start
  6.5 1.3 broadcast_in_dim.19
  7.8 1.4 multiply_add_fusion
  9.2 11.0 %bin_sums.3 = bf16[2048,512]{1,0:T(8,128)(2,1)} custom-call(s32[1,2048]{1,0:T(1,128)} %bitcast.14, f32[1,2048]{1,0:T(1,128)} %bitcast.15, bf16[2048,1024]{1,0:T(8,128)(2,1)} %fp_ref.3), custom_call_target="tpu_custom_call" | custom-call | flops 4294967296 | bytes 4194304 | tf_op jit(solution)/shard_map/bin_sums/pallas_call | solution.py:51
  20.2 0.0 reduce-scatter.5.cloned.1.call-update
  20.2 11.0 %bin_sums.2 = bf16[2048,512]{1,0:T(8,128)(2,1)} custom-call(s32[1,2048]{1,0:T(1,128)} %bitcast.13, f32[1,2048]{1,0:T(1,128)} %bitcast.16, bf16[2048,1024]{1,0:T(8,128)(2,1)} %fp_ref.3), custom_call_target="tpu_custom_call" | custom-call | flops 4294967296 | bytes 4194304 | tf_op jit(solution)/shard_map/bin_sums/pallas_call | solution.py:51
  31.2 31.7 %all_to_all.10.got_ref = bf16[8,256,512]{2,1,0:T(8,128)(2,1)S(1)} all-to-all(bf16[8,256,512]{2,1,0:T(8,128)(2,1)} %bitcast.10), channel_id=1, replica_groups=mesh['ta'=8,'gy'=4,'gx'=8] {'gx'}, dimensions={0} | all-to-all | bytes 4194304 | tf_op jit(solution)/shard_map/all_to_all | solution.py:289
  62.9 5.0 %all-to-all-start.1 = ((bf16[8,64,512]{2,1,0:T(8,128)(2,1)}), bf16[8,64,512]{2,1,0:T(8,128)(2,1)S(1)}, u32[]{:S(2)}, u32[]{:S(2)}) async-start(bf16[8,64,512]{2,1,0:T(8,128)(2,1)} %bitcast.11), calls=%async_computation.3 | async-start | bytes 1048576 | tf_op jit(solution)/shard_map/all_to_all | solution.py:294
  67.9 0.0 reduce-scatter.3.cloned.1.call-start
  67.9 1.6 %sum_first.1 = bf16[256,512]{1,0:T(8,128)(2,1)} custom-call(bf16[8,256,512]{2,1,0:T(8,128)(2,1)S(1)} %all_to_all.10.got_ref), custom_call_target="tpu_custom_call" | custom-call | tf_op jit(solution)/shard_map/sum_first/pallas_call | solution.py:79
  69.6 0.0 reduce-scatter.3.cloned.1.call-update
  69.6 23.6 %reduce-scatter.3.cloned.1.call-done.sum_ref = bf16[64,512]{1,0:T(8,128)(2,1)} async-done(((bf16[256,512]{1,0:T(8,128)(2,1)}), bf16[64,512]{1,0:T(8,128)(2,1)}) %reduce-scatter.3.cloned.1.call-update) | async-done | bytes 65552 | tf_op jit(solution)/shard_map/reduce_scatter | solution.py:293
  93.2 0.0 all-to-all-done.1.got_ref
  93.2 0.8 copy-done.2
  94.1 0.2 tile_sum.1
  94.3 1.9 %collective-permute-start.1 = (bf16[2,64,256]{2,1,0:T(8,128)(2,1)S(1)}, bf16[2,64,256]{2,1,0:T(8,128)(2,1)S(1)}, u32[]{:S(2)}, u32[]{:S(2)}) collective-permute-start(bf16[2,64,256]{2,1,0:T(8,128)(2,1)S(1)} %get-tuple-element.17), channel_id=1, source_target_pairs={{32,0},{64,32},{96,64},{128,96},{160,128},{192,160},{224,192},{33,... | collective-permute-start | bytes 196616 | tf_op jit(solution)/shard_map/ppermute | solution.py:300
  96.3 2.4 %collective-permute-start = (bf16[2,64,256]{2,1,0:T(8,128)(2,1)S(1)}, bf16[2,64,256]{2,1,0:T(8,128)(2,1)S(1)}, u32[]{:S(2)}, u32[]{:S(2)}) collective-permute-start(bf16[2,64,256]{2,1,0:T(8,128)(2,1)S(1)} %get-tuple-element.18), channel_id=1, source_target_pairs={{0,32},{32,64},{64,96},{96,128},{128,160},{160,192},{192,224},{1,3... | collective-permute-start | bytes 196616 | tf_op jit(solution)/shard_map/ppermute | solution.py:299
  98.7 0.0 collective-permute-done.1.refs_2_.f_ref
  98.7 5.3 %collective-permute-done.refs_0_.b_ref = bf16[2,64,256]{2,1,0:T(8,128)(2,1)S(1)} collective-permute-done((bf16[2,64,256]{2,1,0:T(8,128)(2,1)S(1)}, bf16[2,64,256]{2,1,0:T(8,128)(2,1)S(1)}, u32[]{:S(2)}, u32[]{:S(2)}) %collective-permute-start) | collective-permute-done | bytes 65568 | tf_op jit(solution)/shard_map/ppermute | solution.py:299
  104.0 0.0 copy-done
  104.0 0.0 copy-done.1
  104.0 0.2 halo_lon.1
  104.3 2.3 %collective-permute-start.2 = (f32[64,128]{1,0:T(8,128)S(1)}, f32[64,128]{1,0:T(8,128)S(1)}, u32[]{:S(2)}, u32[]{:S(2)}) collective-permute-start(f32[64,128]{1,0:T(8,128)S(1)} %get-tuple-element.13), channel_id=1, source_target_pairs={{0,1},{1,2},{2,3},{3,4},{4,5},{5,6},{6,7},{7,0},{8,9},{9,10},{10,1... | collective-permute-start | bytes 98312 | tf_op jit(solution)/shard_map/ppermute | solution.py:271
  106.6 0.0 collective-permute-start.3
  106.6 1.6 %collective-permute-done.2.refs_5_.l_ref = f32[64,128]{1,0:T(8,128)S(1)} collective-permute-done((f32[64,128]{1,0:T(8,128)S(1)}, f32[64,128]{1,0:T(8,128)S(1)}, u32[]{:S(2)}, u32[]{:S(2)}) %collective-permute-start.2) | collective-permute-done | bytes 32800 | tf_op jit(solution)/shard_map/ppermute | solution.py:271
  108.3 3.2 %collective-permute-done.3.refs_6_.r_ref = f32[64,128]{1,0:T(8,128)S(1)} collective-permute-done((f32[64,128]{1,0:T(8,128)S(1)}, f32[64,128]{1,0:T(8,128)S(1)}, u32[]{:S(2)}, u32[]{:S(2)}) %collective-permute-start.3) | collective-permute-done | bytes 32800 | tf_op jit(solution)/shard_map/ppermute | solution.py:272
  111.5 3.7 %collective-permute-start.4 = (f32[56,256]{1,0:T(8,128)S(1)}, f32[56,256]{1,0:T(8,128)S(1)}, u32[]{:S(2)}, u32[]{:S(2)}) collective-permute-start(f32[56,256]{1,0:T(8,128)S(1)} %get-tuple-element.15), channel_id=1, source_target_pairs={{0,8},{8,16},{16,24},{1,9},{9,17},{17,25},{2,10},{10,18},{18,26},{... | collective-permute-start | bytes 172040 | tf_op jit(solution)/shard_map/ppermute | solution.py:274
  115.2 2.2 %collective-permute-start.5 = (f32[56,256]{1,0:T(8,128)S(1)}, f32[56,256]{1,0:T(8,128)S(1)}, u32[]{:S(2)}, u32[]{:S(2)}) collective-permute-start(f32[56,256]{1,0:T(8,128)S(1)} %get-tuple-element.16), channel_id=1, source_target_pairs={{8,0},{16,8},{24,16},{9,1},{17,9},{25,17},{10,2},{18,10},{26,18},{... | collective-permute-start | bytes 172040 | tf_op jit(solution)/shard_map/ppermute | solution.py:275
  117.3 0.2 collective-permute-done.4.u_ref
  117.5 3.7 %collective-permute-done.5.w_ref = f32[56,256]{1,0:T(8,128)S(1)} collective-permute-done((f32[56,256]{1,0:T(8,128)S(1)}, f32[56,256]{1,0:T(8,128)S(1)}, u32[]{:S(2)}, u32[]{:S(2)}) %collective-permute-start.5) | collective-permute-done | bytes 57376 | tf_op jit(solution)/shard_map/ppermute | solution.py:275
  121.2 0.0 copy-done.3
  121.2 9.1 %diffuse.1 = f32[4,4,64,256]{3,2,1,0:T(8,128)} custom-call(f32[4,5]{1,0:T(4,128)S(1)} %copy-done.3, f32[4,64,256]{2,1,0:T(8,128)S(1)} %get-tuple-element.11.refs_1_.a_ref, bf16[2,64,256]{2,1,0:T(8,128)(2,1)S(1)} %collective-permute-done.refs_0_.b_ref, bf16[2,64,256]{2,1,0:T(8,128)(2,1)S(1)} %collective-permute-done.1.refs_2_.f_ref, ...), custom_call_target="tpu_custom_call" | custom-call | tf_op jit(solution)/shard_map/diffuse/pallas_call | solution.py:247
  (7 shorter events, 0.0 us)
Async XLA Ops:
  6.5 56.4 %reduce-scatter.5.cloned.1.call-start = ((), (), s32[]{:S(2)}) async-start(), calls=%async_computation.5 | async-start | bytes 2621440 | tf_op jit(solution)/shard_map/reduce_scatter | solution.py:288
  62.9 41.1 %copy-start = (f32[4,64,256]{2,1,0:T(8,128)S(1)}, f32[4,64,256]{2,1,0:T(8,128)}, u32[]{:S(2)}) copy-start(f32[4,64,256]{2,1,0:T(8,128)} %s_ref.1) | copy-start | bytes 786436
  62.9 41.1 %copy-start.1 = (f32[64,256]{1,0:T(8,128)S(1)}, f32[64,256]{1,0:T(8,128)}, u32[]{:S(2)}) copy-start(f32[64,256]{1,0:T(8,128)} %param.15) | copy-start | bytes 196612
  62.9 30.3 %all-to-all-start.1 = ((bf16[8,64,512]{2,1,0:T(8,128)(2,1)}), bf16[8,64,512]{2,1,0:T(8,128)(2,1)S(1)}, u32[]{:S(2)}, u32[]{:S(2)}) async-start(bf16[8,64,512]{2,1,0:T(8,128)(2,1)} %bitcast.11), calls=%async_computation.3 | async-start | bytes 1048576 | tf_op jit(solution)/shard_map/all_to_all | solution.py:294
  67.9 53.3 %copy-start.3 = (f32[4,5]{1,0:T(4,128)S(1)}, f32[4,5]{1,0:T(4,128)}, u32[]{:S(2)}) copy-start(f32[4,5]{1,0:T(4,128)} %taps_ref.1) | copy-start | bytes 244
  67.9 25.3 %reduce-scatter.3.cloned.1.call-start = ((), (), s32[]{:S(2)}) async-start(), calls=%async_computation.4 | async-start | bytes 327680 | tf_op jit(solution)/shard_map/reduce_scatter | solution.py:293
  93.2 0.8 copy-start.2
  94.3 4.3 %collective-permute-start.1 = (bf16[2,64,256]{2,1,0:T(8,128)(2,1)S(1)}, bf16[2,64,256]{2,1,0:T(8,128)(2,1)S(1)}, u32[]{:S(2)}, u32[]{:S(2)}) collective-permute-start(bf16[2,64,256]{2,1,0:T(8,128)(2,1)S(1)} %get-tuple-element.17), channel_id=1, source_target_pairs={{32,0},{64,32},{96,64},{128,96},{160,128},{192,160},{224,192},{33,... | collective-permute-start | bytes 196616 | tf_op jit(solution)/shard_map/ppermute | solution.py:300
  96.3 7.8 %collective-permute-start = (bf16[2,64,256]{2,1,0:T(8,128)(2,1)S(1)}, bf16[2,64,256]{2,1,0:T(8,128)(2,1)S(1)}, u32[]{:S(2)}, u32[]{:S(2)}) collective-permute-start(bf16[2,64,256]{2,1,0:T(8,128)(2,1)S(1)} %get-tuple-element.18), channel_id=1, source_target_pairs={{0,32},{32,64},{64,96},{96,128},{128,160},{160,192},{192,224},{1,3... | collective-permute-start | bytes 196616 | tf_op jit(solution)/shard_map/ppermute | solution.py:299
  104.3 4.0 %collective-permute-start.2 = (f32[64,128]{1,0:T(8,128)S(1)}, f32[64,128]{1,0:T(8,128)S(1)}, u32[]{:S(2)}, u32[]{:S(2)}) collective-permute-start(f32[64,128]{1,0:T(8,128)S(1)} %get-tuple-element.13), channel_id=1, source_target_pairs={{0,1},{1,2},{2,3},{3,4},{4,5},{5,6},{6,7},{7,0},{8,9},{9,10},{10,1... | collective-permute-start | bytes 98312 | tf_op jit(solution)/shard_map/ppermute | solution.py:271
  106.6 4.8 %collective-permute-start.3 = (f32[64,128]{1,0:T(8,128)S(1)}, f32[64,128]{1,0:T(8,128)S(1)}, u32[]{:S(2)}, u32[]{:S(2)}) collective-permute-start(f32[64,128]{1,0:T(8,128)S(1)} %get-tuple-element.14), channel_id=1, source_target_pairs={{1,0},{2,1},{3,2},{4,3},{5,4},{6,5},{7,6},{0,7},{9,8},{10,9},{11,1... | collective-permute-start | bytes 98312 | tf_op jit(solution)/shard_map/ppermute | solution.py:272
  111.5 6.1 %collective-permute-start.4 = (f32[56,256]{1,0:T(8,128)S(1)}, f32[56,256]{1,0:T(8,128)S(1)}, u32[]{:S(2)}, u32[]{:S(2)}) collective-permute-start(f32[56,256]{1,0:T(8,128)S(1)} %get-tuple-element.15), channel_id=1, source_target_pairs={{0,8},{8,16},{16,24},{1,9},{9,17},{17,25},{2,10},{10,18},{18,26},{... | collective-permute-start | bytes 172040 | tf_op jit(solution)/shard_map/ppermute | solution.py:274
  115.2 6.1 %collective-permute-start.5 = (f32[56,256]{1,0:T(8,128)S(1)}, f32[56,256]{1,0:T(8,128)S(1)}, u32[]{:S(2)}, u32[]{:S(2)}) collective-permute-start(f32[56,256]{1,0:T(8,128)S(1)} %get-tuple-element.16), channel_id=1, source_target_pairs={{8,0},{16,8},{24,16},{9,1},{17,9},{25,17},{10,2},{18,10},{26,18},{... | collective-permute-start | bytes 172040 | tf_op jit(solution)/shard_map/ppermute | solution.py:275
Sparse Core Ops, SparseCore 0:
  20.3 32.1 reduce-scatter.4
  71.4 21.7 reduce-scatter.2

commit v3 on v2

--- a/solution.py
+++ b/solution.py
@@ -15,7 +15,9 @@
 HALF = FP // 2
 BINS = 64
 SND = 2048
-TILES = 32
+N_GY = 4
+N_GX = 8
+TILES = N_GY * N_GX
 PAD_LAT = LAT + 16
 PAD_LON = LON + 128
 HALO = KSTEPS
@@ -24,103 +26,134 @@
 MIB = 1 << 20
 
 
-def bin_sums(bins, residual, footprint, half, col_blocks):
-    cols = HALF // col_blocks
-    rows = 512
-
-    def body(bins_ref, res_ref, fp_ref, out_ref, sel_ref):
+def bin_sums(ids, residual, footprint, first_col, cols, blocks, gx_first):
+    width = cols // blocks
+    parts = 1 if gx_first else N_GY
+    rows = TILES * BINS // parts
+
+    def body(tile_ref, step_ref, block_ref, res_ref, fp_ref, *refs):
+        sel_ref = refs[-1]
+
         @pl.when(pl.program_id(0) == 0)
         def _():
-            number = lax.broadcasted_iota(jnp.int32, (16, SND), 0)
+            tile = tile_ref[...].reshape(1, SND)
+            block = block_ref[...].reshape(1, SND)
+            local = step_ref[...].reshape(1, SND) * 16 + (block & 1) * 8 + (block >> 1)
+            away = (tile // N_GX - lax.axis_index("gy")) & (N_GY - 1)
+            column = tile & (N_GX - 1)
+            order = column * N_GY + away if gx_first else away * N_GX + column
+            bins = (order * BINS + local).astype(jnp.int16)
+            weight = jnp.broadcast_to(res_ref[...].reshape(1, SND).astype(BF16), (16, SND))
+            number = lax.broadcasted_iota(jnp.int32, (16, SND), 0).astype(jnp.int16)
 
             @pl.loop(0, TILES * BINS // 16, unroll=4)
             def _(m):
-                first = m * 16
-                hit = (bins_ref[...] - first) == number
-                sel_ref[pl.ds(pl.multiple_of(first, 16), 16), :] = jnp.where(
-                    hit, res_ref[...], 0.0
+                hit = (bins - (m * 16).astype(jnp.int16)) == number
+                sel_ref[pl.ds(pl.multiple_of(m * 16, 16), 16), :] = jnp.where(
+                    hit, weight, jnp.zeros((16, SND), BF16)
+                )
+
+        for k, out_ref in enumerate(refs[:-1]):
+            chunk = min(rows, 1024)
+            for m in range(rows // chunk):
+                out_ref[m * chunk : m * chunk + chunk, :] = jnp.dot(
+                    sel_ref[k * rows + m * chunk : k * rows + m * chunk + chunk, :],
+                    fp_ref[...],
+                    preferred_element_type=F32,
                 ).astype(BF16)
 
-        @pl.loop(0, TILES * BINS // rows)
-        def _(m):
-            at = pl.ds(pl.multiple_of(m * rows, rows), rows)
-            out_ref[at, :] = jnp.dot(
-                sel_ref[at, :], fp_ref[...], preferred_element_type=F32
-            ).astype(BF16)
-
-    return pl.pallas_call(
-        body,
-        grid=(col_blocks,),
-        in_specs=[
-            pl.BlockSpec((1, SND), lambda c: (0, 0)),
-            pl.BlockSpec((1, SND), lambda c: (0, 0)),
-            pl.BlockSpec((SND, cols), lambda c: (0, half * col_blocks + c)),
-        ],
-        out_specs=pl.BlockSpec((TILES * BINS, cols), lambda c: (0, c)),
-        out_shape=jax.ShapeDtypeStruct((TILES * BINS, HALF), BF16),
+    one = pl.BlockSpec((SND,), lambda c: (0,))
+    return pl.pallas_call(
+        body,
+        grid=(blocks,),
+        in_specs=[one] * 4 + [pl.BlockSpec((SND, width), lambda c: (0, first_col // width + c))],
+        out_specs=[pl.BlockSpec((rows, width), lambda c: (0, c))] * parts,
+        out_shape=[jax.ShapeDtypeStruct((rows, cols), BF16)] * parts,
         scratch_shapes=[pltpu.VMEM((TILES * BINS, SND), BF16)],
         compiler_params=pltpu.CompilerParams(vmem_limit_bytes=58 * MIB),
         cost_estimate=pl.CostEstimate(
-            flops=2 * TILES * BINS * SND * HALF, bytes_accessed=4 * MIB, transcendentals=0
+            flops=4 * TILES * BINS * SND * cols, bytes_accessed=8 * SND * cols, transcendentals=0
         ),
         name="bin_sums",
-    )(bins, residual, footprint)
-
-
-def sum_first(got, blocks):
+    )(*ids, residual, footprint)
+
+
+def sum_first(got, parts):
     count, rows, cols = got.shape
-
-    def body(got_ref, out_ref):
-        total = got_ref[0].astype(F32)
-        for s in range(1, count):
-            total = total + got_ref[s].astype(F32)
-        out_ref[...] = total.astype(BF16)
-
-    return pl.pallas_call(
-        body,
-        grid=(blocks,),
-        in_specs=[pl.BlockSpec((count, rows // blocks, cols), lambda t: (0, t, 0))],
-        out_specs=pl.BlockSpec((rows // blocks, cols), lambda t: (t, 0)),
+    each = rows // parts
+
+    def body(got_ref, *out_refs):
+        for k, out_ref in enumerate(out_refs):
+            at = pl.ds(k * each, each)
+            total = got_ref[0, at].astype(F32)
+            for s in range(1, count):
+                total = total + got_ref[s, at].astype(F32)
+            out_ref[...] = total.astype(BF16)
+
+    return pl.pallas_call(
+        body,
+        out_shape=[jax.ShapeDtypeStruct((each, cols), BF16)] * parts,
+        compiler_params=pltpu.CompilerParams(vmem_limit_bytes=12 * MIB),
+        name="sum_first",
+    )(got)
+
+
+def sum_arrays(arrays):
+    rows, cols = arrays[0].shape
+    step = 128
+
+    def body(*refs):
+        total = refs[0][...].astype(F32)
+        for ref in refs[1:-1]:
+            total = total + ref[...].astype(F32)
+        refs[-1][...] = total.astype(BF16)
+
+    return pl.pallas_call(
+        body,
+        grid=(rows // step,),
+        in_specs=[pl.BlockSpec((step, cols), lambda t: (t, 0))] * len(arrays),
+        out_specs=pl.BlockSpec((step, cols), lambda t: (t, 0)),
         out_shape=jax.ShapeDtypeStruct((rows, cols), BF16),
         compiler_params=pltpu.CompilerParams(vmem_limit_bytes=8 * MIB),
-        name="sum_first",
-    )(got)
+        name="sum_arrays",
+    )(*arrays)
 
 
 def tile_sum(summed, got):
     count = got.shape[0]
     half_i = HALF // 128
 
-    def body(sum_ref, got_ref, adj_ref, send_ref, half_ref):
-        low = sum_ref[...].astype(F32)
+    def body(*refs):
+        got_ref, adj_ref, low_ref, high_ref, half_ref = refs[-5:]
+        low = refs[0][...].astype(F32)
+        for ref in refs[1:-5]:
+            low = low + ref[...].astype(F32)
         high = got_ref[0].astype(F32)
         for s in range(1, count):
             high = high + got_ref[s].astype(F32)
-        for bc in range(2):
-            for i in range(8):
-                part, k = (low, i) if i < half_i else (high, i - half_i)
-                half_ref[bc, pl.ds(i, 8, stride=8), :] = part[
-                    bc * 8 : bc * 8 + 8, k * 128 : k * 128 + 128
-                ]
-            adj_ref[0, :, bc * 128 : bc * 128 + 128] = half_ref[bc]
-        send_ref[...] = adj_ref[...].astype(BF16)
-
-    return pl.pallas_call(
-        body,
-        grid=(TS_DEV,),
-        in_specs=[
-            pl.BlockSpec((BINS // TS_DEV, HALF), lambda t: (t, 0)),
-            pl.BlockSpec((count, BINS // TS_DEV, HALF), lambda t: (0, t, 0)),
-        ],
-        out_specs=[pl.BlockSpec((1, LAT, LON), lambda t: (t, 0, 0))] * 2,
+        for t in range(TS_DEV):
+            for bc in range(2):
+                row = t * 16 + bc * 8
+                for i in range(8):
+                    part, k = (low, i) if i < half_i else (high, i - half_i)
+                    half_ref[t, bc, pl.ds(i, 8, stride=8), :] = part[
+                        row : row + 8, k * 128 : k * 128 + 128
+                    ]
+                adj_ref[t, :, bc * 128 : bc * 128 + 128] = half_ref[t, bc]
+        low_ref[...] = adj_ref[:HB].astype(BF16)
+        high_ref[...] = adj_ref[TS_DEV - HB :].astype(BF16)
+
+    return pl.pallas_call(
+        body,
         out_shape=[
             jax.ShapeDtypeStruct((TS_DEV, LAT, LON), F32),
-            jax.ShapeDtypeStruct((TS_DEV, LAT, LON), BF16),
+            jax.ShapeDtypeStruct((HB, LAT, LON), BF16),
+            jax.ShapeDtypeStruct((HB, LAT, LON), BF16),
         ],
-        scratch_shapes=[pltpu.VMEM((2, LAT, 128), F32)],
+        scratch_shapes=[pltpu.VMEM((TS_DEV, 2, LAT, 128), F32)],
         compiler_params=pltpu.CompilerParams(vmem_limit_bytes=8 * MIB),
         name="tile_sum",
-    )(summed, got)
+    )(*summed, got)
 
 
 def put_strips(strip, dtype):
@@ -276,28 +309,33 @@
     return left, right, up, down
 
 
+def along_gy(parts):
+    return [parts[0]] + [
+        lax.ppermute(parts[k], "gy", [(i, (i + k) % N_GY) for i in range(N_GY)])
+        for k in range(1, N_GY)
+    ]
+
+
+def along_gx(rows):
+    return lax.all_to_all(
+        rows.reshape(N_GX, rows.shape[0] // N_GX, HALF), "gx", 0, 0, tiled=True
+    )
+
+
 def per_device(residual, footprint, tile_id, step_id, block_id, sigma, taps, diffusivity):
-    rows_gy, cols_gx = lax.axis_size("gy"), lax.axis_size("gx")
-    local = step_id * 16 + (block_id % 2) * 8 + block_id // 2
-    tile = tile_id[:, 0]
-    gy_first = tile * BINS + local
-    gx_first = ((tile % cols_gx) * rows_gy + tile // cols_gx) * BINS + local
-    weight = residual.astype(F32)[None, :]
-    by_gy = bin_sums(gy_first[None, :], weight, footprint, 1, 2)
-    by_gx = bin_sums(gx_first[None, :], weight, footprint, 0, 2)
-    some_gy = lax.psum_scatter(by_gy, "gy", scatter_dimension=0, tiled=True)
-    got_gx = lax.all_to_all(
-        by_gx.reshape(cols_gx, rows_gy * BINS, HALF), "gx", 0, 0, tiled=True
-    )
-    some_gx = sum_first(got_gx, rows_gy)
-    all_gx = lax.psum_scatter(some_gx, "gy", scatter_dimension=0, tiled=True)
-    got_gy = lax.all_to_all(
-        some_gy.reshape(cols_gx, BINS, HALF), "gx", 0, 0, tiled=True
-    )
-    adj, adj16 = tile_sum(all_gx, got_gy)
+    ids = (tile_id[:, 0], step_id, block_id)
+    weight = residual.astype(F32)
+    [first_gx] = bin_sums(ids, weight, footprint, 0, HALF, 2, True)
+    got_gx = along_gx(first_gx)
+    weight, first_gx = lax.optimization_barrier((weight, first_gx))
+    first_gy = bin_sums(ids, weight, footprint, HALF, HALF, 2, False)
+    some_gy = sum_arrays(along_gy(first_gy))
+    all_gx = along_gy(sum_first(got_gx, N_GY))
+    all_gy = along_gx(some_gy)
+    adj, low, high = tile_sum(all_gx, all_gy)
     later, sooner = steps("ta", False)
-    before = lax.ppermute(adj16[TS_DEV - HB :], "ta", later)
-    after = lax.ppermute(adj16[:HB], "ta", sooner)
+    before = lax.ppermute(high, "ta", later)
+    after = lax.ppermute(low, "ta", sooner)
     plane = diffusivity[None]
     sides = halos((before, adj, after, sigma, plane), F32, "halo")
     return diffuse(adj, before, after, sigma, plane, *sides, taps)

time: 138 us -> 107 us (0.78)
  the two profiles are of different devices: /device:TPU:162 before, /device:TPU:67 now
where the time goes in v3:
time: 107 us; the launch traced here: 106 us
  starting transfers between devices  37.5 us (35%)
  waiting for transfers between devices  37 us (35%)
  Pallas kernels  29.1 us (27%)
  other arithmetic  1.28 us (1%)
    ppermute x6, waiting for transfers between devices, along_gy(): lax.ppermute(parts[k], 'gy', [(i, (i + k) % N_GY) for i in range(N_GY)])  22.7 us
    pallas_call x2, Pallas kernels, bin_sums(): pl.pallas_call(body, grid=(blocks,), in_specs=[one] * 4 + [pl.BlockSpec((...  17.8 us
    all_to_all x2, starting transfers between devices, along_gx(): lax.all_to_all(rows.reshape(N_GX, rows.shape[0] // N_GX, HALF), 'gx', 0,...  10.8 us
    pallas_call x1, Pallas kernels, diffuse(): pl.pallas_call(body, grid=(TRACERS,), in_specs=[pl.BlockSpec(memory_space...  9.09 us
    ppermute x6, starting transfers between devices, along_gy(): lax.ppermute(parts[k], 'gy', [(i, (i + k) % N_GY) for i in range(N_GY)])  8.3 us
    ppermute x1, starting transfers between devices, per_device(): before = lax.ppermute(high, 'ta', later)  7.54 us
    ppermute x1, waiting for transfers between devices, per_device(): after = lax.ppermute(low, 'ta', sooner)  6.46 us
    all_to_all x2, waiting for transfers between devices, along_gx(): lax.all_to_all(rows.reshape(N_GX, rows.shape[0] // N_GX, HALF), 'gx', 0,...  3.93 us
  transfers between devices with their start and end apart: 14, of which 7 were waited for; matrix products, arithmetic and copies ran while one was open for 0% of the time, Pallas kernels for 10%

profile of v3, /device:TPU:67, one launch (start us, length us, event | category | flops | bytes accessed | tf_op | source)
XLA Modules:
  0.0 106.0 jit_solution(17629888801761563206)
XLA Ops:
  0.0 1.3 %convert_element_type.3.res_ref = f32[2048]{0:T(1024)} convert(bf16[2048]{0:T(1024)(128)(2,1)} %param.8) | non-fusion elementwise | flops 2048 | bytes 12288 | tf_op jit(solution)/shard_map/convert_element_type | solution.py:327
  1.3 9.0 %bin_sums.2 = bf16[2048,512]{1,0:T(8,128)(2,1)} custom-call(s32[2048]{0:T(1024)} %bitcast.8, s32[2048]{0:T(1024)} %step_ref.3, s32[2048]{0:T(1024)} %block_ref.3, f32[2048]{0:T(1024)} %convert_element_type.3.res_ref, bf16[2048,1024]{1,0:T(8,128)(2,1)} %fp_ref.3), custom_call_target="tpu_custom_call" | custom-call | flops 8589934592 | bytes 8388608 | tf_op jit(solution)/shard_map/bin_sums/pallas_call | solution.py:66
  10.2 5.5 %all-to-all-start = ((bf16[8,256,512]{2,1,0:T(8,128)(2,1)}), bf16[8,256,512]{2,1,0:T(8,128)(2,1)S(1)}, u32[]{:S(2)}, u32[]{:S(2)}) async-start(bf16[8,256,512]{2,1,0:T(8,128)(2,1)} %bitcast.7), calls=%async_computation | async-start | bytes 4194304 | tf_op jit(solution)/shard_map/all_to_all | solution.py:320
  15.8 8.8 %bin_sums.3 = (bf16[512,512]{1,0:T(8,128)(2,1)}, bf16[512,512]{1,0:T(8,128)(2,1)}, bf16[512,512]{1,0:T(8,128)(2,1)}, bf16[512,512]{1,0:T(8,128)(2,1)}) custom-call(s32[2048]{0:T(1024)} %bitcast.9, s32[2048]{0:T(1024)} %step_ref.3, s32[2048]{0:T(1024)} %block_ref.3, f32[2048]{0:T(1024)} %convert_element_type.3.res_ref, bf16[2048,1024]{1,0:T(8,128)(2,1)} %fp_ref.3), custom_call_target="tpu_custom_call" | custom-call | flops 8589934592 | bytes 8388608 | tf_op jit(solution)/shard_map/bin_sums/pallas_call | solution.py:66
  24.6 1.2 %collective-permute-start.3 = (bf16[512,512]{1,0:T(8,128)(2,1)}, bf16[512,512]{1,0:T(8,128)(2,1)S(1)}, u32[]{:S(2)}, u32[]{:S(2)}) collective-permute-start(bf16[512,512]{1,0:T(8,128)(2,1)} %get-tuple-element.27), channel_id=1, source_target_pairs={{0,8},{8,16},{16,24},{24,0},{1,9},{9,17},{17,25},{25,1},{2,10},{10... | collective-permute-start | bytes 1572872 | tf_op jit(solution)/shard_map/ppermute | solution.py:314
  25.8 0.8 collective-permute-start.4
  26.6 1.9 %collective-permute-start.5 = (bf16[512,512]{1,0:T(8,128)(2,1)}, bf16[512,512]{1,0:T(8,128)(2,1)S(1)}, u32[]{:S(2)}, u32[]{:S(2)}) collective-permute-start(bf16[512,512]{1,0:T(8,128)(2,1)} %get-tuple-element.29), channel_id=1, source_target_pairs={{0,24},{8,0},{16,8},{24,16},{1,25},{9,1},{17,9},{25,17},{2,26},{10... | collective-permute-start | bytes 1572872 | tf_op jit(solution)/shard_map/ppermute | solution.py:314
  28.5 8.8 %collective-permute-done.3.refs_1_ = bf16[512,512]{1,0:T(8,128)(2,1)S(1)} collective-permute-done((bf16[512,512]{1,0:T(8,128)(2,1)}, bf16[512,512]{1,0:T(8,128)(2,1)S(1)}, u32[]{:S(2)}, u32[]{:S(2)}) %collective-permute-start.3) | collective-permute-done | bytes 524320 | tf_op jit(solution)/shard_map/ppermute | solution.py:314
  37.3 2.5 %collective-permute-done.4.refs_2_ = bf16[512,512]{1,0:T(8,128)(2,1)S(1)} collective-permute-done((bf16[512,512]{1,0:T(8,128)(2,1)}, bf16[512,512]{1,0:T(8,128)(2,1)S(1)}, u32[]{:S(2)}, u32[]{:S(2)}) %collective-permute-start.4) | collective-permute-done | bytes 524320 | tf_op jit(solution)/shard_map/ppermute | solution.py:314
  39.8 11.4 %collective-permute-done.5.refs_3_ = bf16[512,512]{1,0:T(8,128)(2,1)S(1)} collective-permute-done((bf16[512,512]{1,0:T(8,128)(2,1)}, bf16[512,512]{1,0:T(8,128)(2,1)S(1)}, u32[]{:S(2)}, u32[]{:S(2)}) %collective-permute-start.5) | collective-permute-done | bytes 524320 | tf_op jit(solution)/shard_map/ppermute | solution.py:314
  51.2 1.0 copy-done.2
  52.2 1.5 %sum_arrays.1 = bf16[512,512]{1,0:T(8,128)(2,1)} custom-call(bf16[512,512]{1,0:T(8,128)(2,1)S(1)} %copy-done.2, bf16[512,512]{1,0:T(8,128)(2,1)S(1)} %collective-permute-done.3.refs_1_, bf16[512,512]{1,0:T(8,128)(2,1)S(1)} %collective-permute-done.4.refs_2_, bf16[512,512]{1,0:T(8,128)(2,1)S(1)} %collective-permute-done.5.refs_3_), custom_call_target="tpu_custom_call" | custom-call | tf_op jit(solution)/shard_map/sum_arrays/pallas_call | solution.py:111
  53.8 0.0 all-to-all-done.got_ref
  53.8 5.3 %all-to-all-start.1 = ((bf16[8,64,512]{2,1,0:T(8,128)(2,1)}), bf16[8,64,512]{2,1,0:T(8,128)(2,1)S(1)}, u32[]{:S(2)}, u32[]{:S(2)}) async-start(bf16[8,64,512]{2,1,0:T(8,128)(2,1)} %bitcast.2), calls=%async_computation.1 | async-start | bytes 1048576 | tf_op jit(solution)/shard_map/all_to_all | solution.py:320
  59.0 0.3 sum_first.1
  59.3 0.1 collective-permute-start
  59.4 2.3 %collective-permute-start.1 = (bf16[64,512]{1,0:T(8,128)(2,1)S(1)}, bf16[64,512]{1,0:T(8,128)(2,1)S(1)}, u32[]{:S(2)}, u32[]{:S(2)}) collective-permute-start(bf16[64,512]{1,0:T(8,128)(2,1)S(1)} %get-tuple-element.23), channel_id=1, source_target_pairs={{0,16},{8,24},{16,0},{24,8},{1,17},{9,25},{17,1},{25,9},{2,18},{10... | collective-permute-start | bytes 196616 | tf_op jit(solution)/shard_map/ppermute | solution.py:314
  61.7 2.0 %collective-permute-start.2 = (bf16[64,512]{1,0:T(8,128)(2,1)S(1)}, bf16[64,512]{1,0:T(8,128)(2,1)S(1)}, u32[]{:S(2)}, u32[]{:S(2)}) collective-permute-start(bf16[64,512]{1,0:T(8,128)(2,1)S(1)} %get-tuple-element.24), channel_id=1, source_target_pairs={{0,24},{8,0},{16,8},{24,16},{1,25},{9,1},{17,9},{25,17},{2,26},{10... | collective-permute-start | bytes 196616 | tf_op jit(solution)/shard_map/ppermute | solution.py:314
  63.7 3.9 %all-to-all-done.1.refs_4_ = bf16[8,64,512]{2,1,0:T(8,128)(2,1)S(1)} async-done(((bf16[8,64,512]{2,1,0:T(8,128)(2,1)}), bf16[8,64,512]{2,1,0:T(8,128)(2,1)S(1)}, u32[]{:S(2)}, u32[]{:S(2)}) %all-to-all-start.1) | async-done | bytes 524320 | tf_op jit(solution)/shard_map/all_to_all | solution.py:320
  67.7 0.0 collective-permute-done.2.refs_3_
  67.7 0.2 tile_sum.1
  67.8 7.5 %collective-permute-start.6 = (bf16[2,64,256]{2,1,0:T(8,128)(2,1)S(1)}, bf16[2,64,256]{2,1,0:T(8,128)(2,1)S(1)}, u32[]{:S(2)}, u32[]{:S(2)}) collective-permute-start(bf16[2,64,256]{2,1,0:T(8,128)(2,1)S(1)} %get-tuple-element.31), channel_id=1, source_target_pairs={{0,32},{32,64},{64,96},{96,128},{128,160},{160,192},{192,224},{1,3... | collective-permute-start | bytes 196616 | tf_op jit(solution)/shard_map/ppermute | solution.py:337
  75.4 1.9 %collective-permute-start.7 = (bf16[2,64,256]{2,1,0:T(8,128)(2,1)S(1)}, bf16[2,64,256]{2,1,0:T(8,128)(2,1)S(1)}, u32[]{:S(2)}, u32[]{:S(2)}) collective-permute-start(bf16[2,64,256]{2,1,0:T(8,128)(2,1)S(1)} %get-tuple-element.32), channel_id=1, source_target_pairs={{32,0},{64,32},{96,64},{128,96},{160,128},{192,160},{224,192},{33,... | collective-permute-start | bytes 196616 | tf_op jit(solution)/shard_map/ppermute | solution.py:338
  77.3 6.5 %collective-permute-done.7.refs_2_.f_ref = bf16[2,64,256]{2,1,0:T(8,128)(2,1)S(1)} collective-permute-done((bf16[2,64,256]{2,1,0:T(8,128)(2,1)S(1)}, bf16[2,64,256]{2,1,0:T(8,128)(2,1)S(1)}, u32[]{:S(2)}, u32[]{:S(2)}) %collective-permute-start.7) | collective-permute-done | bytes 65568 | tf_op jit(solution)/shard_map/ppermute | solution.py:338
  83.8 0.2 halo_lon.1
  84.0 0.2 collective-permute-start.8
  84.2 3.5 %collective-permute-start.9 = (f32[64,128]{1,0:T(8,128)S(1)}, f32[64,128]{1,0:T(8,128)S(1)}, u32[]{:S(2)}, u32[]{:S(2)}) collective-permute-start(f32[64,128]{1,0:T(8,128)S(1)} %get-tuple-element.34), channel_id=1, source_target_pairs={{1,0},{2,1},{3,2},{4,3},{5,4},{6,5},{7,6},{0,7},{9,8},{10,9},{11,1... | collective-permute-start | bytes 98312 | tf_op jit(solution)/shard_map/ppermute | solution.py:305
  87.7 1.3 %collective-permute-done.8.refs_5_.l_ref = f32[64,128]{1,0:T(8,128)S(1)} collective-permute-done((f32[64,128]{1,0:T(8,128)S(1)}, f32[64,128]{1,0:T(8,128)S(1)}, u32[]{:S(2)}, u32[]{:S(2)}) %collective-permute-start.8) | collective-permute-done | bytes 32800 | tf_op jit(solution)/shard_map/ppermute | solution.py:304
  89.0 2.1 %collective-permute-start.10 = (f32[56,256]{1,0:T(8,128)S(1)}, f32[56,256]{1,0:T(8,128)S(1)}, u32[]{:S(2)}, u32[]{:S(2)}) collective-permute-start(f32[56,256]{1,0:T(8,128)S(1)} %get-tuple-element.35), channel_id=1, source_target_pairs={{0,8},{8,16},{16,24},{1,9},{9,17},{17,25},{2,10},{10,18},{18,26},{... | collective-permute-start | bytes 172040 | tf_op jit(solution)/shard_map/ppermute | solution.py:307
  91.1 3.2 %collective-permute-start.11 = (f32[56,256]{1,0:T(8,128)S(1)}, f32[56,256]{1,0:T(8,128)S(1)}, u32[]{:S(2)}, u32[]{:S(2)}) collective-permute-start(f32[56,256]{1,0:T(8,128)S(1)} %get-tuple-element.36), channel_id=1, source_target_pairs={{8,0},{16,8},{24,16},{9,1},{17,9},{25,17},{10,2},{18,10},{26,18},{... | collective-permute-start | bytes 172040 | tf_op jit(solution)/shard_map/ppermute | solution.py:308
  94.3 2.6 %collective-permute-done.11.w_ref = f32[56,256]{1,0:T(8,128)S(1)} collective-permute-done((f32[56,256]{1,0:T(8,128)S(1)}, f32[56,256]{1,0:T(8,128)S(1)}, u32[]{:S(2)}, u32[]{:S(2)}) %collective-permute-start.11) | collective-permute-done | bytes 57376 | tf_op jit(solution)/shard_map/ppermute | solution.py:308
  96.9 9.1 %diffuse.1 = f32[4,4,64,256]{3,2,1,0:T(8,128)} custom-call(f32[4,5]{1,0:T(4,128)S(1)} %copy-done.3, f32[4,64,256]{2,1,0:T(8,128)S(1)} %get-tuple-element.30.refs_1_.a_ref, bf16[2,64,256]{2,1,0:T(8,128)(2,1)S(1)} %collective-permute-done.6.refs_0_.b_ref, bf16[2,64,256]{2,1,0:T(8,128)(2,1)S(1)} %collective-permute-done.7.refs_2_.f_ref, ...), custom_call_target="tpu_custom_call" | custom-call | tf_op jit(solution)/shard_map/diffuse/pallas_call | solution.py:280
  (13 shorter events, 0.0 us)
Async XLA Ops:
  10.2 43.5 %all-to-all-start = ((bf16[8,256,512]{2,1,0:T(8,128)(2,1)}), bf16[8,256,512]{2,1,0:T(8,128)(2,1)S(1)}, u32[]{:S(2)}, u32[]{:S(2)}) async-start(bf16[8,256,512]{2,1,0:T(8,128)(2,1)} %bitcast.7), calls=%async_computation | async-start | bytes 4194304 | tf_op jit(solution)/shard_map/all_to_all | solution.py:320
  24.6 12.7 %collective-permute-start.3 = (bf16[512,512]{1,0:T(8,128)(2,1)}, bf16[512,512]{1,0:T(8,128)(2,1)S(1)}, u32[]{:S(2)}, u32[]{:S(2)}) collective-permute-start(bf16[512,512]{1,0:T(8,128)(2,1)} %get-tuple-element.27), channel_id=1, source_target_pairs={{0,8},{8,16},{16,24},{24,0},{1,9},{9,17},{17,25},{25,1},{2,10},{10... | collective-permute-start | bytes 1572872 | tf_op jit(solution)/shard_map/ppermute | solution.py:314
  25.8 14.0 %collective-permute-start.4 = (bf16[512,512]{1,0:T(8,128)(2,1)}, bf16[512,512]{1,0:T(8,128)(2,1)S(1)}, u32[]{:S(2)}, u32[]{:S(2)}) collective-permute-start(bf16[512,512]{1,0:T(8,128)(2,1)} %get-tuple-element.28), channel_id=1, source_target_pairs={{0,16},{8,24},{16,0},{24,8},{1,17},{9,25},{17,1},{25,9},{2,18},{10... | collective-permute-start | bytes 1572872 | tf_op jit(solution)/shard_map/ppermute | solution.py:314
  26.6 24.6 %collective-permute-start.5 = (bf16[512,512]{1,0:T(8,128)(2,1)}, bf16[512,512]{1,0:T(8,128)(2,1)S(1)}, u32[]{:S(2)}, u32[]{:S(2)}) collective-permute-start(bf16[512,512]{1,0:T(8,128)(2,1)} %get-tuple-element.29), channel_id=1, source_target_pairs={{0,24},{8,0},{16,8},{24,16},{1,25},{9,1},{17,9},{25,17},{2,26},{10... | collective-permute-start | bytes 1572872 | tf_op jit(solution)/shard_map/ppermute | solution.py:314
  51.2 1.0 copy-start.2
  53.8 30.0 %copy-start = (f32[4,64,256]{2,1,0:T(8,128)S(1)}, f32[4,64,256]{2,1,0:T(8,128)}, u32[]{:S(2)}) copy-start(f32[4,64,256]{2,1,0:T(8,128)} %s_ref.1) | copy-start | bytes 786436
  53.8 30.0 %copy-start.1 = (f32[64,256]{1,0:T(8,128)S(1)}, f32[64,256]{1,0:T(8,128)}, u32[]{:S(2)}) copy-start(f32[64,256]{1,0:T(8,128)} %param.15) | copy-start | bytes 196612
  53.8 13.9 %all-to-all-start.1 = ((bf16[8,64,512]{2,1,0:T(8,128)(2,1)}), bf16[8,64,512]{2,1,0:T(8,128)(2,1)S(1)}, u32[]{:S(2)}, u32[]{:S(2)}) async-start(bf16[8,64,512]{2,1,0:T(8,128)(2,1)} %bitcast.2), calls=%async_computation.1 | async-start | bytes 1048576 | tf_op jit(solution)/shard_map/all_to_all | solution.py:320
  59.0 37.9 %copy-start.3 = (f32[4,5]{1,0:T(4,128)S(1)}, f32[4,5]{1,0:T(4,128)}, u32[]{:S(2)}) copy-start(f32[4,5]{1,0:T(4,128)} %taps_ref.1) | copy-start | bytes 244
  59.3 8.3 %collective-permute-start = (bf16[64,512]{1,0:T(8,128)(2,1)S(1)}, bf16[64,512]{1,0:T(8,128)(2,1)S(1)}, u32[]{:S(2)}, u32[]{:S(2)}) collective-permute-start(bf16[64,512]{1,0:T(8,128)(2,1)S(1)} %get-tuple-element.22), channel_id=1, source_target_pairs={{0,8},{8,16},{16,24},{24,0},{1,9},{9,17},{17,25},{25,1},{2,10},{10... | collective-permute-start | bytes 196616 | tf_op jit(solution)/shard_map/ppermute | solution.py:314
  59.4 8.2 %collective-permute-start.1 = (bf16[64,512]{1,0:T(8,128)(2,1)S(1)}, bf16[64,512]{1,0:T(8,128)(2,1)S(1)}, u32[]{:S(2)}, u32[]{:S(2)}) collective-permute-start(bf16[64,512]{1,0:T(8,128)(2,1)S(1)} %get-tuple-element.23), channel_id=1, source_target_pairs={{0,16},{8,24},{16,0},{24,8},{1,17},{9,25},{17,1},{25,9},{2,18},{10... | collective-permute-start | bytes 196616 | tf_op jit(solution)/shard_map/ppermute | solution.py:314
  61.7 5.9 %collective-permute-start.2 = (bf16[64,512]{1,0:T(8,128)(2,1)S(1)}, bf16[64,512]{1,0:T(8,128)(2,1)S(1)}, u32[]{:S(2)}, u32[]{:S(2)}) collective-permute-start(bf16[64,512]{1,0:T(8,128)(2,1)S(1)} %get-tuple-element.24), channel_id=1, source_target_pairs={{0,24},{8,0},{16,8},{24,16},{1,25},{9,1},{17,9},{25,17},{2,26},{10... | collective-permute-start | bytes 196616 | tf_op jit(solution)/shard_map/ppermute | solution.py:314
  67.8 9.5 %collective-permute-start.6 = (bf16[2,64,256]{2,1,0:T(8,128)(2,1)S(1)}, bf16[2,64,256]{2,1,0:T(8,128)(2,1)S(1)}, u32[]{:S(2)}, u32[]{:S(2)}) collective-permute-start(bf16[2,64,256]{2,1,0:T(8,128)(2,1)S(1)} %get-tuple-element.31), channel_id=1, source_target_pairs={{0,32},{32,64},{64,96},{96,128},{128,160},{160,192},{192,224},{1,3... | collective-permute-start | bytes 196616 | tf_op jit(solution)/shard_map/ppermute | solution.py:337
  75.4 8.4 %collective-permute-start.7 = (bf16[2,64,256]{2,1,0:T(8,128)(2,1)S(1)}, bf16[2,64,256]{2,1,0:T(8,128)(2,1)S(1)}, u32[]{:S(2)}, u32[]{:S(2)}) collective-permute-start(bf16[2,64,256]{2,1,0:T(8,128)(2,1)S(1)} %get-tuple-element.32), channel_id=1, source_target_pairs={{32,0},{64,32},{96,64},{128,96},{160,128},{192,160},{224,192},{33,... | collective-permute-start | bytes 196616 | tf_op jit(solution)/shard_map/ppermute | solution.py:338
  84.0 5.0 %collective-permute-start.8 = (f32[64,128]{1,0:T(8,128)S(1)}, f32[64,128]{1,0:T(8,128)S(1)}, u32[]{:S(2)}, u32[]{:S(2)}) collective-permute-start(f32[64,128]{1,0:T(8,128)S(1)} %get-tuple-element.33), channel_id=1, source_target_pairs={{0,1},{1,2},{2,3},{3,4},{4,5},{5,6},{6,7},{7,0},{8,9},{9,10},{10,1... | collective-permute-start | bytes 98312 | tf_op jit(solution)/shard_map/ppermute | solution.py:304
  84.2 4.8 %collective-permute-start.9 = (f32[64,128]{1,0:T(8,128)S(1)}, f32[64,128]{1,0:T(8,128)S(1)}, u32[]{:S(2)}, u32[]{:S(2)}) collective-permute-start(f32[64,128]{1,0:T(8,128)S(1)} %get-tuple-element.34), channel_id=1, source_target_pairs={{1,0},{2,1},{3,2},{4,3},{5,4},{6,5},{7,6},{0,7},{9,8},{10,9},{11,1... | collective-permute-start | bytes 98312 | tf_op jit(solution)/shard_map/ppermute | solution.py:305
  89.0 5.3 %collective-permute-start.10 = (f32[56,256]{1,0:T(8,128)S(1)}, f32[56,256]{1,0:T(8,128)S(1)}, u32[]{:S(2)}, u32[]{:S(2)}) collective-permute-start(f32[56,256]{1,0:T(8,128)S(1)} %get-tuple-element.35), channel_id=1, source_target_pairs={{0,8},{8,16},{16,24},{1,9},{9,17},{17,25},{2,10},{10,18},{18,26},{... | collective-permute-start | bytes 172040 | tf_op jit(solution)/shard_map/ppermute | solution.py:307
  91.1 5.8 %collective-permute-start.11 = (f32[56,256]{1,0:T(8,128)S(1)}, f32[56,256]{1,0:T(8,128)S(1)}, u32[]{:S(2)}, u32[]{:S(2)}) collective-permute-start(f32[56,256]{1,0:T(8,128)S(1)} %get-tuple-element.36), channel_id=1, source_target_pairs={{8,0},{16,8},{24,16},{9,1},{17,9},{25,17},{10,2},{18,10},{26,18},{... | collective-permute-start | bytes 172040 | tf_op jit(solution)/shard_map/ppermute | solution.py:308

commit v4 on v3

--- a/solution.py
+++ b/solution.py
@@ -18,7 +18,6 @@
 N_GY = 4
 N_GX = 8
 TILES = N_GY * N_GX
-PAD_LAT = LAT + 16
 PAD_LON = LON + 128
 HALO = KSTEPS
 F32 = jnp.float32
@@ -26,23 +25,23 @@
 MIB = 1 << 20
 
 
-def bin_sums(ids, residual, footprint, first_col, cols, blocks, gx_first):
-    width = cols // blocks
-    parts = 1 if gx_first else N_GY
-    rows = TILES * BINS // parts
-
-    def body(tile_ref, step_ref, block_ref, res_ref, fp_ref, *refs):
+def bin_sums(ids, residual, footprint):
+    blocks = 4
+    width = FP // blocks
+    half = blocks // 2
+    rows = N_GX * BINS
+
+    def body(tile_ref, step_ref, block_ref, res_ref, fp_ref, first_ref, *refs):
         sel_ref = refs[-1]
-
-        @pl.when(pl.program_id(0) == 0)
+        c = pl.program_id(0)
+
+        @pl.when(c == 0)
         def _():
             tile = tile_ref[...].reshape(1, SND)
             block = block_ref[...].reshape(1, SND)
             local = step_ref[...].reshape(1, SND) * 16 + (block & 1) * 8 + (block >> 1)
             away = (tile // N_GX - lax.axis_index("gy")) & (N_GY - 1)
-            column = tile & (N_GX - 1)
-            order = column * N_GY + away if gx_first else away * N_GX + column
-            bins = (order * BINS + local).astype(jnp.int16)
+            bins = ((away * N_GX + (tile & (N_GX - 1))) * BINS + local).astype(jnp.int16)
             weight = jnp.broadcast_to(res_ref[...].reshape(1, SND).astype(BF16), (16, SND))
             number = lax.broadcasted_iota(jnp.int32, (16, SND), 0).astype(jnp.int16)
 
@@ -53,29 +52,45 @@
                     hit, weight, jnp.zeros((16, SND), BF16)
                 )
 
-        for k, out_ref in enumerate(refs[:-1]):
-            chunk = min(rows, 1024)
-            for m in range(rows // chunk):
-                out_ref[m * chunk : m * chunk + chunk, :] = jnp.dot(
-                    sel_ref[k * rows + m * chunk : k * rows + m * chunk + chunk, :],
-                    fp_ref[...],
-                    preferred_element_type=F32,
-                ).astype(BF16)
+        def sums(k):
+            return jnp.dot(
+                sel_ref[k * rows : (k + 1) * rows, :],
+                fp_ref[...],
+                preferred_element_type=F32,
+            ).astype(BF16)
+
+        @pl.when(c < half)
+        def _():
+            for k in range(N_GY):
+                out = sums(k)
+                for q in range(N_GX):
+                    at = (q * N_GY + k) * BINS
+                    first_ref[at : at + BINS, :] = out[q * BINS : (q + 1) * BINS]
+
+        @pl.when(c >= half)
+        def _():
+            for k, out_ref in enumerate(refs[:-1]):
+                out_ref[...] = sums(k)
 
     one = pl.BlockSpec((SND,), lambda c: (0,))
-    return pl.pallas_call(
+    outs = pl.pallas_call(
         body,
         grid=(blocks,),
-        in_specs=[one] * 4 + [pl.BlockSpec((SND, width), lambda c: (0, first_col // width + c))],
-        out_specs=[pl.BlockSpec((rows, width), lambda c: (0, c))] * parts,
-        out_shape=[jax.ShapeDtypeStruct((rows, cols), BF16)] * parts,
+        in_specs=[one] * 4 + [pl.BlockSpec((SND, width), lambda c: (0, c))],
+        out_specs=[
+            pl.BlockSpec((TILES * BINS, width), lambda c: (0, jnp.minimum(c, half - 1)))
+        ]
+        + [pl.BlockSpec((rows, width), lambda c: (0, jnp.maximum(c - half, 0)))] * N_GY,
+        out_shape=[jax.ShapeDtypeStruct((TILES * BINS, HALF), BF16)]
+        + [jax.ShapeDtypeStruct((rows, HALF), BF16)] * N_GY,
         scratch_shapes=[pltpu.VMEM((TILES * BINS, SND), BF16)],
         compiler_params=pltpu.CompilerParams(vmem_limit_bytes=58 * MIB),
         cost_estimate=pl.CostEstimate(
-            flops=4 * TILES * BINS * SND * cols, bytes_accessed=8 * SND * cols, transcendentals=0
+            flops=2 * TILES * BINS * SND * FP, bytes_accessed=8 * MIB, transcendentals=0
         ),
         name="bin_sums",
     )(*ids, residual, footprint)
+    return outs[0], outs[1:]
 
 
 def sum_first(got, parts):
@@ -217,76 +232,125 @@
     )(*arrays, from_left, from_right)
 
 
-def padded_plane(k, n, plane, left, right, up, down):
-    lane = lax.broadcasted_iota(jnp.int32, (PAD_LAT, 128), 1)
-
-    def rows(mid, top, low):
-        zero = jnp.zeros((8 - HALO, mid.shape[1]), F32)
-        return jnp.concatenate([zero, top, mid, low, zero], axis=0)
-
-    def from_end(strips, side):
-        return strips[n * HALO : (n + 1) * HALO, side * 128 : side * 128 + 128]
-
-    main = rows(plane, up[k * HALO : (k + 1) * HALO], down[k * HALO : (k + 1) * HALO])
-    lefts = rows(left, from_end(up, 0), from_end(down, 0))
-    rights = rows(right, from_end(up, 1), from_end(down, 1))
+def beside_lon(k, plane, left, right):
+    lane = lax.broadcasted_iota(jnp.int32, right.shape, 1)
     to_right = (-HALO * k) % 128
     to_left = (128 - HALO - HALO * k) % 128
-    rights = pltpu.roll(rights, to_right, 1) if to_right else rights
-    lefts = pltpu.roll(lefts, to_left, 1) if to_left else lefts
-    side = jnp.where(lane < HALO, rights, jnp.where(lane >= 128 - HALO, lefts, 0.0))
-    return jnp.concatenate([main, side], axis=1)
-
-
-def diffuse(adj, before, after, sigma, diffusivity, left, right, up, down, taps):
+    right = pltpu.roll(right, to_right, 1) if to_right else right
+    left = pltpu.roll(left, to_left, 1) if to_left else left
+    side = jnp.where(lane < HALO, right, jnp.where(lane >= 128 - HALO, left, 0.0))
+    return jnp.concatenate([plane, side], axis=1)
+
+
+def covariance(c, taps_ref, pad_ref, rows):
+    n = TS_DEV + 2 * HB
+    banded = taps_ref[c, 0] * pad_ref[0:TS_DEV]
+    for k in range(1, 2 * HB + 1):
+        banded = banded + taps_ref[c, k] * pad_ref[k : k + TS_DEV]
+    field = pad_ref[n + c][None] * banded
+    for _ in range(KSTEPS):
+        beside = (
+            pltpu.roll(field, 1, 2)
+            + pltpu.roll(field, PAD_LON - 1, 2)
+            + pltpu.roll(field, 1, 1)
+            + pltpu.roll(field, rows - 1, 1)
+        )
+        field = field + pad_ref[n + TRACERS][None] * (beside - 4.0 * field)
+    return field
+
+
+def planes_of(refs):
+    return [ref[k].astype(F32) for ref in refs for k in range(ref.shape[0])]
+
+
+def diffuse_inner(arrays, left, right, taps):
+    count = TS_DEV + 2 * HB + TRACERS + 1
+
+    def body(taps_ref, *refs):
+        l_ref, r_ref, out_ref, pad_ref = refs[-4:]
+        c = pl.program_id(0)
+
+        @pl.when(c == 0)
+        def _():
+            for k, plane in enumerate(planes_of(refs[:-4])):
+                pad_ref[k] = beside_lon(k, plane, l_ref[...], r_ref[...])
+
+        field = covariance(c, taps_ref, pad_ref, LAT)
+        scale = pad_ref[TS_DEV + 2 * HB + c, :, :LON]
+        out_ref[0] = scale[None] * field[:, :, :LON]
+
+    def whole(a):
+        return pl.BlockSpec(a.shape, lambda c: (0,) * a.ndim)
+
+    operands = (*arrays, left, right)
+    return pl.pallas_call(
+        body,
+        grid=(TRACERS,),
+        in_specs=[pl.BlockSpec(memory_space=pltpu.SMEM)] + [whole(a) for a in operands],
+        out_specs=pl.BlockSpec((1, TS_DEV, LAT, LON), lambda c: (c, 0, 0, 0)),
+        out_shape=jax.ShapeDtypeStruct((TRACERS, TS_DEV, LAT, LON), F32),
+        scratch_shapes=[pltpu.VMEM((count, LAT, PAD_LON), F32)],
+        compiler_params=pltpu.CompilerParams(vmem_limit_bytes=20 * MIB),
+        cost_estimate=pl.CostEstimate(
+            flops=200 * MIB, bytes_accessed=16 * MIB, transcendentals=0
+        ),
+        name="diffuse_inner",
+    )(taps, *operands)
+
+
+def diffuse_edges(inner, arrays, left, right, up, down, taps):
     n = TS_DEV + 2 * HB
     count = n + TRACERS + 1
-
-    def body(
-        taps_ref, a_ref, b_ref, f_ref, s_ref, d_ref, l_ref, r_ref, u_ref, w_ref, out_ref, pad_ref
-    ):
-        c = pl.program_id(0)
-
-        @pl.when(c == 0)
-        def _():
-            planes = [b_ref[k].astype(F32) for k in range(HB)]
-            planes += [a_ref[k] for k in range(TS_DEV)]
-            planes += [f_ref[k].astype(F32) for k in range(HB)]
-            planes += [s_ref[k] for k in range(TRACERS)] + [d_ref[0]]
-            for k in range(count):
-                pad_ref[k] = padded_plane(
-                    k, count, planes[k], l_ref[...], r_ref[...], u_ref[...], w_ref[...]
-                )
-
-        for t in range(TS_DEV):
-            banded = taps_ref[c, 0] * pad_ref[t]
-            for k in range(1, 2 * HB + 1):
-                banded = banded + taps_ref[c, k] * pad_ref[t + k]
-            field = pad_ref[n + c] * banded
-            for _ in range(KSTEPS):
-                beside = (
-                    pltpu.roll(field, 1, 1)
-                    + pltpu.roll(field, PAD_LON - 1, 1)
-                    + pltpu.roll(field, 1, 0)
-                    + pltpu.roll(field, PAD_LAT - 1, 0)
-                )
-                field = field + pad_ref[count - 1] * (beside - 4.0 * field)
-            out_ref[0, t] = s_ref[c] * field[8 : 8 + LAT, :LON]
-
-    def whole(a):
-        return pl.BlockSpec(a.shape, lambda c: (0,) * a.ndim)
-
-    arrays = (adj, before, after, sigma, diffusivity, left, right, up, down)
-    return pl.pallas_call(
-        body,
-        grid=(TRACERS,),
-        in_specs=[pl.BlockSpec(memory_space=pltpu.SMEM)] + [whole(a) for a in arrays],
-        out_specs=pl.BlockSpec((1, TS_DEV, LAT, LON), lambda c: (c, 0, 0, 0)),
-        out_shape=jax.ShapeDtypeStruct((TRACERS, TS_DEV, LAT, LON), F32),
-        scratch_shapes=[pltpu.VMEM((count, PAD_LAT, PAD_LON), F32)],
-        compiler_params=pltpu.CompilerParams(vmem_limit_bytes=24 * MIB),
-        name="diffuse",
-    )(taps, *arrays)
+    near = 8 + HALO
+    rows = 2 * (near + HALO)
+
+    def body(taps_ref, *refs):
+        l_ref, r_ref, u_ref, w_ref, _, out_ref, pad_ref, edge_ref, sems = refs[-9:]
+
+        def cut(top, plane, low):
+            return jnp.concatenate([top, plane[:near], plane[LAT - near :], low], axis=0)
+
+        def end(ref, side):
+            return ref[count * HALO : (count + 1) * HALO, side * 128 : side * 128 + 128]
+
+        left_ = cut(end(u_ref, 0), l_ref[...], end(w_ref, 0))
+        right_ = cut(end(u_ref, 1), r_ref[...], end(w_ref, 1))
+        for k, plane in enumerate(planes_of(refs[:-9])):
+            at = pl.ds(k * HALO, HALO)
+            pad_ref[k] = beside_lon(k, cut(u_ref[at], plane, w_ref[at]), left_, right_)
+        for c in range(TRACERS):
+            field = covariance(c, taps_ref, pad_ref, rows)
+            done = (pad_ref[n + c, :, :LON])[None] * field[:, :, :LON]
+            edge_ref[0, c] = done[:, HALO : HALO + 8]
+            edge_ref[1, c] = done[:, rows - HALO - 8 : rows - HALO]
+        copies = [
+            pltpu.make_async_copy(
+                edge_ref.at[e], out_ref.at[:, :, pl.ds(e * (LAT - 8), 8), :], sems.at[e]
+            )
+            for e in range(2)
+        ]
+        for copy in copies:
+            copy.start()
+        for copy in copies:
+            copy.wait()
+
+    operands = (*arrays, left, right, up, down)
+    return pl.pallas_call(
+        body,
+        in_specs=[pl.BlockSpec(memory_space=pltpu.SMEM)]
+        + [pl.BlockSpec(a.shape, lambda *_, d=a.ndim: (0,) * d) for a in operands]
+        + [pl.BlockSpec(memory_space=pl.ANY)],
+        out_specs=pl.BlockSpec(memory_space=pl.ANY),
+        out_shape=jax.ShapeDtypeStruct(inner.shape, F32),
+        input_output_aliases={len(operands) + 1: 0},
+        scratch_shapes=[
+            pltpu.VMEM((count, rows, PAD_LON), F32),
+            pltpu.VMEM((2, TRACERS, TS_DEV, 8, LON), F32),
+            pltpu.SemaphoreType.DMA((2,)),
+        ],
+        compiler_params=pltpu.CompilerParams(vmem_limit_bytes=12 * MIB),
+        name="diffuse_edges",
+    )(taps, *operands, inner)
 
 
 def steps(axis, periodic):
@@ -297,18 +361,6 @@
     return forward, [(b, a) for a, b in forward]
 
 
-def halos(arrays, dtype, name):
-    east, west = steps("gx", True)
-    south, north = steps("gy", False)
-    to_left, to_right = pack_lon(arrays, dtype, name + "_lon")
-    left = lax.ppermute(to_right, "gx", east)
-    right = lax.ppermute(to_left, "gx", west)
-    to_up, to_down = pack_lat(arrays, left, right, dtype, name + "_lat")
-    up = lax.ppermute(to_down, "gy", south)
-    down = lax.ppermute(to_up, "gy", north)
-    return left, right, up, down
-
-
 def along_gy(parts):
     return [parts[0]] + [
         lax.ppermute(parts[k], "gy", [(i, (i + k) % N_GY) for i in range(N_GY)])
@@ -324,11 +376,8 @@
 
 def per_device(residual, footprint, tile_id, step_id, block_id, sigma, taps, diffusivity):
     ids = (tile_id[:, 0], step_id, block_id)
-    weight = residual.astype(F32)
-    [first_gx] = bin_sums(ids, weight, footprint, 0, HALF, 2, True)
+    first_gx, first_gy = bin_sums(ids, residual.astype(F32), footprint)
     got_gx = along_gx(first_gx)
-    weight, first_gx = lax.optimization_barrier((weight, first_gx))
-    first_gy = bin_sums(ids, weight, footprint, HALF, HALF, 2, False)
     some_gy = sum_arrays(along_gy(first_gy))
     all_gx = along_gy(sum_first(got_gx, N_GY))
     all_gy = along_gx(some_gy)
@@ -336,9 +385,17 @@
     later, sooner = steps("ta", False)
     before = lax.ppermute(high, "ta", later)
     after = lax.ppermute(low, "ta", sooner)
-    plane = diffusivity[None]
-    sides = halos((before, adj, after, sigma, plane), F32, "halo")
-    return diffuse(adj, before, after, sigma, plane, *sides, taps)
+    arrays = (before, adj, after, sigma, diffusivity[None])
+    east, west = steps("gx", True)
+    south, north = steps("gy", False)
+    to_left, to_right = pack_lon(arrays, F32, "halo_lon")
+    left = lax.ppermute(to_right, "gx", east)
+    right = lax.ppermute(to_left, "gx", west)
+    to_up, to_down = pack_lat(arrays, left, right, F32, "halo_lat")
+    up = lax.ppermute(to_down, "gy", south)
+    down = lax.ppermute(to_up, "gy", north)
+    inner = diffuse_inner(arrays, left, right, taps)
+    return diffuse_edges(inner, arrays, left, right, up, down, taps)
 
 
 def solution(mesh):

time: 107 us -> 101 us (0.944)
  waiting for transfers between devices: 37 us -> 33.3 us
  Pallas kernels: 29.1 us -> 26.4 us
    pallas_call x2 -> x1, Pallas kernels: 17.8 us -> 14.2 us  [bin_sums(): pl.pallas_call(body, grid=(blocks,), in_specs=[one] * 4 + [pl.BlockSpec((...]
    ppermute x4, waiting for transfers between devices: 3.9 us -> 1.31 us  [the longest x1 1.3 us: per_device(): left = lax.ppermute(to_right, 'gx', east)]
    pallas_call x1 -> x2, Pallas kernels: 9.09 us -> 10 us  [the longest x1 6.19 us: diffuse_inner(): pl.pallas_call(body, grid=(TRACERS,), in_specs=[pl.BlockSpec(memory_space...]
  transfers between devices with their start and end apart: 14 -> 14, of which waited for: 7 -> 6; matrix products, arithmetic and copies ran while one was open for 0% -> 0% of each run, Pallas kernels for 10% -> 8%
where the time goes in v4:
time: 101 us; the launch traced here: 99.8 us
  starting transfers between devices  38.5 us (38%)
  waiting for transfers between devices  33.3 us (33%)
  Pallas kernels  26.4 us (26%)
  other arithmetic  1.28 us (1%)
    ppermute x6, waiting for transfers between devices, along_gy(): lax.ppermute(parts[k], 'gy', [(i, (i + k) % N_GY) for i in range(N_GY)])  22.3 us
    pallas_call x1, Pallas kernels, bin_sums(): pl.pallas_call(body, grid=(blocks,), in_specs=[one] * 4 + [pl.BlockSpec((...  14.2 us
    all_to_all x2, starting transfers between devices, along_gx(): lax.all_to_all(rows.reshape(N_GX, rows.shape[0] // N_GX, HALF), 'gx', 0,...  11 us
    ppermute x6, starting transfers between devices, along_gy(): lax.ppermute(parts[k], 'gy', [(i, (i + k) % N_GY) for i in range(N_GY)])  8.72 us
    ppermute x1, starting transfers between devices, per_device(): before = lax.ppermute(high, 'ta', later)  7.74 us
    ppermute x1, waiting for transfers between devices, per_device(): after = lax.ppermute(low, 'ta', sooner)  6.46 us
    pallas_call x1, Pallas kernels, diffuse_inner(): pl.pallas_call(body, grid=(TRACERS,), in_specs=[pl.BlockSpec(memory_space...  6.19 us
    pallas_call x1, Pallas kernels, diffuse_edges(): pl.pallas_call(body, in_specs=[pl.BlockSpec(memory_space=pltpu.SMEM)] + [...  3.83 us
  transfers between devices with their start and end apart: 14, of which 6 were waited for; matrix products, arithmetic and copies ran while one was open for 0% of the time, Pallas kernels for 8%

profile of v4, /device:TPU:67, one launch (start us, length us, event | category | flops | bytes accessed | tf_op | source)
XLA Modules:
  0.0 99.8 jit_solution(1446613204208256964)
XLA Ops:
  0.0 1.3 %convert_element_type.3.res_ref = f32[2048]{0:T(1024)} convert(bf16[2048]{0:T(1024)(128)(2,1)} %param.8) | non-fusion elementwise | flops 2048 | bytes 12288 | tf_op jit(solution)/shard_map/convert_element_type | solution.py:379
  1.3 14.2 %bin_sums.1 = (bf16[2048,512]{1,0:T(8,128)(2,1)}, bf16[512,512]{1,0:T(8,128)(2,1)}, bf16[512,512]{1,0:T(8,128)(2,1)}, bf16[512,512]{1,0:T(8,128)(2,1)}, bf16[512,512]{1,0:T(8,128)(2,1)}) custom-call(s32[2048]{0:T(1024)} %bitcast.9, s32[2048]{0:T(1024)} %step_ref.1, s32[2048]{0:T(1024)} %block_ref.1, f32[2048]{0:T(1024)} %convert_element_type.3.res_ref, ...), custom_call_target="tpu_custom_call" | custom-call | flops 8589934592 | bytes 8388608 | tf_op jit(solution)/shard_map/bin_sums/pallas_call | solution.py:76
  15.4 5.7 %all-to-all-start = ((bf16[8,256,512]{2,1,0:T(8,128)(2,1)}), bf16[8,256,512]{2,1,0:T(8,128)(2,1)S(1)}, u32[]{:S(2)}, u32[]{:S(2)}) async-start(bf16[8,256,512]{2,1,0:T(8,128)(2,1)} %bitcast.8), calls=%async_computation | async-start | bytes 4194304 | tf_op jit(solution)/shard_map/all_to_all | solution.py:372
  21.1 1.2 %collective-permute-start.3 = (bf16[512,512]{1,0:T(8,128)(2,1)}, bf16[512,512]{1,0:T(8,128)(2,1)S(1)}, u32[]{:S(2)}, u32[]{:S(2)}) collective-permute-start(bf16[512,512]{1,0:T(8,128)(2,1)} %get-tuple-element.27), channel_id=1, source_target_pairs={{0,8},{8,16},{16,24},{24,0},{1,9},{9,17},{17,25},{25,1},{2,10},{10... | collective-permute-start | bytes 1572872 | tf_op jit(solution)/shard_map/ppermute | solution.py:366
  22.3 0.8 collective-permute-start.4
  23.2 1.9 %collective-permute-start.5 = (bf16[512,512]{1,0:T(8,128)(2,1)S(1)}, bf16[512,512]{1,0:T(8,128)(2,1)S(1)}, u32[]{:S(2)}, u32[]{:S(2)}) collective-permute-start(bf16[512,512]{1,0:T(8,128)(2,1)S(1)} %copy-done.4), channel_id=1, source_target_pairs={{0,24},{8,0},{16,8},{24,16},{1,25},{9,1},{17,9},{25,17},{2,26},{10... | collective-permute-start | bytes 1572872 | tf_op jit(solution)/shard_map/ppermute | solution.py:366
  25.1 8.8 %collective-permute-done.3.refs_1_ = bf16[512,512]{1,0:T(8,128)(2,1)S(1)} collective-permute-done((bf16[512,512]{1,0:T(8,128)(2,1)}, bf16[512,512]{1,0:T(8,128)(2,1)S(1)}, u32[]{:S(2)}, u32[]{:S(2)}) %collective-permute-start.3) | collective-permute-done | bytes 524320 | tf_op jit(solution)/shard_map/ppermute | solution.py:366
  33.8 2.5 %collective-permute-done.4.refs_2_ = bf16[512,512]{1,0:T(8,128)(2,1)S(1)} collective-permute-done((bf16[512,512]{1,0:T(8,128)(2,1)}, bf16[512,512]{1,0:T(8,128)(2,1)S(1)}, u32[]{:S(2)}, u32[]{:S(2)}) %collective-permute-start.4) | collective-permute-done | bytes 524320 | tf_op jit(solution)/shard_map/ppermute | solution.py:366
  36.3 11.0 %collective-permute-done.5.refs_3_ = bf16[512,512]{1,0:T(8,128)(2,1)S(1)} collective-permute-done((bf16[512,512]{1,0:T(8,128)(2,1)S(1)}, bf16[512,512]{1,0:T(8,128)(2,1)S(1)}, u32[]{:S(2)}, u32[]{:S(2)}) %collective-permute-start.5) | collective-permute-done | bytes 524320 | tf_op jit(solution)/shard_map/ppermute | solution.py:366
  47.3 1.5 %sum_arrays.1 = bf16[512,512]{1,0:T(8,128)(2,1)} custom-call(bf16[512,512]{1,0:T(8,128)(2,1)S(1)} %copy-done.2, bf16[512,512]{1,0:T(8,128)(2,1)S(1)} %collective-permute-done.3.refs_1_, bf16[512,512]{1,0:T(8,128)(2,1)S(1)} %collective-permute-done.4.refs_2_, bf16[512,512]{1,0:T(8,128)(2,1)S(1)} %collective-permute-done.5.refs_3_), custom_call_target="tpu_custom_call" | custom-call | tf_op jit(solution)/shard_map/sum_arrays/pallas_call | solution.py:126
  48.8 0.0 all-to-all-done.got_ref
  48.8 5.3 %all-to-all-start.1 = ((bf16[8,64,512]{2,1,0:T(8,128)(2,1)}), bf16[8,64,512]{2,1,0:T(8,128)(2,1)S(1)}, u32[]{:S(2)}, u32[]{:S(2)}) async-start(bf16[8,64,512]{2,1,0:T(8,128)(2,1)} %bitcast.2), calls=%async_computation.1 | async-start | bytes 1048576 | tf_op jit(solution)/shard_map/all_to_all | solution.py:372
  54.1 0.3 sum_first.1
  54.4 0.3 collective-permute-start
  54.7 2.5 %collective-permute-start.1 = (bf16[64,512]{1,0:T(8,128)(2,1)S(1)}, bf16[64,512]{1,0:T(8,128)(2,1)S(1)}, u32[]{:S(2)}, u32[]{:S(2)}) collective-permute-start(bf16[64,512]{1,0:T(8,128)(2,1)S(1)} %get-tuple-element.24), channel_id=1, source_target_pairs={{0,16},{8,24},{16,0},{24,8},{1,17},{9,25},{17,1},{25,9},{2,18},{10... | collective-permute-start | bytes 196616 | tf_op jit(solution)/shard_map/ppermute | solution.py:366
  57.2 2.0 %collective-permute-start.2 = (bf16[64,512]{1,0:T(8,128)(2,1)S(1)}, bf16[64,512]{1,0:T(8,128)(2,1)S(1)}, u32[]{:S(2)}, u32[]{:S(2)}) collective-permute-start(bf16[64,512]{1,0:T(8,128)(2,1)S(1)} %get-tuple-element.25), channel_id=1, source_target_pairs={{0,24},{8,0},{16,8},{24,16},{1,25},{9,1},{17,9},{25,17},{2,26},{10... | collective-permute-start | bytes 196616 | tf_op jit(solution)/shard_map/ppermute | solution.py:366
  59.2 3.3 %all-to-all-done.1.refs_4_ = bf16[8,64,512]{2,1,0:T(8,128)(2,1)S(1)} async-done(((bf16[8,64,512]{2,1,0:T(8,128)(2,1)}), bf16[8,64,512]{2,1,0:T(8,128)(2,1)S(1)}, u32[]{:S(2)}, u32[]{:S(2)}) %all-to-all-start.1) | async-done | bytes 524320 | tf_op jit(solution)/shard_map/all_to_all | solution.py:372
  62.5 0.2 tile_sum.1
  62.7 7.7 %collective-permute-start.6 = (bf16[2,64,256]{2,1,0:T(8,128)(2,1)S(1)}, bf16[2,64,256]{2,1,0:T(8,128)(2,1)S(1)}, u32[]{:S(2)}, u32[]{:S(2)}) collective-permute-start(bf16[2,64,256]{2,1,0:T(8,128)(2,1)S(1)} %get-tuple-element.30), channel_id=1, source_target_pairs={{0,32},{32,64},{64,96},{96,128},{128,160},{160,192},{192,224},{1,3... | collective-permute-start | bytes 196616 | tf_op jit(solution)/shard_map/ppermute | solution.py:386
  70.5 1.9 %collective-permute-start.7 = (bf16[2,64,256]{2,1,0:T(8,128)(2,1)S(1)}, bf16[2,64,256]{2,1,0:T(8,128)(2,1)S(1)}, u32[]{:S(2)}, u32[]{:S(2)}) collective-permute-start(bf16[2,64,256]{2,1,0:T(8,128)(2,1)S(1)} %get-tuple-element.32), channel_id=1, source_target_pairs={{32,0},{64,32},{96,64},{128,96},{160,128},{192,160},{224,192},{33,... | collective-permute-start | bytes 196616 | tf_op jit(solution)/shard_map/ppermute | solution.py:387
  72.4 6.5 %collective-permute-done.7.refs_2_ = bf16[2,64,256]{2,1,0:T(8,128)(2,1)S(1)} collective-permute-done((bf16[2,64,256]{2,1,0:T(8,128)(2,1)S(1)}, bf16[2,64,256]{2,1,0:T(8,128)(2,1)S(1)}, u32[]{:S(2)}, u32[]{:S(2)}) %collective-permute-start.7) | collective-permute-done | bytes 65568 | tf_op jit(solution)/shard_map/ppermute | solution.py:387
  78.9 0.2 halo_lon.1
  79.1 0.4 collective-permute-start.8
  79.5 3.3 %collective-permute-start.9 = (f32[64,128]{1,0:T(8,128)S(1)}, f32[64,128]{1,0:T(8,128)S(1)}, u32[]{:S(2)}, u32[]{:S(2)}) collective-permute-start(f32[64,128]{1,0:T(8,128)S(1)} %get-tuple-element.34), channel_id=1, source_target_pairs={{1,0},{2,1},{3,2},{4,3},{5,4},{6,5},{7,6},{0,7},{9,8},{10,9},{11,1... | collective-permute-start | bytes 98312 | tf_op jit(solution)/shard_map/ppermute | solution.py:393
  82.8 1.3 %collective-permute-done.8.refs_5_ = f32[64,128]{1,0:T(8,128)S(1)} collective-permute-done((f32[64,128]{1,0:T(8,128)S(1)}, f32[64,128]{1,0:T(8,128)S(1)}, u32[]{:S(2)}, u32[]{:S(2)}) %collective-permute-start.8) | collective-permute-done | bytes 32800 | tf_op jit(solution)/shard_map/ppermute | solution.py:392
  84.1 0.0 collective-permute-done.9.refs_6_
  84.1 2.5 %collective-permute-start.10 = (f32[56,256]{1,0:T(8,128)S(1)}, f32[56,256]{1,0:T(8,128)S(1)}, u32[]{:S(2)}, u32[]{:S(2)}) collective-permute-start(f32[56,256]{1,0:T(8,128)S(1)} %get-tuple-element.35), channel_id=1, source_target_pairs={{0,8},{8,16},{16,24},{1,9},{9,17},{17,25},{2,10},{10,18},{18,26},{... | collective-permute-start | bytes 172040 | tf_op jit(solution)/shard_map/ppermute | solution.py:395
  86.6 3.0 %collective-permute-start.11 = (f32[56,256]{1,0:T(8,128)S(1)}, f32[56,256]{1,0:T(8,128)S(1)}, u32[]{:S(2)}, u32[]{:S(2)}) collective-permute-start(f32[56,256]{1,0:T(8,128)S(1)} %get-tuple-element.36), channel_id=1, source_target_pairs={{8,0},{16,8},{24,16},{9,1},{17,9},{25,17},{10,2},{18,10},{26,18},{... | collective-permute-start | bytes 172040 | tf_op jit(solution)/shard_map/ppermute | solution.py:396
  89.6 6.2 %diffuse_inner.1.refs_9_ = f32[4,4,64,256]{3,2,1,0:T(8,128)} custom-call(f32[4,5]{1,0:T(4,128)S(1)} %copy-done.3, bf16[2,64,256]{2,1,0:T(8,128)(2,1)S(1)} %collective-permute-done.6.refs_0_, f32[4,64,256]{2,1,0:T(8,128)S(1)} %get-tuple-element.31.refs_1_, bf16[2,64,256]{2,1,0:T(8,128)(2,1)S(1)} %collective-permute-done.7.refs_2_, f32[4,64,256]{2,1,0:T(8,128)S(1)} %copy-done, ...), custom_call_target="tpu_custom_call" | custom-call | flops 209715200 | bytes 16777216 | tf_op jit(solution)/shard_map/diffuse_inner/pallas_call | solution.py:286
  95.8 0.0 collective-permute-done.10.refs_7_
  95.8 0.0 collective-permute-done.11.refs_8_
  95.8 3.8 %diffuse_edges.1 = f32[4,4,64,256]{3,2,1,0:T(8,128)} custom-call(f32[4,5]{1,0:T(4,128)S(1)} %copy-done.3, bf16[2,64,256]{2,1,0:T(8,128)(2,1)S(1)} %collective-permute-done.6.refs_0_, f32[4,64,256]{2,1,0:T(8,128)S(1)} %get-tuple-element.31.refs_1_, bf16[2,64,256]{2,1,0:T(8,128)(2,1)S(1)} %collective-permute-done.7.refs_2_, ...), custom_call_target="tpu_custom_call", output_to_operand_aliasing={{}: (10, {})} | custom-call | tf_op jit(solution)/shard_map/diffuse_edges/pallas_call | solution.py:338
  (15 shorter events, 0.0 us)
Async XLA Ops:
  15.4 7.7 %copy-start.4 = (bf16[512,512]{1,0:T(8,128)(2,1)S(1)}, bf16[512,512]{1,0:T(8,128)(2,1)}, u32[]{:S(2)}) copy-start(bf16[512,512]{1,0:T(8,128)(2,1)} %get-tuple-element.29) | copy-start | bytes 1572868
  15.4 31.9 %copy-start.2 = (bf16[512,512]{1,0:T(8,128)(2,1)S(1)}, bf16[512,512]{1,0:T(8,128)(2,1)}, u32[]{:S(2)}) copy-start(bf16[512,512]{1,0:T(8,128)(2,1)} %get-tuple-element.26.refs_0_) | copy-start | bytes 1572868
  15.4 33.4 %all-to-all-start = ((bf16[8,256,512]{2,1,0:T(8,128)(2,1)}), bf16[8,256,512]{2,1,0:T(8,128)(2,1)S(1)}, u32[]{:S(2)}, u32[]{:S(2)}) async-start(bf16[8,256,512]{2,1,0:T(8,128)(2,1)} %bitcast.8), calls=%async_computation | async-start | bytes 4194304 | tf_op jit(solution)/shard_map/all_to_all | solution.py:372
  21.1 12.7 %collective-permute-start.3 = (bf16[512,512]{1,0:T(8,128)(2,1)}, bf16[512,512]{1,0:T(8,128)(2,1)S(1)}, u32[]{:S(2)}, u32[]{:S(2)}) collective-permute-start(bf16[512,512]{1,0:T(8,128)(2,1)} %get-tuple-element.27), channel_id=1, source_target_pairs={{0,8},{8,16},{16,24},{24,0},{1,9},{9,17},{17,25},{25,1},{2,10},{10... | collective-permute-start | bytes 1572872 | tf_op jit(solution)/shard_map/ppermute | solution.py:366
  22.3 14.0 %collective-permute-start.4 = (bf16[512,512]{1,0:T(8,128)(2,1)}, bf16[512,512]{1,0:T(8,128)(2,1)S(1)}, u32[]{:S(2)}, u32[]{:S(2)}) collective-permute-start(bf16[512,512]{1,0:T(8,128)(2,1)} %get-tuple-element.28), channel_id=1, source_target_pairs={{0,16},{8,24},{16,0},{24,8},{1,17},{9,25},{17,1},{25,9},{2,18},{10... | collective-permute-start | bytes 1572872 | tf_op jit(solution)/shard_map/ppermute | solution.py:366
  23.2 24.1 %collective-permute-start.5 = (bf16[512,512]{1,0:T(8,128)(2,1)S(1)}, bf16[512,512]{1,0:T(8,128)(2,1)S(1)}, u32[]{:S(2)}, u32[]{:S(2)}) collective-permute-start(bf16[512,512]{1,0:T(8,128)(2,1)S(1)} %copy-done.4), channel_id=1, source_target_pairs={{0,24},{8,0},{16,8},{24,16},{1,25},{9,1},{17,9},{25,17},{2,26},{10... | collective-permute-start | bytes 1572872 | tf_op jit(solution)/shard_map/ppermute | solution.py:366
  48.8 30.0 %copy-start = (f32[4,64,256]{2,1,0:T(8,128)S(1)}, f32[4,64,256]{2,1,0:T(8,128)}, u32[]{:S(2)}) copy-start(f32[4,64,256]{2,1,0:T(8,128)} %refs_3_.7) | copy-start | bytes 786436
  48.8 30.0 %copy-start.1 = (f32[64,256]{1,0:T(8,128)S(1)}, f32[64,256]{1,0:T(8,128)}, u32[]{:S(2)}) copy-start(f32[64,256]{1,0:T(8,128)} %param.15) | copy-start | bytes 196612
  48.8 13.7 %all-to-all-start.1 = ((bf16[8,64,512]{2,1,0:T(8,128)(2,1)}), bf16[8,64,512]{2,1,0:T(8,128)(2,1)S(1)}, u32[]{:S(2)}, u32[]{:S(2)}) async-start(bf16[8,64,512]{2,1,0:T(8,128)(2,1)} %bitcast.2), calls=%async_computation.1 | async-start | bytes 1048576 | tf_op jit(solution)/shard_map/all_to_all | solution.py:372
  54.1 35.4 %copy-start.3 = (f32[4,5]{1,0:T(4,128)S(1)}, f32[4,5]{1,0:T(4,128)}, u32[]{:S(2)}) copy-start(f32[4,5]{1,0:T(4,128)} %taps_ref.3) | copy-start | bytes 244
  54.4 8.1 %collective-permute-start = (bf16[64,512]{1,0:T(8,128)(2,1)S(1)}, bf16[64,512]{1,0:T(8,128)(2,1)S(1)}, u32[]{:S(2)}, u32[]{:S(2)}) collective-permute-start(bf16[64,512]{1,0:T(8,128)(2,1)S(1)} %get-tuple-element.23), channel_id=1, source_target_pairs={{0,8},{8,16},{16,24},{24,0},{1,9},{9,17},{17,25},{25,1},{2,10},{10... | collective-permute-start | bytes 196616 | tf_op jit(solution)/shard_map/ppermute | solution.py:366
  54.7 7.8 %collective-permute-start.1 = (bf16[64,512]{1,0:T(8,128)(2,1)S(1)}, bf16[64,512]{1,0:T(8,128)(2,1)S(1)}, u32[]{:S(2)}, u32[]{:S(2)}) collective-permute-start(bf16[64,512]{1,0:T(8,128)(2,1)S(1)} %get-tuple-element.24), channel_id=1, source_target_pairs={{0,16},{8,24},{16,0},{24,8},{1,17},{9,25},{17,1},{25,9},{2,18},{10... | collective-permute-start | bytes 196616 | tf_op jit(solution)/shard_map/ppermute | solution.py:366
  57.2 5.3 %collective-permute-start.2 = (bf16[64,512]{1,0:T(8,128)(2,1)S(1)}, bf16[64,512]{1,0:T(8,128)(2,1)S(1)}, u32[]{:S(2)}, u32[]{:S(2)}) collective-permute-start(bf16[64,512]{1,0:T(8,128)(2,1)S(1)} %get-tuple-element.25), channel_id=1, source_target_pairs={{0,24},{8,0},{16,8},{24,16},{1,25},{9,1},{17,9},{25,17},{2,26},{10... | collective-permute-start | bytes 196616 | tf_op jit(solution)/shard_map/ppermute | solution.py:366
  62.7 9.7 %collective-permute-start.6 = (bf16[2,64,256]{2,1,0:T(8,128)(2,1)S(1)}, bf16[2,64,256]{2,1,0:T(8,128)(2,1)S(1)}, u32[]{:S(2)}, u32[]{:S(2)}) collective-permute-start(bf16[2,64,256]{2,1,0:T(8,128)(2,1)S(1)} %get-tuple-element.30), channel_id=1, source_target_pairs={{0,32},{32,64},{64,96},{96,128},{128,160},{160,192},{192,224},{1,3... | collective-permute-start | bytes 196616 | tf_op jit(solution)/shard_map/ppermute | solution.py:386
  70.5 8.4 %collective-permute-start.7 = (bf16[2,64,256]{2,1,0:T(8,128)(2,1)S(1)}, bf16[2,64,256]{2,1,0:T(8,128)(2,1)S(1)}, u32[]{:S(2)}, u32[]{:S(2)}) collective-permute-start(bf16[2,64,256]{2,1,0:T(8,128)(2,1)S(1)} %get-tuple-element.32), channel_id=1, source_target_pairs={{32,0},{64,32},{96,64},{128,96},{160,128},{192,160},{224,192},{33,... | collective-permute-start | bytes 196616 | tf_op jit(solution)/shard_map/ppermute | solution.py:387
  79.1 5.0 %collective-permute-start.8 = (f32[64,128]{1,0:T(8,128)S(1)}, f32[64,128]{1,0:T(8,128)S(1)}, u32[]{:S(2)}, u32[]{:S(2)}) collective-permute-start(f32[64,128]{1,0:T(8,128)S(1)} %get-tuple-element.33), channel_id=1, source_target_pairs={{0,1},{1,2},{2,3},{3,4},{4,5},{5,6},{6,7},{7,0},{8,9},{9,10},{10,1... | collective-permute-start | bytes 98312 | tf_op jit(solution)/shard_map/ppermute | solution.py:392
  79.5 4.6 %collective-permute-start.9 = (f32[64,128]{1,0:T(8,128)S(1)}, f32[64,128]{1,0:T(8,128)S(1)}, u32[]{:S(2)}, u32[]{:S(2)}) collective-permute-start(f32[64,128]{1,0:T(8,128)S(1)} %get-tuple-element.34), channel_id=1, source_target_pairs={{1,0},{2,1},{3,2},{4,3},{5,4},{6,5},{7,6},{0,7},{9,8},{10,9},{11,1... | collective-permute-start | bytes 98312 | tf_op jit(solution)/shard_map/ppermute | solution.py:393
  84.1 11.7 %collective-permute-start.10 = (f32[56,256]{1,0:T(8,128)S(1)}, f32[56,256]{1,0:T(8,128)S(1)}, u32[]{:S(2)}, u32[]{:S(2)}) collective-permute-start(f32[56,256]{1,0:T(8,128)S(1)} %get-tuple-element.35), channel_id=1, source_target_pairs={{0,8},{8,16},{16,24},{1,9},{9,17},{17,25},{2,10},{10,18},{18,26},{... | collective-permute-start | bytes 172040 | tf_op jit(solution)/shard_map/ppermute | solution.py:395
  86.6 9.2 %collective-permute-start.11 = (f32[56,256]{1,0:T(8,128)S(1)}, f32[56,256]{1,0:T(8,128)S(1)}, u32[]{:S(2)}, u32[]{:S(2)}) collective-permute-start(f32[56,256]{1,0:T(8,128)S(1)} %get-tuple-element.36), channel_id=1, source_target_pairs={{8,0},{16,8},{24,16},{9,1},{17,9},{25,17},{10,2},{18,10},{26,18},{... | collective-permute-start | bytes 172040 | tf_op jit(solution)/shard_map/ppermute | solution.py:396

commit v5 on v4

v5 whole, which is shorter than its diff:
```python
import jax
import jax.numpy as jnp
from jax import lax
from jax.experimental import pallas as pl
from jax.experimental.pallas import tpu as pltpu
from jax.sharding import PartitionSpec as P

TS_DEV = 4
TRACERS = 4
HB = 2
KSTEPS = 4
LAT = 64
LON = 256
FP = 1024
HALF = FP // 2
BINS = 64
SND = 2048
N_GY = 4
N_GX = 8
TILES = N_GY * N_GX
PAD_LAT = LAT + 16
PAD_LON = LON + 128
ROWS = BINS + 16
HALO = KSTEPS
F32 = jnp.float32
BF16 = jnp.bfloat16
MIB = 1 << 20


def bin_sums(ids, residual, footprint):
    rows = N_GX * BINS

    def body(tile_ref, step_ref, block_ref, res_ref, fp_ref, first_ref, *refs):
        sel_ref = refs[-1]
        c = pl.program_id(0)

        @pl.when(c == 0)
        def _():
            tile = tile_ref[...].reshape(1, SND)
            block = block_ref[...].reshape(1, SND)
            local = (block >> 1) * 8 + step_ref[...].reshape(1, SND) * 2 + (block & 1)
            away = (tile // N_GX - lax.axis_index("gy")) & (N_GY - 1)
            bins = ((away * N_GX + (tile & (N_GX - 1))) * BINS + local).astype(jnp.int16)
            weight = jnp.broadcast_to(res_ref[...].reshape(1, SND).astype(BF16), (16, SND))
            number = lax.broadcasted_iota(jnp.int32, (16, SND), 0).astype(jnp.int16)
            above = bins - number

            @pl.loop(0, TILES * BINS // 16, unroll=4)
            def _(m):
                hit = above == (m * 16).astype(jnp.int16)
                sel_ref[pl.ds(pl.multiple_of(m * 16, 16), 16), :] = jnp.where(
                    hit, weight, jnp.zeros((16, SND), BF16)
                )

        def sums(k):
            return jnp.dot(
                sel_ref[k * rows : (k + 1) * rows, :],
                fp_ref[...],
                preferred_element_type=F32,
            )

        @pl.when(c == 0)
        def _():
            for k in range(N_GY):
                out = sums(k).astype(BF16)
                for q in range(N_GX):
                    at = (q * N_GY + k) * BINS
                    first_ref[at : at + BINS, :] = out[q * BINS : (q + 1) * BINS]

        @pl.when(c == 1)
        def _():
            for k in range(N_GY):
                out = sums(k)
                refs[k][:rows, :] = out.astype(BF16)
                last = [out[(q + 1) * BINS - 8 : (q + 1) * BINS] for q in range(N_GX)]
                refs[(k + 1) % N_GY][rows:, :] = jnp.concatenate(last, axis=0).astype(BF16)

    one = pl.BlockSpec((SND,), lambda c: (0,))
    each = rows + N_GX * 8
    outs = pl.pallas_call(
        body,
        grid=(2,),
        in_specs=[one] * 4 + [pl.BlockSpec((SND, HALF), lambda c: (0, c))],
        out_specs=[pl.BlockSpec((TILES * BINS, HALF), lambda c: (0, 0))]
        + [pl.BlockSpec((each, HALF), lambda c: (0, 0))] * N_GY,
        out_shape=[jax.ShapeDtypeStruct((TILES * BINS, HALF), BF16)]
        + [jax.ShapeDtypeStruct((each, HALF), BF16)] * N_GY,
        scratch_shapes=[pltpu.VMEM((TILES * BINS, SND), BF16)],
        compiler_params=pltpu.CompilerParams(vmem_limit_bytes=58 * MIB),
        cost_estimate=pl.CostEstimate(
            flops=2 * TILES * BINS * SND * FP, bytes_accessed=8 * MIB, transcendentals=0
        ),
        name="bin_sums",
    )(*ids, residual, footprint)
    return outs[0], outs[1:]


def sum_first(got):
    count, rows, cols = got.shape

    def body(got_ref, *out_refs):
        totals = []
        for k in range(N_GY):
            at = pl.ds(k * BINS, BINS)
            total = got_ref[0, at].astype(F32)
            for s in range(1, count):
                total = total + got_ref[s, at].astype(F32)
            totals.append(total)
        none = jnp.zeros((8, cols), F32)
        for k, out_ref in enumerate(out_refs):
            below = totals[(k + 1) % N_GY][:8]
            out_ref[...] = jnp.concatenate([totals[k], below, none], axis=0).astype(BF16)

    return pl.pallas_call(
        body,
        out_shape=[jax.ShapeDtypeStruct((ROWS, cols), BF16)] * N_GY,
        compiler_params=pltpu.CompilerParams(vmem_limit_bytes=12 * MIB),
        name="sum_first",
    )(got)


def sum_arrays(arrays):
    cols = arrays[0].shape[1]

    def body(*refs):
        def total(at):
            out = refs[0][at].astype(F32)
            for ref in refs[1:-1]:
                out = out + ref[at].astype(F32)
            return out

        above = total(pl.ds(N_GX * BINS, N_GX * 8))
        none = jnp.zeros((8, cols), F32)
        for q in range(N_GX):
            halo = jnp.concatenate([above[q * 8 : q * 8 + 8], none], axis=0)
            refs[-1][q, :BINS] = total(pl.ds(q * BINS, BINS)).astype(BF16)
            refs[-1][q, BINS:] = halo.astype(BF16)

    return pl.pallas_call(
        body,
        out_shape=jax.ShapeDtypeStruct((N_GX, ROWS, cols), BF16),
        compiler_params=pltpu.CompilerParams(vmem_limit_bytes=12 * MIB),
        name="sum_arrays",
    )(*arrays)


def tile_sum(summed, got):
    count = got.shape[0]

    def body(*refs):
        got_ref, adj_ref, low_ref, high_ref, by_row = refs[-5:]
        first = refs[0][...].astype(F32)
        for ref in refs[1:-5]:
            first = first + ref[...].astype(F32)
        last = got_ref[0].astype(F32)
        for s in range(1, count):
            last = last + got_ref[s].astype(F32)
        by_row[...] = jnp.zeros_like(by_row)

        def put(row, part, at, i):
            by_row[pl.ds(row, 8, stride=PAD_LAT), :] = part[
                at : at + 8, i * 128 : i * 128 + 128
            ]

        for i in range(4):
            for br in range(8):
                put(8 + br * 8 + i, first, br * 8, i)
                put(8 + br * 8 + 4 + i, last, br * 8, i)
            put(4 + i, last, BINS, i)
            put(8 + LAT + i, first, BINS, i)
        for t in range(TS_DEV):
            for bc in range(2):
                at = (t * 2 + bc) * PAD_LAT
                adj_ref[t, :, bc * 128 : bc * 128 + 128] = by_row[at : at + PAD_LAT]
        low_ref[...] = adj_ref[:HB].astype(BF16)
        high_ref[...] = adj_ref[TS_DEV - HB :].astype(BF16)

    return pl.pallas_call(
        body,
        out_shape=[
            jax.ShapeDtypeStruct((TS_DEV, PAD_LAT, LON), F32),
            jax.ShapeDtypeStruct((HB, PAD_LAT, LON), BF16),
            jax.ShapeDtypeStruct((HB, PAD_LAT, LON), BF16),
        ],
        scratch_shapes=[pltpu.VMEM((TS_DEV * 2 * PAD_LAT, 128), F32)],
        compiler_params=pltpu.CompilerParams(vmem_limit_bytes=8 * MIB),
        name="tile_sum",
    )(*summed, got)


def put_strips(strip, dtype):
    rows = strip[0].shape[0]
    lane = lax.broadcasted_iota(jnp.int32, (rows, 128), 1)

    def packed(planes, side):
        out = jnp.zeros((rows, 128), F32)
        for k, plane in enumerate(planes):
            if side == 0:
                part = plane[:, :128]
                shift = HALO * k
            else:
                part = plane[:, LON - 128 :]
                shift = HALO * k + HALO
            moved = pltpu.roll(part, shift % 128, 1) if shift % 128 else part
            out = jnp.where((lane >= HALO * k) & (lane < HALO * k + HALO), moved, out)
        return out.astype(dtype)

    return packed(strip, 0), packed(strip, 1)


def pack_lon(arrays, dtype, name):
    counts = [a.shape[0] for a in arrays]

    def body(*refs):
        planes = [
            ref[k].astype(F32) for ref, count in zip(refs, counts) for k in range(count)
        ]
        refs[-2][...], refs[-1][...] = put_strips(planes, dtype)

    return pl.pallas_call(
        body,
        out_shape=[jax.ShapeDtypeStruct((arrays[0].shape[1], 128), dtype)] * 2,
        compiler_params=pltpu.CompilerParams(vmem_limit_bytes=8 * MIB),
        name=name,
    )(*arrays)


def pack_lat(arrays, from_left, from_right, dtype, name):
    counts = [a.shape[0] for a in arrays]
    n = sum(counts)

    def body(*refs):
        up_ref, down_ref = refs[-2:]
        strips = jnp.concatenate(
            [refs[-4][...].astype(F32), refs[-3][...].astype(F32)], axis=1
        )
        planes = [
            ref[k].astype(F32) for ref, count in zip(refs, counts) for k in range(count)
        ] + [strips]
        up = jnp.concatenate([p[:HALO] for p in planes], axis=0)
        down = jnp.concatenate([p[LAT - HALO :] for p in planes], axis=0)
        up_ref[...] = up.astype(dtype)
        down_ref[...] = down.astype(dtype)

    return pl.pallas_call(
        body,
        out_shape=[jax.ShapeDtypeStruct(((n + 1) * HALO, LON), dtype)] * 2,
        compiler_params=pltpu.CompilerParams(vmem_limit_bytes=8 * MIB),
        name=name,
    )(*arrays, from_left, from_right)


def beside_lon(k, plane, left, right):
    lane = lax.broadcasted_iota(jnp.int32, right.shape, 1)
    to_right = (-HALO * k) % 128
    to_left = (128 - HALO - HALO * k) % 128
    right = pltpu.roll(right, to_right, 1) if to_right else right
    left = pltpu.roll(left, to_left, 1) if to_left else left
    side = jnp.where(lane < HALO, right, jnp.where(lane >= 128 - HALO, left, 0.0))
    return jnp.concatenate([plane, side], axis=1)


def planes_of(refs):
    return [ref[k].astype(F32) for ref in refs for k in range(ref.shape[0])]


def pad_static(arrays, left, right, up, down):
    n = TRACERS + 1

    def body(*refs):
        l_ref, r_ref, u_ref, w_ref, out_ref = refs[-5:]
        none = [jnp.zeros((8 - HALO, 128), F32), jnp.zeros((8 - HALO, LON), F32)]

        def rows(top, mid, low):
            zero = none[mid.shape[1] // LON]
            return jnp.concatenate([zero, top, mid, low, zero], axis=0)

        def end(ref, side):
            return ref[n * HALO : (n + 1) * HALO, side * 128 : side * 128 + 128]

        left_ = rows(end(u_ref, 0), l_ref[...], end(w_ref, 0))
        right_ = rows(end(u_ref, 1), r_ref[...], end(w_ref, 1))
        for k, plane in enumerate(planes_of(refs[:-5])):
            at = pl.ds(k * HALO, HALO)
            out_ref[k] = beside_lon(k, rows(u_ref[at], plane, w_ref[at]), left_, right_)

    return pl.pallas_call(
        body,
        out_shape=jax.ShapeDtypeStruct((n, PAD_LAT, PAD_LON), F32),
        compiler_params=pltpu.CompilerParams(vmem_limit_bytes=8 * MIB),
        name="pad_static",
    )(*arrays, left, right, up, down)


def diffuse(arrays, left, right, static, taps):
    n = TS_DEV + 2 * HB

    def body(taps_ref, *refs):
        l_ref, r_ref, st_ref, out_ref, pad_ref = refs[-5:]
        c = pl.program_id(0)

        @pl.when(c == 0)
        def _():
            for k, plane in enumerate(planes_of(refs[:-5])):
                pad_ref[k] = beside_lon(k, plane, l_ref[...], r_ref[...])

        banded = taps_ref[c, 0] * pad_ref[0:TS_DEV]
        for k in range(1, 2 * HB + 1):
            banded = banded + taps_ref[c, k] * pad_ref[k : k + TS_DEV]
        field = st_ref[c][None] * banded
        rate = st_ref[TRACERS][None]
        for _ in range(KSTEPS):
            beside = (
                pltpu.roll(field, 1, 2)
                + pltpu.roll(field, PAD_LON - 1, 2)
                + pltpu.roll(field, 1, 1)
                + pltpu.roll(field, PAD_LAT - 1, 1)
            )
            field = field + rate * (beside - 4.0 * field)
        scale = st_ref[c, 8 : 8 + LAT, :LON]
        out_ref[0] = scale[None] * field[:, 8 : 8 + LAT, :LON]

    def whole(a):
        return pl.BlockSpec(a.shape, lambda c: (0,) * a.ndim)

    operands = (*arrays, left, right, static)
    return pl.pallas_call(
        body,
        grid=(TRACERS,),
        in_specs=[pl.BlockSpec(memory_space=pltpu.SMEM)] + [whole(a) for a in operands],
        out_specs=pl.BlockSpec((1, TS_DEV, LAT, LON), lambda c: (c, 0, 0, 0)),
        out_shape=jax.ShapeDtypeStruct((TRACERS, TS_DEV, LAT, LON), F32),
        scratch_shapes=[pltpu.VMEM((n, PAD_LAT, PAD_LON), F32)],
        compiler_params=pltpu.CompilerParams(vmem_limit_bytes=20 * MIB),
        name="diffuse",
    )(taps, *operands)


def steps(axis, periodic):
    count = lax.axis_size(axis)
    forward = [(i, i + 1) for i in range(count - 1)]
    if periodic:
        forward.append((count - 1, 0))
    return forward, [(b, a) for a, b in forward]


def along_gy(parts):
    return [parts[0]] + [
        lax.ppermute(parts[k], "gy", [(i, (i + k) % N_GY) for i in range(N_GY)])
        for k in range(1, N_GY)
    ]


def along_gx(rows):
    return lax.all_to_all(rows, "gx", 0, 0, tiled=True)


def per_device(residual, footprint, tile_id, step_id, block_id, sigma, taps, diffusivity):
    east, west = steps("gx", True)
    south, north = steps("gy", False)
    later, sooner = steps("ta", False)
    ids = (tile_id[:, 0], step_id, block_id)
    first_gx, first_gy = bin_sums(ids, residual, footprint)
    got_gx = along_gx(first_gx.reshape(N_GX, N_GY * BINS, HALF))
    came_gy = along_gy(first_gy)

    fixed = (sigma, diffusivity[None])
    fixed, first_gy = lax.optimization_barrier((fixed, first_gy))
    to_left, to_right = pack_lon(fixed, F32, "static_lon")
    left = lax.ppermute(to_right, "gx", east)
    right = lax.ppermute(to_left, "gx", west)
    to_up, to_down = pack_lat(fixed, left, right, F32, "static_lat")
    up = lax.ppermute(to_down, "gy", south)
    down = lax.ppermute(to_up, "gy", north)
    static = pad_static(fixed, left, right, up, down)
    static, came_gy = lax.optimization_barrier((static, came_gy))

    all_gx = along_gy(sum_first(got_gx))
    all_gy = along_gx(sum_arrays(came_gy))
    adj, low, high = tile_sum(all_gx, all_gy)
    before = lax.ppermute(high, "ta", later)
    after = lax.ppermute(low, "ta", sooner)
    arrays = (before, adj, after)
    to_left, to_right = pack_lon(arrays, F32, "adjoint_lon")
    left = lax.ppermute(to_right, "gx", east)
    right = lax.ppermute(to_left, "gx", west)
    return diffuse(arrays, left, right, static, taps)


def solution(mesh):
    return jax.shard_map(
        per_device,
        mesh=mesh,
        in_specs=(
            P(("ta", "gy", "gx")),
            P(("ta", "gy", "gx"), None),
            P(("ta", "gy", "gx"), None),
            P(("ta", "gy", "gx")),
            P(("ta", "gy", "gx")),
            P(None, "gy", "gx"),
            P(),
            P("gy", "gx"),
        ),
        out_specs=P(None, "ta", "gy", "gx"),
        check_vma=False,
    )
```

time: 101 us -> 98.7 us (0.977)
  Pallas kernels: 26.4 us -> 23.3 us
  starting transfers between devices: 38.5 us -> 40.4 us
  other arithmetic: 1.28 us -> 0 us
  waiting for transfers between devices: 33.3 us -> 34.4 us
    ppermute x6, waiting for transfers between devices: 22.3 us -> 0.02 us  [along_gy(): lax.ppermute(parts[k], 'gy', [(i, (i + k) % N_GY) for i in range(N_GY)])]
    ppermute x1 -> x2, waiting for transfers between devices: 1.3 us -> 20.3 us  [per_device(): left = lax.ppermute(to_right, 'gx', east)]
    pallas_call x7 -> x8, Pallas kernels: 26.4 us -> 23.3 us  [the longest x1 14 us: bin_sums(): pl.pallas_call(body, grid=(2,), in_specs=[one] * 4 + [pl.BlockSpec((SND,...]
    ppermute x1 -> x2, starting transfers between devices: 3.3 us -> 5.76 us  [per_device(): right = lax.ppermute(to_left, 'gx', west)]
    ppermute x1, waiting for transfers between devices: 0.01 us -> 2.41 us  [per_device(): down = lax.ppermute(to_up, 'gy', north)]
    ppermute x1, starting transfers between devices: 7.74 us -> 9.86 us  [per_device(): before = lax.ppermute(high, 'ta', later)]
    ppermute x6, starting transfers between devices: 8.72 us -> 6.84 us  [along_gy(): lax.ppermute(parts[k], 'gy', [(i, (i + k) % N_GY) for i in range(N_GY)])]
    all_to_all x2, starting transfers between devices: 11 us -> 9.23 us  [along_gx(): return lax.all_to_all(rows, 'gx', 0, 0, tiled=True)]
  transfers between devices with their start and end apart: 14 -> 16, of which waited for: 6 -> 5; matrix products, arithmetic and copies ran while one was open for 0% -> 0% of each run, Pallas kernels for 8% -> 2%
where the time goes in v5:
time: 98.7 us; the launch traced here: 98.4 us
  starting transfers between devices  40.4 us (41%)
  waiting for transfers between devices  34.4 us (35%)
  Pallas kernels  23.3 us (24%)
    ppermute x2, waiting for transfers between devices, per_device(): left = lax.ppermute(to_right, 'gx', east)  20.3 us
    pallas_call x1, Pallas kernels, bin_sums(): pl.pallas_call(body, grid=(2,), in_specs=[one] * 4 + [pl.BlockSpec((SND,...  14 us
    ppermute x1, starting transfers between devices, per_device(): before = lax.ppermute(high, 'ta', later)  9.86 us
    all_to_all x2, starting transfers between devices, along_gx(): return lax.all_to_all(rows, 'gx', 0, 0, tiled=True)  9.23 us
    ppermute x1, waiting for transfers between devices, per_device(): after = lax.ppermute(low, 'ta', sooner)  7.1 us
    ppermute x6, starting transfers between devices, along_gy(): lax.ppermute(parts[k], 'gy', [(i, (i + k) % N_GY) for i in range(N_GY)])  6.84 us
    pallas_call x1, Pallas kernels, diffuse(): pl.pallas_call(body, grid=(TRACERS,), in_specs=[pl.BlockSpec(memory_space...  6.71 us
    ppermute x2, starting transfers between devices, per_device(): right = lax.ppermute(to_left, 'gx', west)  5.76 us
  transfers between devices with their start and end apart: 16, of which 5 were waited for; matrix products, arithmetic and copies ran while one was open for 0% of the time, Pallas kernels for 2%

profile of v5, /device:TPU:67, one launch (start us, length us, event | category | flops | bytes accessed | tf_op | source)
XLA Modules:
  0.0 98.4 jit_solution(14022687365601062316)
XLA Ops:
  0.0 14.0 %bin_sums.1 = (bf16[2048,512]{1,0:T(8,128)(2,1)}, bf16[576,512]{1,0:T(8,128)(2,1)}, bf16[576,512]{1,0:T(8,128)(2,1)}, bf16[576,512]{1,0:T(8,128)(2,1)}, bf16[576,512]{1,0:T(8,128)(2,1)}) custom-call(s32[2048]{0:T(1024)} %bitcast.7, s32[2048]{0:T(1024)} %step_ref.1, s32[2048]{0:T(1024)} %block_ref.1, bf16[2048]{0:T(1024)(128)(2,1)} %res_ref.1, ...), custom_call_target="tpu_custom_call" | custom-call | flops 8589934592 | bytes 8388608 | tf_op jit(solution)/shard_map/bin_sums/pallas_call | solution.py:80
  14.0 5.7 %all-to-all-start = ((bf16[8,256,512]{2,1,0:T(8,128)(2,1)}), bf16[8,256,512]{2,1,0:T(8,128)(2,1)S(1)}, u32[]{:S(2)}, u32[]{:S(2)}) async-start(bf16[8,256,512]{2,1,0:T(8,128)(2,1)} %bitcast.6), calls=%async_computation | async-start | bytes 4194304 | tf_op jit(solution)/shard_map/all_to_all | solution.py:355
  19.6 1.3 %collective-permute-start.7 = (bf16[576,512]{1,0:T(8,128)(2,1)}, bf16[576,512]{1,0:T(8,128)(2,1)S(1)}, u32[]{:S(2)}, u32[]{:S(2)}) collective-permute-start(bf16[576,512]{1,0:T(8,128)(2,1)} %get-tuple-element.36), channel_id=1, source_target_pairs={{0,8},{8,16},{16,24},{24,0},{1,9},{9,17},{17,25},{25,1},{2,10},{10... | collective-permute-start | bytes 1769480 | tf_op jit(solution)/shard_map/ppermute | solution.py:349
  20.9 0.8 collective-permute-start.8
  21.8 1.9 %collective-permute-start.9 = (bf16[576,512]{1,0:T(8,128)(2,1)}, bf16[576,512]{1,0:T(8,128)(2,1)S(1)}, u32[]{:S(2)}, u32[]{:S(2)}) collective-permute-start(bf16[576,512]{1,0:T(8,128)(2,1)} %get-tuple-element.38), channel_id=1, source_target_pairs={{0,24},{8,0},{16,8},{24,16},{1,25},{9,1},{17,9},{25,17},{2,26},{10... | collective-permute-start | bytes 1769480 | tf_op jit(solution)/shard_map/ppermute | solution.py:349
  23.7 0.1 static_lon.1
  23.8 1.5 %collective-permute-start.3 = (f32[64,128]{1,0:T(8,128)S(1)}, f32[64,128]{1,0:T(8,128)S(1)}, u32[]{:S(2)}, u32[]{:S(2)}) collective-permute-start(f32[64,128]{1,0:T(8,128)S(1)} %get-tuple-element.41), channel_id=1, source_target_pairs={{0,1},{1,2},{2,3},{3,4},{4,5},{5,6},{6,7},{7,0},{8,9},{9,10},{10,1... | collective-permute-start | bytes 98312 | tf_op jit(solution)/shard_map/ppermute | solution.py:370
  25.3 2.2 %collective-permute-start.4 = (f32[64,128]{1,0:T(8,128)S(1)}, f32[64,128]{1,0:T(8,128)S(1)}, u32[]{:S(2)}, u32[]{:S(2)}) collective-permute-start(f32[64,128]{1,0:T(8,128)S(1)} %get-tuple-element.42), channel_id=1, source_target_pairs={{1,0},{2,1},{3,2},{4,3},{5,4},{6,5},{7,6},{0,7},{9,8},{10,9},{11,1... | collective-permute-start | bytes 98312 | tf_op jit(solution)/shard_map/ppermute | solution.py:371
  27.5 18.9 %collective-permute-done.3.refs_2_ = f32[64,128]{1,0:T(8,128)S(1)} collective-permute-done((f32[64,128]{1,0:T(8,128)S(1)}, f32[64,128]{1,0:T(8,128)S(1)}, u32[]{:S(2)}, u32[]{:S(2)}) %collective-permute-start.3) | collective-permute-done | bytes 32800 | tf_op jit(solution)/shard_map/ppermute | solution.py:370
  46.4 3.1 %collective-permute-start.5 = (f32[24,256]{1,0:T(8,128)S(1)}, f32[24,256]{1,0:T(8,128)S(1)}, u32[]{:S(2)}, u32[]{:S(2)}) collective-permute-start(f32[24,256]{1,0:T(8,128)S(1)} %get-tuple-element.43), channel_id=1, source_target_pairs={{0,8},{8,16},{16,24},{1,9},{9,17},{17,25},{2,10},{10,18},{18,26},{... | collective-permute-start | bytes 73736 | tf_op jit(solution)/shard_map/ppermute | solution.py:373
  49.6 2.1 %collective-permute-start.6 = (f32[24,256]{1,0:T(8,128)S(1)}, f32[24,256]{1,0:T(8,128)S(1)}, u32[]{:S(2)}, u32[]{:S(2)}) collective-permute-start(f32[24,256]{1,0:T(8,128)S(1)} %get-tuple-element.44), channel_id=1, source_target_pairs={{8,0},{16,8},{24,16},{9,1},{17,9},{25,17},{10,2},{18,10},{26,18},{... | collective-permute-start | bytes 73736 | tf_op jit(solution)/shard_map/ppermute | solution.py:374
  51.7 2.4 %collective-permute-done.6.refs_5_ = f32[24,256]{1,0:T(8,128)S(1)} collective-permute-done((f32[24,256]{1,0:T(8,128)S(1)}, f32[24,256]{1,0:T(8,128)S(1)}, u32[]{:S(2)}, u32[]{:S(2)}) %collective-permute-start.6) | collective-permute-done | bytes 24608 | tf_op jit(solution)/shard_map/ppermute | solution.py:374
  54.1 0.2 pad_static.1.refs_5_
  54.3 0.0 collective-permute-done.7.refs_1_
  54.3 1.1 %sum_arrays.1 = bf16[8,80,512]{2,1,0:T(8,128)(2,1)} custom-call(bf16[576,512]{1,0:T(8,128)(2,1)S(1)} %copy-done.2, bf16[576,512]{1,0:T(8,128)(2,1)S(1)} %collective-permute-done.7.refs_1_, bf16[576,512]{1,0:T(8,128)(2,1)S(1)} %collective-permute-done.8.refs_2_, bf16[576,512]{1,0:T(8,128)(2,1)S(1)} %collective-permute-done.9.refs_3_), custom_call_target="tpu_custom_call" | custom-call | tf_op jit(solution)/shard_map/sum_arrays/pallas_call | solution.py:139
  55.5 0.0 all-to-all-done.got_ref
  55.5 3.5 %all-to-all-start.1 = ((bf16[8,80,512]{2,1,0:T(8,128)(2,1)}), bf16[8,80,512]{2,1,0:T(8,128)(2,1)S(1)}, u32[]{:S(2)}, u32[]{:S(2)}) async-start(bf16[8,80,512]{2,1,0:T(8,128)(2,1)} %sum_arrays.1), calls=%async_computation.1 | async-start | bytes 1310720 | tf_op jit(solution)/shard_map/all_to_all | solution.py:355
  59.0 0.0 copy-start.3
  59.0 0.8 sum_first.1
  59.8 1.1 %collective-permute-start = (bf16[80,512]{1,0:T(8,128)(2,1)}, bf16[80,512]{1,0:T(8,128)(2,1)S(1)}, u32[]{:S(2)}, u32[]{:S(2)}) collective-permute-start(bf16[80,512]{1,0:T(8,128)(2,1)} %get-tuple-element.32), channel_id=1, source_target_pairs={{0,8},{8,16},{16,24},{24,0},{1,9},{9,17},{17,25},{25,1},{2,10},{10... | collective-permute-start | bytes 245768 | tf_op jit(solution)/shard_map/ppermute | solution.py:349
  60.9 1.0 collective-permute-start.1
  61.9 0.8 collective-permute-start.2
  62.7 4.6 %all-to-all-done.1.refs_4_ = bf16[8,80,512]{2,1,0:T(8,128)(2,1)S(1)} async-done(((bf16[8,80,512]{2,1,0:T(8,128)(2,1)}), bf16[8,80,512]{2,1,0:T(8,128)(2,1)S(1)}, u32[]{:S(2)}, u32[]{:S(2)}) %all-to-all-start.1) | async-done | bytes 655392 | tf_op jit(solution)/shard_map/all_to_all | solution.py:355
  67.2 0.3 tile_sum.1
  67.5 9.9 %collective-permute-start.10 = (bf16[2,80,256]{2,1,0:T(8,128)(2,1)S(1)}, bf16[2,80,256]{2,1,0:T(8,128)(2,1)S(1)}, u32[]{:S(2)}, u32[]{:S(2)}) collective-permute-start(bf16[2,80,256]{2,1,0:T(8,128)(2,1)S(1)} %get-tuple-element.49), channel_id=1, source_target_pairs={{0,32},{32,64},{64,96},{96,128},{128,160},{160,192},{192,224},{1,3... | collective-permute-start | bytes 245768 | tf_op jit(solution)/shard_map/ppermute | solution.py:381
  77.4 1.9 %collective-permute-start.11 = (bf16[2,80,256]{2,1,0:T(8,128)(2,1)S(1)}, bf16[2,80,256]{2,1,0:T(8,128)(2,1)S(1)}, u32[]{:S(2)}, u32[]{:S(2)}) collective-permute-start(bf16[2,80,256]{2,1,0:T(8,128)(2,1)S(1)} %get-tuple-element.51), channel_id=1, source_target_pairs={{32,0},{64,32},{96,64},{128,96},{160,128},{192,160},{224,192},{33,... | collective-permute-start | bytes 245768 | tf_op jit(solution)/shard_map/ppermute | solution.py:382
  79.3 7.1 %collective-permute-done.11.refs_2_ = bf16[2,80,256]{2,1,0:T(8,128)(2,1)S(1)} collective-permute-done((bf16[2,80,256]{2,1,0:T(8,128)(2,1)S(1)}, bf16[2,80,256]{2,1,0:T(8,128)(2,1)S(1)}, u32[]{:S(2)}, u32[]{:S(2)}) %collective-permute-start.11) | collective-permute-done | bytes 81952 | tf_op jit(solution)/shard_map/ppermute | solution.py:382
  86.4 0.2 adjoint_lon.1
  86.6 0.1 collective-permute-start.12
  86.7 3.6 %collective-permute-start.13 = (f32[80,128]{1,0:T(8,128)S(1)}, f32[80,128]{1,0:T(8,128)S(1)}, u32[]{:S(2)}, u32[]{:S(2)}) collective-permute-start(f32[80,128]{1,0:T(8,128)S(1)} %get-tuple-element.53), channel_id=1, source_target_pairs={{1,0},{2,1},{3,2},{4,3},{5,4},{6,5},{7,6},{0,7},{9,8},{10,9},{11,1... | collective-permute-start | bytes 122888 | tf_op jit(solution)/shard_map/ppermute | solution.py:386
  90.3 1.4 %collective-permute-done.12.refs_3_ = f32[80,128]{1,0:T(8,128)S(1)} collective-permute-done((f32[80,128]{1,0:T(8,128)S(1)}, f32[80,128]{1,0:T(8,128)S(1)}, u32[]{:S(2)}, u32[]{:S(2)}) %collective-permute-start.12) | collective-permute-done | bytes 40992 | tf_op jit(solution)/shard_map/ppermute | solution.py:385
  91.7 6.7 %diffuse.1 = f32[4,4,64,256]{3,2,1,0:T(8,128)} custom-call(f32[4,5]{1,0:T(4,128)S(1)} %copy-done.3, bf16[2,80,256]{2,1,0:T(8,128)(2,1)S(1)} %collective-permute-done.10.refs_0_, f32[4,80,256]{2,1,0:T(8,128)S(1)} %get-tuple-element.50.refs_1_, bf16[2,80,256]{2,1,0:T(8,128)(2,1)S(1)} %collective-permute-done.11.refs_2_, ...), custom_call_target="tpu_custom_call" | custom-call | tf_op jit(solution)/shard_map/diffuse/pallas_call | solution.py:327
  (17 shorter events, 0.0 us)
Async XLA Ops:
  14.0 9.7 %copy-start = (f32[4,64,256]{2,1,0:T(8,128)S(1)}, f32[4,64,256]{2,1,0:T(8,128)}, u32[]{:S(2)}) copy-start(f32[4,64,256]{2,1,0:T(8,128)} %refs_0_.2) | copy-start | bytes 786436
  14.0 9.7 %copy-start.1 = (f32[64,256]{1,0:T(8,128)S(1)}, f32[64,256]{1,0:T(8,128)}, u32[]{:S(2)}) copy-start(f32[64,256]{1,0:T(8,128)} %param.15) | copy-start | bytes 196612
  14.0 41.5 %all-to-all-start = ((bf16[8,256,512]{2,1,0:T(8,128)(2,1)}), bf16[8,256,512]{2,1,0:T(8,128)(2,1)S(1)}, u32[]{:S(2)}, u32[]{:S(2)}) async-start(bf16[8,256,512]{2,1,0:T(8,128)(2,1)} %bitcast.6), calls=%async_computation | async-start | bytes 4194304 | tf_op jit(solution)/shard_map/all_to_all | solution.py:355
  19.6 34.7 %copy-start.2 = (bf16[576,512]{1,0:T(8,128)(2,1)S(1)}, bf16[576,512]{1,0:T(8,128)(2,1)}, u32[]{:S(2)}) copy-start(bf16[576,512]{1,0:T(8,128)(2,1)} %get-tuple-element.45.refs_0_) | copy-start | bytes 1769476
  19.6 34.7 %collective-permute-start.7 = (bf16[576,512]{1,0:T(8,128)(2,1)}, bf16[576,512]{1,0:T(8,128)(2,1)S(1)}, u32[]{:S(2)}, u32[]{:S(2)}) collective-permute-start(bf16[576,512]{1,0:T(8,128)(2,1)} %get-tuple-element.36), channel_id=1, source_target_pairs={{0,8},{8,16},{16,24},{24,0},{1,9},{9,17},{17,25},{25,1},{2,10},{10... | collective-permute-start | bytes 1769480 | tf_op jit(solution)/shard_map/ppermute | solution.py:349
  20.9 33.4 %collective-permute-start.8 = (bf16[576,512]{1,0:T(8,128)(2,1)}, bf16[576,512]{1,0:T(8,128)(2,1)S(1)}, u32[]{:S(2)}, u32[]{:S(2)}) collective-permute-start(bf16[576,512]{1,0:T(8,128)(2,1)} %get-tuple-element.37), channel_id=1, source_target_pairs={{0,16},{8,24},{16,0},{24,8},{1,17},{9,25},{17,1},{25,9},{2,18},{10... | collective-permute-start | bytes 1769480 | tf_op jit(solution)/shard_map/ppermute | solution.py:349
  21.8 32.6 %collective-permute-start.9 = (bf16[576,512]{1,0:T(8,128)(2,1)}, bf16[576,512]{1,0:T(8,128)(2,1)S(1)}, u32[]{:S(2)}, u32[]{:S(2)}) collective-permute-start(bf16[576,512]{1,0:T(8,128)(2,1)} %get-tuple-element.38), channel_id=1, source_target_pairs={{0,24},{8,0},{16,8},{24,16},{1,25},{9,1},{17,9},{25,17},{2,26},{10... | collective-permute-start | bytes 1769480 | tf_op jit(solution)/shard_map/ppermute | solution.py:349
  23.8 22.6 %collective-permute-start.3 = (f32[64,128]{1,0:T(8,128)S(1)}, f32[64,128]{1,0:T(8,128)S(1)}, u32[]{:S(2)}, u32[]{:S(2)}) collective-permute-start(f32[64,128]{1,0:T(8,128)S(1)} %get-tuple-element.41), channel_id=1, source_target_pairs={{0,1},{1,2},{2,3},{3,4},{4,5},{5,6},{6,7},{7,0},{8,9},{9,10},{10,1... | collective-permute-start | bytes 98312 | tf_op jit(solution)/shard_map/ppermute | solution.py:370
  25.3 21.1 %collective-permute-start.4 = (f32[64,128]{1,0:T(8,128)S(1)}, f32[64,128]{1,0:T(8,128)S(1)}, u32[]{:S(2)}, u32[]{:S(2)}) collective-permute-start(f32[64,128]{1,0:T(8,128)S(1)} %get-tuple-element.42), channel_id=1, source_target_pairs={{1,0},{2,1},{3,2},{4,3},{5,4},{6,5},{7,6},{0,7},{9,8},{10,9},{11,1... | collective-permute-start | bytes 98312 | tf_op jit(solution)/shard_map/ppermute | solution.py:371
  46.4 5.3 %collective-permute-start.5 = (f32[24,256]{1,0:T(8,128)S(1)}, f32[24,256]{1,0:T(8,128)S(1)}, u32[]{:S(2)}, u32[]{:S(2)}) collective-permute-start(f32[24,256]{1,0:T(8,128)S(1)} %get-tuple-element.43), channel_id=1, source_target_pairs={{0,8},{8,16},{16,24},{1,9},{9,17},{17,25},{2,10},{10,18},{18,26},{... | collective-permute-start | bytes 73736 | tf_op jit(solution)/shard_map/ppermute | solution.py:373
  49.6 4.6 %collective-permute-start.6 = (f32[24,256]{1,0:T(8,128)S(1)}, f32[24,256]{1,0:T(8,128)S(1)}, u32[]{:S(2)}, u32[]{:S(2)}) collective-permute-start(f32[24,256]{1,0:T(8,128)S(1)} %get-tuple-element.44), channel_id=1, source_target_pairs={{8,0},{16,8},{24,16},{9,1},{17,9},{25,17},{10,2},{18,10},{26,18},{... | collective-permute-start | bytes 73736 | tf_op jit(solution)/shard_map/ppermute | solution.py:374
  55.5 11.8 %all-to-all-start.1 = ((bf16[8,80,512]{2,1,0:T(8,128)(2,1)}), bf16[8,80,512]{2,1,0:T(8,128)(2,1)S(1)}, u32[]{:S(2)}, u32[]{:S(2)}) async-start(bf16[8,80,512]{2,1,0:T(8,128)(2,1)} %sum_arrays.1), calls=%async_computation.1 | async-start | bytes 1310720 | tf_op jit(solution)/shard_map/all_to_all | solution.py:355
  59.0 32.6 %copy-start.3 = (f32[4,5]{1,0:T(4,128)S(1)}, f32[4,5]{1,0:T(4,128)}, u32[]{:S(2)}) copy-start(f32[4,5]{1,0:T(4,128)} %taps_ref.1) | copy-start | bytes 244
  59.8 7.4 %collective-permute-start = (bf16[80,512]{1,0:T(8,128)(2,1)}, bf16[80,512]{1,0:T(8,128)(2,1)S(1)}, u32[]{:S(2)}, u32[]{:S(2)}) collective-permute-start(bf16[80,512]{1,0:T(8,128)(2,1)} %get-tuple-element.32), channel_id=1, source_target_pairs={{0,8},{8,16},{16,24},{24,0},{1,9},{9,17},{17,25},{25,1},{2,10},{10... | collective-permute-start | bytes 245768 | tf_op jit(solution)/shard_map/ppermute | solution.py:349
  60.9 6.4 %collective-permute-start.1 = (bf16[80,512]{1,0:T(8,128)(2,1)}, bf16[80,512]{1,0:T(8,128)(2,1)S(1)}, u32[]{:S(2)}, u32[]{:S(2)}) collective-permute-start(bf16[80,512]{1,0:T(8,128)(2,1)} %get-tuple-element.33), channel_id=1, source_target_pairs={{0,16},{8,24},{16,0},{24,8},{1,17},{9,25},{17,1},{25,9},{2,18},{10... | collective-permute-start | bytes 245768 | tf_op jit(solution)/shard_map/ppermute | solution.py:349
  61.9 5.4 %collective-permute-start.2 = (bf16[80,512]{1,0:T(8,128)(2,1)S(1)}, bf16[80,512]{1,0:T(8,128)(2,1)S(1)}, u32[]{:S(2)}, u32[]{:S(2)}) collective-permute-start(bf16[80,512]{1,0:T(8,128)(2,1)S(1)} %get-tuple-element.34), channel_id=1, source_target_pairs={{0,24},{8,0},{16,8},{24,16},{1,25},{9,1},{17,9},{25,17},{2,26},{10... | collective-permute-start | bytes 245768 | tf_op jit(solution)/shard_map/ppermute | solution.py:349
  67.5 11.8 %collective-permute-start.10 = (bf16[2,80,256]{2,1,0:T(8,128)(2,1)S(1)}, bf16[2,80,256]{2,1,0:T(8,128)(2,1)S(1)}, u32[]{:S(2)}, u32[]{:S(2)}) collective-permute-start(bf16[2,80,256]{2,1,0:T(8,128)(2,1)S(1)} %get-tuple-element.49), channel_id=1, source_target_pairs={{0,32},{32,64},{64,96},{96,128},{128,160},{160,192},{192,224},{1,3... | collective-permute-start | bytes 245768 | tf_op jit(solution)/shard_map/ppermute | solution.py:381
  77.4 9.0 %collective-permute-start.11 = (bf16[2,80,256]{2,1,0:T(8,128)(2,1)S(1)}, bf16[2,80,256]{2,1,0:T(8,128)(2,1)S(1)}, u32[]{:S(2)}, u32[]{:S(2)}) collective-permute-start(bf16[2,80,256]{2,1,0:T(8,128)(2,1)S(1)} %get-tuple-element.51), channel_id=1, source_target_pairs={{32,0},{64,32},{96,64},{128,96},{160,128},{192,160},{224,192},{33,... | collective-permute-start | bytes 245768 | tf_op jit(solution)/shard_map/ppermute | solution.py:382
  86.6 5.0 %collective-permute-start.12 = (f32[80,128]{1,0:T(8,128)S(1)}, f32[80,128]{1,0:T(8,128)S(1)}, u32[]{:S(2)}, u32[]{:S(2)}) collective-permute-start(f32[80,128]{1,0:T(8,128)S(1)} %get-tuple-element.52), channel_id=1, source_target_pairs={{0,1},{1,2},{2,3},{3,4},{4,5},{5,6},{6,7},{7,0},{8,9},{9,10},{10,1... | collective-permute-start | bytes 122888 | tf_op jit(solution)/shard_map/ppermute | solution.py:385
  86.7 5.0 %collective-permute-start.13 = (f32[80,128]{1,0:T(8,128)S(1)}, f32[80,128]{1,0:T(8,128)S(1)}, u32[]{:S(2)}, u32[]{:S(2)}) collective-permute-start(f32[80,128]{1,0:T(8,128)S(1)} %get-tuple-element.53), channel_id=1, source_target_pairs={{1,0},{2,1},{3,2},{4,3},{5,4},{6,5},{7,6},{0,7},{9,8},{10,9},{11,1... | collective-permute-start | bytes 122888 | tf_op jit(solution)/shard_map/ppermute | solution.py:386

commit v6 on v5

--- a/solution.py
+++ b/solution.py
@@ -225,29 +225,38 @@
     )(*arrays)
 
 
-def pack_lat(arrays, from_left, from_right, dtype, name):
-    counts = [a.shape[0] for a in arrays]
-    n = sum(counts)
-
-    def body(*refs):
-        up_ref, down_ref = refs[-2:]
-        strips = jnp.concatenate(
-            [refs[-4][...].astype(F32), refs[-3][...].astype(F32)], axis=1
-        )
-        planes = [
-            ref[k].astype(F32) for ref, count in zip(refs, counts) for k in range(count)
-        ] + [strips]
-        up = jnp.concatenate([p[:HALO] for p in planes], axis=0)
-        down = jnp.concatenate([p[LAT - HALO :] for p in planes], axis=0)
-        up_ref[...] = up.astype(dtype)
-        down_ref[...] = down.astype(dtype)
-
-    return pl.pallas_call(
-        body,
-        out_shape=[jax.ShapeDtypeStruct(((n + 1) * HALO, LON), dtype)] * 2,
+def pack_rows(arrays):
+    n = sum(a.shape[0] for a in arrays)
+
+    def body(*refs):
+        planes = planes_of(refs[:-2])
+        refs[-2][...] = jnp.concatenate([p[:HALO] for p in planes], axis=0)
+        refs[-1][...] = jnp.concatenate([p[LAT - HALO :] for p in planes], axis=0)
+
+    return pl.pallas_call(
+        body,
+        out_shape=[jax.ShapeDtypeStruct((n * HALO, LON), F32)] * 2,
         compiler_params=pltpu.CompilerParams(vmem_limit_bytes=8 * MIB),
-        name=name,
-    )(*arrays, from_left, from_right)
+        name="static_rows",
+    )(*arrays)
+
+
+def beside_lat(arrays, up, down):
+    n = sum(a.shape[0] for a in arrays)
+
+    def body(*refs):
+        u_ref, w_ref, out_ref = refs[-3:]
+        zero = jnp.zeros((8 - HALO, LON), F32)
+        for k, plane in enumerate(planes_of(refs[:-3])):
+            at = pl.ds(k * HALO, HALO)
+            out_ref[k] = jnp.concatenate([zero, u_ref[at], plane, w_ref[at], zero], axis=0)
+
+    return pl.pallas_call(
+        body,
+        out_shape=jax.ShapeDtypeStruct((n, PAD_LAT, LON), F32),
+        compiler_params=pltpu.CompilerParams(vmem_limit_bytes=8 * MIB),
+        name="static_planes",
+    )(*arrays, up, down)
 
 
 def beside_lon(k, plane, left, right):
@@ -264,51 +273,23 @@
     return [ref[k].astype(F32) for ref in refs for k in range(ref.shape[0])]
 
 
-def pad_static(arrays, left, right, up, down):
-    n = TRACERS + 1
-
-    def body(*refs):
-        l_ref, r_ref, u_ref, w_ref, out_ref = refs[-5:]
-        none = [jnp.zeros((8 - HALO, 128), F32), jnp.zeros((8 - HALO, LON), F32)]
-
-        def rows(top, mid, low):
-            zero = none[mid.shape[1] // LON]
-            return jnp.concatenate([zero, top, mid, low, zero], axis=0)
-
-        def end(ref, side):
-            return ref[n * HALO : (n + 1) * HALO, side * 128 : side * 128 + 128]
-
-        left_ = rows(end(u_ref, 0), l_ref[...], end(w_ref, 0))
-        right_ = rows(end(u_ref, 1), r_ref[...], end(w_ref, 1))
-        for k, plane in enumerate(planes_of(refs[:-5])):
-            at = pl.ds(k * HALO, HALO)
-            out_ref[k] = beside_lon(k, rows(u_ref[at], plane, w_ref[at]), left_, right_)
-
-    return pl.pallas_call(
-        body,
-        out_shape=jax.ShapeDtypeStruct((n, PAD_LAT, PAD_LON), F32),
-        compiler_params=pltpu.CompilerParams(vmem_limit_bytes=8 * MIB),
-        name="pad_static",
-    )(*arrays, left, right, up, down)
-
-
-def diffuse(arrays, left, right, static, taps):
+def diffuse(arrays, left, right, taps):
     n = TS_DEV + 2 * HB
 
     def body(taps_ref, *refs):
-        l_ref, r_ref, st_ref, out_ref, pad_ref = refs[-5:]
+        l_ref, r_ref, out_ref, pad_ref = refs[-4:]
         c = pl.program_id(0)
 
         @pl.when(c == 0)
         def _():
-            for k, plane in enumerate(planes_of(refs[:-5])):
+            for k, plane in enumerate(planes_of(refs[:-4])):
                 pad_ref[k] = beside_lon(k, plane, l_ref[...], r_ref[...])
 
         banded = taps_ref[c, 0] * pad_ref[0:TS_DEV]
         for k in range(1, 2 * HB + 1):
             banded = banded + taps_ref[c, k] * pad_ref[k : k + TS_DEV]
-        field = st_ref[c][None] * banded
-        rate = st_ref[TRACERS][None]
+        field = pad_ref[n + c][None] * banded
+        rate = pad_ref[n + TRACERS][None]
         for _ in range(KSTEPS):
             beside = (
                 pltpu.roll(field, 1, 2)
@@ -317,20 +298,20 @@
                 + pltpu.roll(field, PAD_LAT - 1, 1)
             )
             field = field + rate * (beside - 4.0 * field)
-        scale = st_ref[c, 8 : 8 + LAT, :LON]
+        scale = pad_ref[n + c, 8 : 8 + LAT, :LON]
         out_ref[0] = scale[None] * field[:, 8 : 8 + LAT, :LON]
 
     def whole(a):
         return pl.BlockSpec(a.shape, lambda c: (0,) * a.ndim)
 
-    operands = (*arrays, left, right, static)
+    operands = (*arrays, left, right)
     return pl.pallas_call(
         body,
         grid=(TRACERS,),
         in_specs=[pl.BlockSpec(memory_space=pltpu.SMEM)] + [whole(a) for a in operands],
         out_specs=pl.BlockSpec((1, TS_DEV, LAT, LON), lambda c: (c, 0, 0, 0)),
         out_shape=jax.ShapeDtypeStruct((TRACERS, TS_DEV, LAT, LON), F32),
-        scratch_shapes=[pltpu.VMEM((n, PAD_LAT, PAD_LON), F32)],
+        scratch_shapes=[pltpu.VMEM((n + TRACERS + 1, PAD_LAT, PAD_LON), F32)],
         compiler_params=pltpu.CompilerParams(vmem_limit_bytes=20 * MIB),
         name="diffuse",
     )(taps, *operands)
@@ -366,25 +347,24 @@
 
     fixed = (sigma, diffusivity[None])
     fixed, first_gy = lax.optimization_barrier((fixed, first_gy))
-    to_left, to_right = pack_lon(fixed, F32, "static_lon")
-    left = lax.ppermute(to_right, "gx", east)
-    right = lax.ppermute(to_left, "gx", west)
-    to_up, to_down = pack_lat(fixed, left, right, F32, "static_lat")
+    to_up, to_down = pack_rows(fixed)
     up = lax.ppermute(to_down, "gy", south)
     down = lax.ppermute(to_up, "gy", north)
-    static = pad_static(fixed, left, right, up, down)
-    static, came_gy = lax.optimization_barrier((static, came_gy))
-
-    all_gx = along_gy(sum_first(got_gx))
+    static = beside_lat(fixed, up, down)
+
+    parts = sum_first(got_gx)
+    all_gx = along_gy(parts)
+    came_gy, all_gx[0] = lax.optimization_barrier((came_gy, all_gx[0]))
     all_gy = along_gx(sum_arrays(came_gy))
+    all_gx, static = lax.optimization_barrier((all_gx, static))
     adj, low, high = tile_sum(all_gx, all_gy)
     before = lax.ppermute(high, "ta", later)
     after = lax.ppermute(low, "ta", sooner)
-    arrays = (before, adj, after)
-    to_left, to_right = pack_lon(arrays, F32, "adjoint_lon")
+    arrays = (before, adj, after, static)
+    to_left, to_right = pack_lon(arrays, F32, "halo_lon")
     left = lax.ppermute(to_right, "gx", east)
     right = lax.ppermute(to_left, "gx", west)
-    return diffuse(arrays, left, right, static, taps)
+    return diffuse(arrays, left, right, taps)
 
 
 def solution(mesh):

time: 98.7 us -> 98.1 us (level); the launches traced: 98.4 us -> 96.7 us
  starting transfers between devices: 40.4 us -> 38.4 us
  waiting for transfers between devices: 34.4 us -> 33.4 us
    ppermute x2 -> x1, waiting for transfers between devices: 20.3 us -> 1.3 us  [per_device(): left = lax.ppermute(to_right, 'gx', east)]
    all_to_all x2, waiting for transfers between devices: 4.56 us -> 22.1 us  [along_gx(): return lax.all_to_all(rows, 'gx', 0, 0, tiled=True)]
    ppermute x2 -> x1, starting transfers between devices: 5.76 us -> 2.2 us  [per_device(): right = lax.ppermute(to_left, 'gx', west)]
    ppermute x6, waiting for transfers between devices: 0.02 us -> 2.64 us  [along_gy(): lax.ppermute(parts[k], 'gy', [(i, (i + k) % N_GY) for i in range(N_GY)])]
    ppermute x1, starting transfers between devices: 9.86 us -> 7.94 us  [per_device(): before = lax.ppermute(high, 'ta', later)]
    ppermute x6, starting transfers between devices: 6.84 us -> 8.38 us  [along_gy(): lax.ppermute(parts[k], 'gy', [(i, (i + k) % N_GY) for i in range(N_GY)])]
    all_to_all x2, starting transfers between devices: 9.23 us -> 10.7 us  [along_gx(): return lax.all_to_all(rows, 'gx', 0, 0, tiled=True)]
    pallas_call x1, Pallas kernels: 1.13 us -> 2.42 us  [sum_arrays(): pl.pallas_call(body, out_shape=jax.ShapeDtypeStruct((N_GX, ROWS, cols), B...]
  transfers between devices with their start and end apart: 16 -> 14, of which waited for: 5 -> 5; matrix products, arithmetic and copies ran while one was open for 0% -> 0% of each run, Pallas kernels for 2% -> 0%
where the time goes in v6:
time: 98.1 us; the launch traced here: 96.7 us
  starting transfers between devices  38.4 us (39%)
  waiting for transfers between devices  33.4 us (34%)
  Pallas kernels  24.1 us (25%)
    all_to_all x2, waiting for transfers between devices, along_gx(): return lax.all_to_all(rows, 'gx', 0, 0, tiled=True)  22.1 us
    pallas_call x1, Pallas kernels, bin_sums(): pl.pallas_call(body, grid=(2,), in_specs=[one] * 4 + [pl.BlockSpec((SND,...  14 us
    all_to_all x2, starting transfers between devices, along_gx(): return lax.all_to_all(rows, 'gx', 0, 0, tiled=True)  10.7 us
    ppermute x6, starting transfers between devices, along_gy(): lax.ppermute(parts[k], 'gy', [(i, (i + k) % N_GY) for i in range(N_GY)])  8.38 us
    ppermute x1, starting transfers between devices, per_device(): before = lax.ppermute(high, 'ta', later)  7.94 us
    pallas_call x1, Pallas kernels, diffuse(): pl.pallas_call(body, grid=(TRACERS,), in_specs=[pl.BlockSpec(memory_space...  6.84 us
    ppermute x1, waiting for transfers between devices, per_device(): after = lax.ppermute(low, 'ta', sooner)  5.93 us
    ppermute x1, starting transfers between devices, per_device(): down = lax.ppermute(to_up, 'gy', north)  3.36 us
  transfers between devices with their start and end apart: 14, of which 5 were waited for; matrix products, arithmetic and copies ran while one was open for 0% of the time, Pallas kernels for 0%

profile of v6, /device:TPU:67, one launch (start us, length us, event | category | flops | bytes accessed | tf_op | source)
XLA Modules:
  0.0 96.7 jit_solution(3799529239243545569)
XLA Ops:
  0.0 14.0 %bin_sums.1 = (bf16[2048,512]{1,0:T(8,128)(2,1)}, bf16[576,512]{1,0:T(8,128)(2,1)}, bf16[576,512]{1,0:T(8,128)(2,1)}, bf16[576,512]{1,0:T(8,128)(2,1)}, bf16[576,512]{1,0:T(8,128)(2,1)}) custom-call(s32[2048]{0:T(1024)} %bitcast.6, s32[2048]{0:T(1024)} %step_ref.1, s32[2048]{0:T(1024)} %block_ref.1, bf16[2048]{0:T(1024)(128)(2,1)} %res_ref.1, ...), custom_call_target="tpu_custom_call" | custom-call | flops 8589934592 | bytes 8388608 | tf_op jit(solution)/shard_map/bin_sums/pallas_call | solution.py:80
  14.0 5.5 %all-to-all-start = ((bf16[8,256,512]{2,1,0:T(8,128)(2,1)}), bf16[8,256,512]{2,1,0:T(8,128)(2,1)S(1)}, u32[]{:S(2)}, u32[]{:S(2)}) async-start(bf16[8,256,512]{2,1,0:T(8,128)(2,1)} %bitcast.5), calls=%async_computation | async-start | bytes 4194304 | tf_op jit(solution)/shard_map/all_to_all | solution.py:336
  19.5 1.3 %collective-permute-start = (bf16[576,512]{1,0:T(8,128)(2,1)}, bf16[576,512]{1,0:T(8,128)(2,1)S(1)}, u32[]{:S(2)}, u32[]{:S(2)}) collective-permute-start(bf16[576,512]{1,0:T(8,128)(2,1)} %get-tuple-element.34), channel_id=1, source_target_pairs={{0,8},{8,16},{16,24},{24,0},{1,9},{9,17},{17,25},{25,1},{2,10},{10... | collective-permute-start | bytes 1769480 | tf_op jit(solution)/shard_map/ppermute | solution.py:330
  20.8 0.8 collective-permute-start.1
  21.6 1.9 %collective-permute-start.2 = (bf16[576,512]{1,0:T(8,128)(2,1)}, bf16[576,512]{1,0:T(8,128)(2,1)}, u32[]{:S(2)}, u32[]{:S(2)}) collective-permute-start(bf16[576,512]{1,0:T(8,128)(2,1)} %get-tuple-element.36), channel_id=1, source_target_pairs={{0,24},{8,0},{16,8},{24,16},{1,25},{9,1},{17,9},{25,17},{2,26},{10... | collective-permute-start | bytes 1769480 | tf_op jit(solution)/shard_map/ppermute | solution.py:330
  23.5 22.1 %all-to-all-done.got_ref = bf16[8,256,512]{2,1,0:T(8,128)(2,1)S(1)} async-done(((bf16[8,256,512]{2,1,0:T(8,128)(2,1)}), bf16[8,256,512]{2,1,0:T(8,128)(2,1)S(1)}, u32[]{:S(2)}, u32[]{:S(2)}) %all-to-all-start) | async-done | bytes 2097184 | tf_op jit(solution)/shard_map/all_to_all | solution.py:336
  45.6 0.3 sum_first.1
  45.8 0.6 copy-done.4
  46.5 0.0 collective-permute-done.1.refs_2_
  46.5 2.6 %collective-permute-done.2.refs_3_ = bf16[576,512]{1,0:T(8,128)(2,1)} collective-permute-done((bf16[576,512]{1,0:T(8,128)(2,1)}, bf16[576,512]{1,0:T(8,128)(2,1)}, u32[]{:S(2)}, u32[]{:S(2)}) %collective-permute-start.2) | collective-permute-done | bytes 589856 | tf_op jit(solution)/shard_map/ppermute | solution.py:330
  49.1 2.4 %sum_arrays.1 = bf16[8,80,512]{2,1,0:T(8,128)(2,1)} custom-call(bf16[576,512]{1,0:T(8,128)(2,1)S(1)} %copy-done.1, bf16[576,512]{1,0:T(8,128)(2,1)S(1)} %collective-permute-done.refs_1_, bf16[576,512]{1,0:T(8,128)(2,1)} %collective-permute-done.1.refs_2_, bf16[576,512]{1,0:T(8,128)(2,1)} %collective-permute-done.2.refs_3_), custom_call_target="tpu_custom_call" | custom-call | tf_op jit(solution)/shard_map/sum_arrays/pallas_call | solution.py:139
  51.5 5.2 %all-to-all-start.1 = ((bf16[8,80,512]{2,1,0:T(8,128)(2,1)}), bf16[8,80,512]{2,1,0:T(8,128)(2,1)S(1)}, u32[]{:S(2)}, u32[]{:S(2)}) async-start(bf16[8,80,512]{2,1,0:T(8,128)(2,1)} %sum_arrays.1), calls=%async_computation.1 | async-start | bytes 1310720 | tf_op jit(solution)/shard_map/all_to_all | solution.py:336
  56.7 0.1 collective-permute-start.3
  56.8 2.3 %collective-permute-start.4 = (bf16[80,512]{1,0:T(8,128)(2,1)S(1)}, bf16[80,512]{1,0:T(8,128)(2,1)S(1)}, u32[]{:S(2)}, u32[]{:S(2)}) collective-permute-start(bf16[80,512]{1,0:T(8,128)(2,1)S(1)} %get-tuple-element.41), channel_id=1, source_target_pairs={{0,16},{8,24},{16,0},{24,8},{1,17},{9,25},{17,1},{25,9},{2,18},{10... | collective-permute-start | bytes 245768 | tf_op jit(solution)/shard_map/ppermute | solution.py:330
  59.2 2.0 %collective-permute-start.5 = (bf16[80,512]{1,0:T(8,128)(2,1)S(1)}, bf16[80,512]{1,0:T(8,128)(2,1)S(1)}, u32[]{:S(2)}, u32[]{:S(2)}) collective-permute-start(bf16[80,512]{1,0:T(8,128)(2,1)S(1)} %get-tuple-element.42), channel_id=1, source_target_pairs={{0,24},{8,0},{16,8},{24,16},{1,25},{9,1},{17,9},{25,17},{2,26},{10... | collective-permute-start | bytes 245768 | tf_op jit(solution)/shard_map/ppermute | solution.py:330
  61.1 1.9 %collective-permute-start.6 = (f32[20,256]{1,0:T(8,128)S(1)}, f32[20,256]{1,0:T(8,128)S(1)}, u32[]{:S(2)}, u32[]{:S(2)}) collective-permute-start(f32[20,256]{1,0:T(8,128)S(1)} %get-tuple-element.45), channel_id=1, source_target_pairs={{0,8},{8,16},{16,24},{1,9},{9,17},{17,25},{2,10},{10,18},{18,26},{... | collective-permute-start | bytes 61448 | tf_op jit(solution)/shard_map/ppermute | solution.py:351
  63.1 3.4 %collective-permute-start.7 = (f32[20,256]{1,0:T(8,128)S(1)}, f32[20,256]{1,0:T(8,128)S(1)}, u32[]{:S(2)}, u32[]{:S(2)}) collective-permute-start(f32[20,256]{1,0:T(8,128)S(1)} %get-tuple-element.46), channel_id=1, source_target_pairs={{8,0},{16,8},{24,16},{9,1},{17,9},{25,17},{10,2},{18,10},{26,18},{... | collective-permute-start | bytes 61448 | tf_op jit(solution)/shard_map/ppermute | solution.py:352
  66.4 0.0 collective-permute-done.6.refs_2_
  66.5 1.5 %collective-permute-done.7.refs_3_ = f32[20,256]{1,0:T(8,128)S(1)} collective-permute-done((f32[20,256]{1,0:T(8,128)S(1)}, f32[20,256]{1,0:T(8,128)S(1)}, u32[]{:S(2)}, u32[]{:S(2)}) %collective-permute-start.7) | collective-permute-done | bytes 20512 | tf_op jit(solution)/shard_map/ppermute | solution.py:352
  68.0 0.0 collective-permute-done.5.refs_3_
  68.0 0.0 all-to-all-done.1.refs_4_
  68.0 0.3 tile_sum.1
  68.3 7.9 %collective-permute-start.8 = (bf16[2,80,256]{2,1,0:T(8,128)(2,1)S(1)}, bf16[2,80,256]{2,1,0:T(8,128)(2,1)S(1)}, u32[]{:S(2)}, u32[]{:S(2)}) collective-permute-start(bf16[2,80,256]{2,1,0:T(8,128)(2,1)S(1)} %get-tuple-element.55), channel_id=1, source_target_pairs={{0,32},{32,64},{64,96},{96,128},{128,160},{160,192},{192,224},{1,3... | collective-permute-start | bytes 245768 | tf_op jit(solution)/shard_map/ppermute | solution.py:361
  76.2 1.9 %collective-permute-start.9 = (bf16[2,80,256]{2,1,0:T(8,128)(2,1)S(1)}, bf16[2,80,256]{2,1,0:T(8,128)(2,1)S(1)}, u32[]{:S(2)}, u32[]{:S(2)}) collective-permute-start(bf16[2,80,256]{2,1,0:T(8,128)(2,1)S(1)} %get-tuple-element.57), channel_id=1, source_target_pairs={{32,0},{64,32},{96,64},{128,96},{160,128},{192,160},{224,192},{33,... | collective-permute-start | bytes 245768 | tf_op jit(solution)/shard_map/ppermute | solution.py:362
  78.2 0.0 collective-permute-done.8.refs_0_
  78.2 5.9 %collective-permute-done.9.refs_2_ = bf16[2,80,256]{2,1,0:T(8,128)(2,1)S(1)} collective-permute-done((bf16[2,80,256]{2,1,0:T(8,128)(2,1)S(1)}, bf16[2,80,256]{2,1,0:T(8,128)(2,1)S(1)}, u32[]{:S(2)}, u32[]{:S(2)}) %collective-permute-start.9) | collective-permute-done | bytes 81952 | tf_op jit(solution)/shard_map/ppermute | solution.py:362
  84.1 0.3 halo_lon.1
  84.4 1.9 %collective-permute-start.10 = (f32[80,128]{1,0:T(8,128)S(1)}, f32[80,128]{1,0:T(8,128)S(1)}, u32[]{:S(2)}, u32[]{:S(2)}) collective-permute-start(f32[80,128]{1,0:T(8,128)S(1)} %get-tuple-element.59), channel_id=1, source_target_pairs={{0,1},{1,2},{2,3},{3,4},{4,5},{5,6},{6,7},{7,0},{8,9},{9,10},{10,1... | collective-permute-start | bytes 122888 | tf_op jit(solution)/shard_map/ppermute | solution.py:365
  86.3 2.2 %collective-permute-start.11 = (f32[80,128]{1,0:T(8,128)S(1)}, f32[80,128]{1,0:T(8,128)S(1)}, u32[]{:S(2)}, u32[]{:S(2)}) collective-permute-start(f32[80,128]{1,0:T(8,128)S(1)} %get-tuple-element.60), channel_id=1, source_target_pairs={{1,0},{2,1},{3,2},{4,3},{5,4},{6,5},{7,6},{0,7},{9,8},{10,9},{11,1... | collective-permute-start | bytes 122888 | tf_op jit(solution)/shard_map/ppermute | solution.py:366
  88.5 1.3 %collective-permute-done.10.refs_4_ = f32[80,128]{1,0:T(8,128)S(1)} collective-permute-done((f32[80,128]{1,0:T(8,128)S(1)}, f32[80,128]{1,0:T(8,128)S(1)}, u32[]{:S(2)}, u32[]{:S(2)}) %collective-permute-start.10) | collective-permute-done | bytes 40992 | tf_op jit(solution)/shard_map/ppermute | solution.py:365
  89.8 0.0 collective-permute-done.11.refs_5_
  89.8 6.8 %diffuse.1 = f32[4,4,64,256]{3,2,1,0:T(8,128)} custom-call(f32[4,5]{1,0:T(4,128)S(1)} %copy-done.3, bf16[2,80,256]{2,1,0:T(8,128)(2,1)S(1)} %collective-permute-done.8.refs_0_, f32[4,80,256]{2,1,0:T(8,128)S(1)} %get-tuple-element.56.refs_1_, bf16[2,80,256]{2,1,0:T(8,128)(2,1)S(1)} %collective-permute-done.9.refs_2_, f32[5,80,256]{2,1,0:T(8,128)S(1)} %static_planes.1.refs_3_, ...), custom_call_target="tpu_custom_call" | custom-call | tf_op jit(solution)/shard_map/diffuse/pallas_call | solution.py:308
  (16 shorter events, 0.1 us)
Async XLA Ops:
  14.0 31.6 %all-to-all-start = ((bf16[8,256,512]{2,1,0:T(8,128)(2,1)}), bf16[8,256,512]{2,1,0:T(8,128)(2,1)S(1)}, u32[]{:S(2)}, u32[]{:S(2)}) async-start(bf16[8,256,512]{2,1,0:T(8,128)(2,1)} %bitcast.5), calls=%async_computation | async-start | bytes 4194304 | tf_op jit(solution)/shard_map/all_to_all | solution.py:336
  19.5 29.6 %copy-start.1 = (bf16[576,512]{1,0:T(8,128)(2,1)S(1)}, bf16[576,512]{1,0:T(8,128)(2,1)}, u32[]{:S(2)}) copy-start(bf16[576,512]{1,0:T(8,128)(2,1)} %get-tuple-element.51.refs_0_) | copy-start | bytes 1769476
  19.5 27.0 %collective-permute-start = (bf16[576,512]{1,0:T(8,128)(2,1)}, bf16[576,512]{1,0:T(8,128)(2,1)S(1)}, u32[]{:S(2)}, u32[]{:S(2)}) collective-permute-start(bf16[576,512]{1,0:T(8,128)(2,1)} %get-tuple-element.34), channel_id=1, source_target_pairs={{0,8},{8,16},{16,24},{24,0},{1,9},{9,17},{17,25},{25,1},{2,10},{10... | collective-permute-start | bytes 1769480 | tf_op jit(solution)/shard_map/ppermute | solution.py:330
  20.8 25.7 %collective-permute-start.1 = (bf16[576,512]{1,0:T(8,128)(2,1)}, bf16[576,512]{1,0:T(8,128)(2,1)}, u32[]{:S(2)}, u32[]{:S(2)}) collective-permute-start(bf16[576,512]{1,0:T(8,128)(2,1)} %get-tuple-element.35), channel_id=1, source_target_pairs={{0,16},{8,24},{16,0},{24,8},{1,17},{9,25},{17,1},{25,9},{2,18},{10... | collective-permute-start | bytes 1769480 | tf_op jit(solution)/shard_map/ppermute | solution.py:330
  21.6 27.5 %collective-permute-start.2 = (bf16[576,512]{1,0:T(8,128)(2,1)}, bf16[576,512]{1,0:T(8,128)(2,1)}, u32[]{:S(2)}, u32[]{:S(2)}) collective-permute-start(bf16[576,512]{1,0:T(8,128)(2,1)} %get-tuple-element.36), channel_id=1, source_target_pairs={{0,24},{8,0},{16,8},{24,16},{1,25},{9,1},{17,9},{25,17},{2,26},{10... | collective-permute-start | bytes 1769480 | tf_op jit(solution)/shard_map/ppermute | solution.py:330
  45.8 0.6 copy-start.4
  49.1 7.6 %copy-start.5 = (bf16[80,512]{1,0:T(8,128)(2,1)S(1)}, bf16[80,512]{1,0:T(8,128)(2,1)}, u32[]{:S(2)}) copy-start(bf16[80,512]{1,0:T(8,128)(2,1)} %copy-done.4) | copy-start | bytes 245764
  49.1 12.0 %copy-start = (f32[4,64,256]{2,1,0:T(8,128)S(1)}, f32[4,64,256]{2,1,0:T(8,128)}, u32[]{:S(2)}) copy-start(f32[4,64,256]{2,1,0:T(8,128)} %refs_0_.1) | copy-start | bytes 786436
  49.1 12.0 %copy-start.2 = (f32[64,256]{1,0:T(8,128)S(1)}, f32[64,256]{1,0:T(8,128)}, u32[]{:S(2)}) copy-start(f32[64,256]{1,0:T(8,128)} %param.15) | copy-start | bytes 196612
  51.5 38.3 %copy-start.3 = (f32[4,5]{1,0:T(4,128)S(1)}, f32[4,5]{1,0:T(4,128)}, u32[]{:S(2)}) copy-start(f32[4,5]{1,0:T(4,128)} %taps_ref.1) | copy-start | bytes 244
  51.5 16.5 %all-to-all-start.1 = ((bf16[8,80,512]{2,1,0:T(8,128)(2,1)}), bf16[8,80,512]{2,1,0:T(8,128)(2,1)S(1)}, u32[]{:S(2)}, u32[]{:S(2)}) async-start(bf16[8,80,512]{2,1,0:T(8,128)(2,1)} %sum_arrays.1), calls=%async_computation.1 | async-start | bytes 1310720 | tf_op jit(solution)/shard_map/all_to_all | solution.py:336
  56.7 11.2 %collective-permute-start.3 = (bf16[80,512]{1,0:T(8,128)(2,1)S(1)}, bf16[80,512]{1,0:T(8,128)(2,1)S(1)}, u32[]{:S(2)}, u32[]{:S(2)}) collective-permute-start(bf16[80,512]{1,0:T(8,128)(2,1)S(1)} %copy-done.5), channel_id=1, source_target_pairs={{0,8},{8,16},{16,24},{24,0},{1,9},{9,17},{17,25},{25,1},{2,10},{10... | collective-permute-start | bytes 245768 | tf_op jit(solution)/shard_map/ppermute | solution.py:330
  56.8 11.2 %collective-permute-start.4 = (bf16[80,512]{1,0:T(8,128)(2,1)S(1)}, bf16[80,512]{1,0:T(8,128)(2,1)S(1)}, u32[]{:S(2)}, u32[]{:S(2)}) collective-permute-start(bf16[80,512]{1,0:T(8,128)(2,1)S(1)} %get-tuple-element.41), channel_id=1, source_target_pairs={{0,16},{8,24},{16,0},{24,8},{1,17},{9,25},{17,1},{25,9},{2,18},{10... | collective-permute-start | bytes 245768 | tf_op jit(solution)/shard_map/ppermute | solution.py:330
  59.2 8.8 %collective-permute-start.5 = (bf16[80,512]{1,0:T(8,128)(2,1)S(1)}, bf16[80,512]{1,0:T(8,128)(2,1)S(1)}, u32[]{:S(2)}, u32[]{:S(2)}) collective-permute-start(bf16[80,512]{1,0:T(8,128)(2,1)S(1)} %get-tuple-element.42), channel_id=1, source_target_pairs={{0,24},{8,0},{16,8},{24,16},{1,25},{9,1},{17,9},{25,17},{2,26},{10... | collective-permute-start | bytes 245768 | tf_op jit(solution)/shard_map/ppermute | solution.py:330
  61.1 5.3 %collective-permute-start.6 = (f32[20,256]{1,0:T(8,128)S(1)}, f32[20,256]{1,0:T(8,128)S(1)}, u32[]{:S(2)}, u32[]{:S(2)}) collective-permute-start(f32[20,256]{1,0:T(8,128)S(1)} %get-tuple-element.45), channel_id=1, source_target_pairs={{0,8},{8,16},{16,24},{1,9},{9,17},{17,25},{2,10},{10,18},{18,26},{... | collective-permute-start | bytes 61448 | tf_op jit(solution)/shard_map/ppermute | solution.py:351
  63.1 4.9 %collective-permute-start.7 = (f32[20,256]{1,0:T(8,128)S(1)}, f32[20,256]{1,0:T(8,128)S(1)}, u32[]{:S(2)}, u32[]{:S(2)}) collective-permute-start(f32[20,256]{1,0:T(8,128)S(1)} %get-tuple-element.46), channel_id=1, source_target_pairs={{8,0},{16,8},{24,16},{9,1},{17,9},{25,17},{10,2},{18,10},{26,18},{... | collective-permute-start | bytes 61448 | tf_op jit(solution)/shard_map/ppermute | solution.py:352
  68.3 9.9 %collective-permute-start.8 = (bf16[2,80,256]{2,1,0:T(8,128)(2,1)S(1)}, bf16[2,80,256]{2,1,0:T(8,128)(2,1)S(1)}, u32[]{:S(2)}, u32[]{:S(2)}) collective-permute-start(bf16[2,80,256]{2,1,0:T(8,128)(2,1)S(1)} %get-tuple-element.55), channel_id=1, source_target_pairs={{0,32},{32,64},{64,96},{96,128},{128,160},{160,192},{192,224},{1,3... | collective-permute-start | bytes 245768 | tf_op jit(solution)/shard_map/ppermute | solution.py:361
  76.2 7.9 %collective-permute-start.9 = (bf16[2,80,256]{2,1,0:T(8,128)(2,1)S(1)}, bf16[2,80,256]{2,1,0:T(8,128)(2,1)S(1)}, u32[]{:S(2)}, u32[]{:S(2)}) collective-permute-start(bf16[2,80,256]{2,1,0:T(8,128)(2,1)S(1)} %get-tuple-element.57), channel_id=1, source_target_pairs={{32,0},{64,32},{96,64},{128,96},{160,128},{192,160},{224,192},{33,... | collective-permute-start | bytes 245768 | tf_op jit(solution)/shard_map/ppermute | solution.py:362
  84.4 5.4 %collective-permute-start.10 = (f32[80,128]{1,0:T(8,128)S(1)}, f32[80,128]{1,0:T(8,128)S(1)}, u32[]{:S(2)}, u32[]{:S(2)}) collective-permute-start(f32[80,128]{1,0:T(8,128)S(1)} %get-tuple-element.59), channel_id=1, source_target_pairs={{0,1},{1,2},{2,3},{3,4},{4,5},{5,6},{6,7},{7,0},{8,9},{9,10},{10,1... | collective-permute-start | bytes 122888 | tf_op jit(solution)/shard_map/ppermute | solution.py:365
  86.3 3.5 %collective-permute-start.11 = (f32[80,128]{1,0:T(8,128)S(1)}, f32[80,128]{1,0:T(8,128)S(1)}, u32[]{:S(2)}, u32[]{:S(2)}) collective-permute-start(f32[80,128]{1,0:T(8,128)S(1)} %get-tuple-element.60), channel_id=1, source_target_pairs={{1,0},{2,1},{3,2},{4,3},{5,4},{6,5},{7,6},{0,7},{9,8},{10,9},{11,1... | collective-permute-start | bytes 122888 | tf_op jit(solution)/shard_map/ppermute | solution.py:366

commit v7 on v6

--- a/solution.py
+++ b/solution.py
@@ -350,13 +350,11 @@
     to_up, to_down = pack_rows(fixed)
     up = lax.ppermute(to_down, "gy", south)
     down = lax.ppermute(to_up, "gy", north)
+    came_gy, up, down = lax.optimization_barrier((came_gy, up, down))
     static = beside_lat(fixed, up, down)
 
-    parts = sum_first(got_gx)
-    all_gx = along_gy(parts)
-    came_gy, all_gx[0] = lax.optimization_barrier((came_gy, all_gx[0]))
+    all_gx = along_gy(sum_first(got_gx))
     all_gy = along_gx(sum_arrays(came_gy))
-    all_gx, static = lax.optimization_barrier((all_gx, static))
     adj, low, high = tile_sum(all_gx, all_gy)
     before = lax.ppermute(high, "ta", later)
     after = lax.ppermute(low, "ta", sooner)

time: 98.1 us -> 95.2 us (0.970); the launches traced: 96.7 us -> 94.8 us
  waiting for transfers between devices: 33.4 us -> 34.8 us
  Pallas kernels: 24.1 us -> 22.8 us
  starting transfers between devices: 38.4 us -> 37.2 us
    ppermute x1, waiting for transfers between devices: 0.01 us -> 18.1 us  [per_device(): up = lax.ppermute(to_down, 'gy', south)]
    all_to_all x2, waiting for transfers between devices: 22.1 us -> 5.88 us  [along_gx(): return lax.all_to_all(rows, 'gx', 0, 0, tiled=True)]
    ppermute x6, waiting for transfers between devices: 2.64 us -> 0.02 us  [along_gy(): lax.ppermute(parts[k], 'gy', [(i, (i + k) % N_GY) for i in range(N_GY)])]
    ppermute x1, starting transfers between devices: 1.92 us -> 0.44 us  [per_device(): left = lax.ppermute(to_right, 'gx', east)]
    pallas_call x1, Pallas kernels: 2.42 us -> 1.13 us  [sum_arrays(): pl.pallas_call(body, out_shape=jax.ShapeDtypeStruct((N_GX, ROWS, cols), B...]
    ppermute x1, starting transfers between devices: 2.2 us -> 3.39 us  [per_device(): right = lax.ppermute(to_left, 'gx', west)]
    ppermute x1, waiting for transfers between devices: 1.49 us -> 2.64 us  [per_device(): down = lax.ppermute(to_up, 'gy', north)]
  transfers between devices with their start and end apart: 14 -> 14, of which waited for: 5 -> 5; matrix products, arithmetic and copies ran while one was open for 0% -> 0% of each run, Pallas kernels for 0% -> 2%
where the time goes in v7:
time: 95.2 us; the launch traced here: 94.8 us
  starting transfers between devices  37.2 us (39%)
  waiting for transfers between devices  34.8 us (37%)
  Pallas kernels  22.8 us (24%)
    ppermute x1, waiting for transfers between devices, per_device(): up = lax.ppermute(to_down, 'gy', south)  18.1 us
    pallas_call x1, Pallas kernels, bin_sums(): pl.pallas_call(body, grid=(2,), in_specs=[one] * 4 + [pl.BlockSpec((SND,...  14 us
    all_to_all x2, starting transfers between devices, along_gx(): return lax.all_to_all(rows, 'gx', 0, 0, tiled=True)  10.8 us
    ppermute x6, starting transfers between devices, along_gy(): lax.ppermute(parts[k], 'gy', [(i, (i + k) % N_GY) for i in range(N_GY)])  7.76 us
    ppermute x1, starting transfers between devices, per_device(): before = lax.ppermute(high, 'ta', later)  7.53 us
    pallas_call x1, Pallas kernels, diffuse(): pl.pallas_call(body, grid=(TRACERS,), in_specs=[pl.BlockSpec(memory_space...  6.84 us
    ppermute x1, waiting for transfers between devices, per_device(): after = lax.ppermute(low, 'ta', sooner)  6.77 us
    all_to_all x2, waiting for transfers between devices, along_gx(): return lax.all_to_all(rows, 'gx', 0, 0, tiled=True)  5.88 us
  transfers between devices with their start and end apart: 14, of which 5 were waited for; matrix products, arithmetic and copies ran while one was open for 0% of the time, Pallas kernels for 2%

profile of v7, /device:TPU:67, one launch (start us, length us, event | category | flops | bytes accessed | tf_op | source)
XLA Modules:
  0.0 94.8 jit_solution(13664995936260826555)
XLA Ops:
  0.0 14.0 %bin_sums.1 = (bf16[2048,512]{1,0:T(8,128)(2,1)}, bf16[576,512]{1,0:T(8,128)(2,1)}, bf16[576,512]{1,0:T(8,128)(2,1)}, bf16[576,512]{1,0:T(8,128)(2,1)}, bf16[576,512]{1,0:T(8,128)(2,1)}) custom-call(s32[2048]{0:T(1024)} %bitcast.6, s32[2048]{0:T(1024)} %step_ref.1, s32[2048]{0:T(1024)} %block_ref.1, bf16[2048]{0:T(1024)(128)(2,1)} %res_ref.1, ...), custom_call_target="tpu_custom_call" | custom-call | flops 8589934592 | bytes 8388608 | tf_op jit(solution)/shard_map/bin_sums/pallas_call | solution.py:80
  14.0 5.7 %all-to-all-start = ((bf16[8,256,512]{2,1,0:T(8,128)(2,1)}), bf16[8,256,512]{2,1,0:T(8,128)(2,1)S(1)}, u32[]{:S(2)}, u32[]{:S(2)}) async-start(bf16[8,256,512]{2,1,0:T(8,128)(2,1)} %bitcast.5), calls=%async_computation | async-start | bytes 4194304 | tf_op jit(solution)/shard_map/all_to_all | solution.py:336
  19.7 1.2 %collective-permute-start.3 = (bf16[576,512]{1,0:T(8,128)(2,1)}, bf16[576,512]{1,0:T(8,128)(2,1)S(1)}, u32[]{:S(2)}, u32[]{:S(2)}) collective-permute-start(bf16[576,512]{1,0:T(8,128)(2,1)} %get-tuple-element.35), channel_id=1, source_target_pairs={{0,8},{8,16},{16,24},{24,0},{1,9},{9,17},{17,25},{25,1},{2,10},{10... | collective-permute-start | bytes 1769480 | tf_op jit(solution)/shard_map/ppermute | solution.py:330
  20.9 0.8 collective-permute-start.4
  21.7 1.9 %collective-permute-start.5 = (bf16[576,512]{1,0:T(8,128)(2,1)}, bf16[576,512]{1,0:T(8,128)(2,1)S(1)}, u32[]{:S(2)}, u32[]{:S(2)}) collective-permute-start(bf16[576,512]{1,0:T(8,128)(2,1)} %get-tuple-element.37), channel_id=1, source_target_pairs={{0,24},{8,0},{16,8},{24,16},{1,25},{9,1},{17,9},{25,17},{2,26},{10... | collective-permute-start | bytes 1769480 | tf_op jit(solution)/shard_map/ppermute | solution.py:330
  23.6 1.9 %collective-permute-start.6 = (f32[20,256]{1,0:T(8,128)S(1)}, f32[20,256]{1,0:T(8,128)S(1)}, u32[]{:S(2)}, u32[]{:S(2)}) collective-permute-start(f32[20,256]{1,0:T(8,128)S(1)} %get-tuple-element.40), channel_id=1, source_target_pairs={{0,8},{8,16},{16,24},{1,9},{9,17},{17,25},{2,10},{10,18},{18,26},{... | collective-permute-start | bytes 61448 | tf_op jit(solution)/shard_map/ppermute | solution.py:351
  25.5 3.4 %collective-permute-start.7 = (f32[20,256]{1,0:T(8,128)S(1)}, f32[20,256]{1,0:T(8,128)S(1)}, u32[]{:S(2)}, u32[]{:S(2)}) collective-permute-start(f32[20,256]{1,0:T(8,128)S(1)} %get-tuple-element.41), channel_id=1, source_target_pairs={{8,0},{16,8},{24,16},{9,1},{17,9},{25,17},{10,2},{18,10},{26,18},{... | collective-permute-start | bytes 61448 | tf_op jit(solution)/shard_map/ppermute | solution.py:352
  28.9 18.1 %collective-permute-done.6.refs_2_ = f32[20,256]{1,0:T(8,128)S(1)} collective-permute-done((f32[20,256]{1,0:T(8,128)S(1)}, f32[20,256]{1,0:T(8,128)S(1)}, u32[]{:S(2)}, u32[]{:S(2)}) %collective-permute-start.6) | collective-permute-done | bytes 20512 | tf_op jit(solution)/shard_map/ppermute | solution.py:351
  46.9 2.6 %collective-permute-done.7.refs_3_ = f32[20,256]{1,0:T(8,128)S(1)} collective-permute-done((f32[20,256]{1,0:T(8,128)S(1)}, f32[20,256]{1,0:T(8,128)S(1)}, u32[]{:S(2)}, u32[]{:S(2)}) %collective-permute-start.7) | collective-permute-done | bytes 20512 | tf_op jit(solution)/shard_map/ppermute | solution.py:352
  49.6 0.0 collective-permute-done.3.refs_1_
  49.6 0.0 collective-permute-done.4.refs_2_
  49.6 0.0 collective-permute-done.5.refs_3_
  49.6 1.1 %sum_arrays.1 = bf16[8,80,512]{2,1,0:T(8,128)(2,1)} custom-call(bf16[576,512]{1,0:T(8,128)(2,1)S(1)} %copy-done.1, bf16[576,512]{1,0:T(8,128)(2,1)S(1)} %collective-permute-done.3.refs_1_, bf16[576,512]{1,0:T(8,128)(2,1)S(1)} %collective-permute-done.4.refs_2_, bf16[576,512]{1,0:T(8,128)(2,1)S(1)} %collective-permute-done.5.refs_3_), custom_call_target="tpu_custom_call" | custom-call | tf_op jit(solution)/shard_map/sum_arrays/pallas_call | solution.py:139
  50.7 0.0 all-to-all-done.got_ref
  50.7 5.1 %all-to-all-start.1 = ((bf16[8,80,512]{2,1,0:T(8,128)(2,1)}), bf16[8,80,512]{2,1,0:T(8,128)(2,1)S(1)}, u32[]{:S(2)}, u32[]{:S(2)}) async-start(bf16[8,80,512]{2,1,0:T(8,128)(2,1)} %sum_arrays.1), calls=%async_computation.1 | async-start | bytes 1310720 | tf_op jit(solution)/shard_map/all_to_all | solution.py:336
  55.9 0.3 sum_first.1
  56.2 0.1 collective-permute-start
  56.3 1.8 %collective-permute-start.1 = (bf16[80,512]{1,0:T(8,128)(2,1)S(1)}, bf16[80,512]{1,0:T(8,128)(2,1)S(1)}, u32[]{:S(2)}, u32[]{:S(2)}) collective-permute-start(bf16[80,512]{1,0:T(8,128)(2,1)S(1)} %get-tuple-element.32), channel_id=1, source_target_pairs={{0,16},{8,24},{16,0},{24,8},{1,17},{9,25},{17,1},{25,9},{2,18},{10... | collective-permute-start | bytes 245768 | tf_op jit(solution)/shard_map/ppermute | solution.py:330
  58.0 2.0 %collective-permute-start.2 = (bf16[80,512]{1,0:T(8,128)(2,1)S(1)}, bf16[80,512]{1,0:T(8,128)(2,1)S(1)}, u32[]{:S(2)}, u32[]{:S(2)}) collective-permute-start(bf16[80,512]{1,0:T(8,128)(2,1)S(1)} %get-tuple-element.33), channel_id=1, source_target_pairs={{0,24},{8,0},{16,8},{24,16},{1,25},{9,1},{17,9},{25,17},{2,26},{10... | collective-permute-start | bytes 245768 | tf_op jit(solution)/shard_map/ppermute | solution.py:330
  60.0 5.9 %all-to-all-done.1.refs_4_ = bf16[8,80,512]{2,1,0:T(8,128)(2,1)S(1)} async-done(((bf16[8,80,512]{2,1,0:T(8,128)(2,1)}), bf16[8,80,512]{2,1,0:T(8,128)(2,1)S(1)}, u32[]{:S(2)}, u32[]{:S(2)}) %all-to-all-start.1) | async-done | bytes 655392 | tf_op jit(solution)/shard_map/all_to_all | solution.py:336
  65.9 0.0 collective-permute-done.refs_1_
  65.9 0.3 tile_sum.1
  66.2 7.5 %collective-permute-start.8 = (bf16[2,80,256]{2,1,0:T(8,128)(2,1)S(1)}, bf16[2,80,256]{2,1,0:T(8,128)(2,1)S(1)}, u32[]{:S(2)}, u32[]{:S(2)}) collective-permute-start(bf16[2,80,256]{2,1,0:T(8,128)(2,1)S(1)} %get-tuple-element.46), channel_id=1, source_target_pairs={{0,32},{32,64},{64,96},{96,128},{128,160},{160,192},{192,224},{1,3... | collective-permute-start | bytes 245768 | tf_op jit(solution)/shard_map/ppermute | solution.py:359
  73.7 1.9 %collective-permute-start.9 = (bf16[2,80,256]{2,1,0:T(8,128)(2,1)S(1)}, bf16[2,80,256]{2,1,0:T(8,128)(2,1)S(1)}, u32[]{:S(2)}, u32[]{:S(2)}) collective-permute-start(bf16[2,80,256]{2,1,0:T(8,128)(2,1)S(1)} %get-tuple-element.48), channel_id=1, source_target_pairs={{32,0},{64,32},{96,64},{128,96},{160,128},{192,160},{224,192},{33,... | collective-permute-start | bytes 245768 | tf_op jit(solution)/shard_map/ppermute | solution.py:360
  75.7 0.0 collective-permute-done.8.refs_0_
  75.7 6.8 %collective-permute-done.9.refs_2_ = bf16[2,80,256]{2,1,0:T(8,128)(2,1)S(1)} collective-permute-done((bf16[2,80,256]{2,1,0:T(8,128)(2,1)S(1)}, bf16[2,80,256]{2,1,0:T(8,128)(2,1)S(1)}, u32[]{:S(2)}, u32[]{:S(2)}) %collective-permute-start.9) | collective-permute-done | bytes 81952 | tf_op jit(solution)/shard_map/ppermute | solution.py:360
  82.5 0.3 halo_lon.1
  82.8 0.4 collective-permute-start.10
  83.2 3.4 %collective-permute-start.11 = (f32[80,128]{1,0:T(8,128)S(1)}, f32[80,128]{1,0:T(8,128)S(1)}, u32[]{:S(2)}, u32[]{:S(2)}) collective-permute-start(f32[80,128]{1,0:T(8,128)S(1)} %get-tuple-element.52), channel_id=1, source_target_pairs={{1,0},{2,1},{3,2},{4,3},{5,4},{6,5},{7,6},{0,7},{9,8},{10,9},{11,1... | collective-permute-start | bytes 122888 | tf_op jit(solution)/shard_map/ppermute | solution.py:364
  86.6 1.4 %collective-permute-done.10.refs_4_ = f32[80,128]{1,0:T(8,128)S(1)} collective-permute-done((f32[80,128]{1,0:T(8,128)S(1)}, f32[80,128]{1,0:T(8,128)S(1)}, u32[]{:S(2)}, u32[]{:S(2)}) %collective-permute-start.10) | collective-permute-done | bytes 40992 | tf_op jit(solution)/shard_map/ppermute | solution.py:363
  88.0 0.0 collective-permute-done.11.refs_5_
  88.0 6.8 %diffuse.1 = f32[4,4,64,256]{3,2,1,0:T(8,128)} custom-call(f32[4,5]{1,0:T(4,128)S(1)} %copy-done.3, bf16[2,80,256]{2,1,0:T(8,128)(2,1)S(1)} %collective-permute-done.8.refs_0_, f32[4,80,256]{2,1,0:T(8,128)S(1)} %get-tuple-element.47.refs_1_, bf16[2,80,256]{2,1,0:T(8,128)(2,1)S(1)} %collective-permute-done.9.refs_2_, f32[5,80,256]{2,1,0:T(8,128)S(1)} %static_planes.1.refs_3_, ...), custom_call_target="tpu_custom_call" | custom-call | tf_op jit(solution)/shard_map/diffuse/pallas_call | solution.py:308
  (12 shorter events, 0.1 us)
Async XLA Ops:
  14.0 9.6 %copy-start = (f32[4,64,256]{2,1,0:T(8,128)S(1)}, f32[4,64,256]{2,1,0:T(8,128)}, u32[]{:S(2)}) copy-start(f32[4,64,256]{2,1,0:T(8,128)} %refs_0_.1) | copy-start | bytes 786436
  14.0 9.6 %copy-start.2 = (f32[64,256]{1,0:T(8,128)S(1)}, f32[64,256]{1,0:T(8,128)}, u32[]{:S(2)}) copy-start(f32[64,256]{1,0:T(8,128)} %param.15) | copy-start | bytes 196612
  14.0 35.6 %copy-start.1 = (bf16[576,512]{1,0:T(8,128)(2,1)S(1)}, bf16[576,512]{1,0:T(8,128)(2,1)}, u32[]{:S(2)}) copy-start(bf16[576,512]{1,0:T(8,128)(2,1)} %get-tuple-element.42.refs_0_) | copy-start | bytes 1769476
  14.0 36.8 %all-to-all-start = ((bf16[8,256,512]{2,1,0:T(8,128)(2,1)}), bf16[8,256,512]{2,1,0:T(8,128)(2,1)S(1)}, u32[]{:S(2)}, u32[]{:S(2)}) async-start(bf16[8,256,512]{2,1,0:T(8,128)(2,1)} %bitcast.5), calls=%async_computation | async-start | bytes 4194304 | tf_op jit(solution)/shard_map/all_to_all | solution.py:336
  19.7 29.9 %collective-permute-start.3 = (bf16[576,512]{1,0:T(8,128)(2,1)}, bf16[576,512]{1,0:T(8,128)(2,1)S(1)}, u32[]{:S(2)}, u32[]{:S(2)}) collective-permute-start(bf16[576,512]{1,0:T(8,128)(2,1)} %get-tuple-element.35), channel_id=1, source_target_pairs={{0,8},{8,16},{16,24},{24,0},{1,9},{9,17},{17,25},{25,1},{2,10},{10... | collective-permute-start | bytes 1769480 | tf_op jit(solution)/shard_map/ppermute | solution.py:330
  20.9 28.7 %collective-permute-start.4 = (bf16[576,512]{1,0:T(8,128)(2,1)}, bf16[576,512]{1,0:T(8,128)(2,1)S(1)}, u32[]{:S(2)}, u32[]{:S(2)}) collective-permute-start(bf16[576,512]{1,0:T(8,128)(2,1)} %get-tuple-element.36), channel_id=1, source_target_pairs={{0,16},{8,24},{16,0},{24,8},{1,17},{9,25},{17,1},{25,9},{2,18},{10... | collective-permute-start | bytes 1769480 | tf_op jit(solution)/shard_map/ppermute | solution.py:330
  21.7 27.9 %collective-permute-start.5 = (bf16[576,512]{1,0:T(8,128)(2,1)}, bf16[576,512]{1,0:T(8,128)(2,1)S(1)}, u32[]{:S(2)}, u32[]{:S(2)}) collective-permute-start(bf16[576,512]{1,0:T(8,128)(2,1)} %get-tuple-element.37), channel_id=1, source_target_pairs={{0,24},{8,0},{16,8},{24,16},{1,25},{9,1},{17,9},{25,17},{2,26},{10... | collective-permute-start | bytes 1769480 | tf_op jit(solution)/shard_map/ppermute | solution.py:330
  23.6 23.4 %collective-permute-start.6 = (f32[20,256]{1,0:T(8,128)S(1)}, f32[20,256]{1,0:T(8,128)S(1)}, u32[]{:S(2)}, u32[]{:S(2)}) collective-permute-start(f32[20,256]{1,0:T(8,128)S(1)} %get-tuple-element.40), channel_id=1, source_target_pairs={{0,8},{8,16},{16,24},{1,9},{9,17},{17,25},{2,10},{10,18},{18,26},{... | collective-permute-start | bytes 61448 | tf_op jit(solution)/shard_map/ppermute | solution.py:351
  25.5 24.1 %collective-permute-start.7 = (f32[20,256]{1,0:T(8,128)S(1)}, f32[20,256]{1,0:T(8,128)S(1)}, u32[]{:S(2)}, u32[]{:S(2)}) collective-permute-start(f32[20,256]{1,0:T(8,128)S(1)} %get-tuple-element.41), channel_id=1, source_target_pairs={{8,0},{16,8},{24,16},{9,1},{17,9},{25,17},{10,2},{18,10},{26,18},{... | collective-permute-start | bytes 61448 | tf_op jit(solution)/shard_map/ppermute | solution.py:352
  50.7 15.1 %all-to-all-start.1 = ((bf16[8,80,512]{2,1,0:T(8,128)(2,1)}), bf16[8,80,512]{2,1,0:T(8,128)(2,1)S(1)}, u32[]{:S(2)}, u32[]{:S(2)}) async-start(bf16[8,80,512]{2,1,0:T(8,128)(2,1)} %sum_arrays.1), calls=%async_computation.1 | async-start | bytes 1310720 | tf_op jit(solution)/shard_map/all_to_all | solution.py:336
  55.9 32.1 %copy-start.3 = (f32[4,5]{1,0:T(4,128)S(1)}, f32[4,5]{1,0:T(4,128)}, u32[]{:S(2)}) copy-start(f32[4,5]{1,0:T(4,128)} %taps_ref.1) | copy-start | bytes 244
  56.2 9.7 %collective-permute-start = (bf16[80,512]{1,0:T(8,128)(2,1)S(1)}, bf16[80,512]{1,0:T(8,128)(2,1)S(1)}, u32[]{:S(2)}, u32[]{:S(2)}) collective-permute-start(bf16[80,512]{1,0:T(8,128)(2,1)S(1)} %get-tuple-element.31), channel_id=1, source_target_pairs={{0,8},{8,16},{16,24},{24,0},{1,9},{9,17},{17,25},{25,1},{2,10},{10... | collective-permute-start | bytes 245768 | tf_op jit(solution)/shard_map/ppermute | solution.py:330
  56.3 9.6 %collective-permute-start.1 = (bf16[80,512]{1,0:T(8,128)(2,1)S(1)}, bf16[80,512]{1,0:T(8,128)(2,1)S(1)}, u32[]{:S(2)}, u32[]{:S(2)}) collective-permute-start(bf16[80,512]{1,0:T(8,128)(2,1)S(1)} %get-tuple-element.32), channel_id=1, source_target_pairs={{0,16},{8,24},{16,0},{24,8},{1,17},{9,25},{17,1},{25,9},{2,18},{10... | collective-permute-start | bytes 245768 | tf_op jit(solution)/shard_map/ppermute | solution.py:330
  58.0 7.9 %collective-permute-start.2 = (bf16[80,512]{1,0:T(8,128)(2,1)S(1)}, bf16[80,512]{1,0:T(8,128)(2,1)S(1)}, u32[]{:S(2)}, u32[]{:S(2)}) collective-permute-start(bf16[80,512]{1,0:T(8,128)(2,1)S(1)} %get-tuple-element.33), channel_id=1, source_target_pairs={{0,24},{8,0},{16,8},{24,16},{1,25},{9,1},{17,9},{25,17},{2,26},{10... | collective-permute-start | bytes 245768 | tf_op jit(solution)/shard_map/ppermute | solution.py:330
  66.2 9.5 %collective-permute-start.8 = (bf16[2,80,256]{2,1,0:T(8,128)(2,1)S(1)}, bf16[2,80,256]{2,1,0:T(8,128)(2,1)S(1)}, u32[]{:S(2)}, u32[]{:S(2)}) collective-permute-start(bf16[2,80,256]{2,1,0:T(8,128)(2,1)S(1)} %get-tuple-element.46), channel_id=1, source_target_pairs={{0,32},{32,64},{64,96},{96,128},{128,160},{160,192},{192,224},{1,3... | collective-permute-start | bytes 245768 | tf_op jit(solution)/shard_map/ppermute | solution.py:359
  73.7 8.7 %collective-permute-start.9 = (bf16[2,80,256]{2,1,0:T(8,128)(2,1)S(1)}, bf16[2,80,256]{2,1,0:T(8,128)(2,1)S(1)}, u32[]{:S(2)}, u32[]{:S(2)}) collective-permute-start(bf16[2,80,256]{2,1,0:T(8,128)(2,1)S(1)} %get-tuple-element.48), channel_id=1, source_target_pairs={{32,0},{64,32},{96,64},{128,96},{160,128},{192,160},{224,192},{33,... | collective-permute-start | bytes 245768 | tf_op jit(solution)/shard_map/ppermute | solution.py:360
  82.8 5.2 %collective-permute-start.10 = (f32[80,128]{1,0:T(8,128)S(1)}, f32[80,128]{1,0:T(8,128)S(1)}, u32[]{:S(2)}, u32[]{:S(2)}) collective-permute-start(f32[80,128]{1,0:T(8,128)S(1)} %get-tuple-element.51), channel_id=1, source_target_pairs={{0,1},{1,2},{2,3},{3,4},{4,5},{5,6},{6,7},{7,0},{8,9},{9,10},{10,1... | collective-permute-start | bytes 122888 | tf_op jit(solution)/shard_map/ppermute | solution.py:363
  83.2 4.8 %collective-permute-start.11 = (f32[80,128]{1,0:T(8,128)S(1)}, f32[80,128]{1,0:T(8,128)S(1)}, u32[]{:S(2)}, u32[]{:S(2)}) collective-permute-start(f32[80,128]{1,0:T(8,128)S(1)} %get-tuple-element.52), channel_id=1, source_target_pairs={{1,0},{2,1},{3,2},{4,3},{5,4},{6,5},{7,6},{0,7},{9,8},{10,9},{11,1... | collective-permute-start | bytes 122888 | tf_op jit(solution)/shard_map/ppermute | solution.py:364

commit v8 on v7

--- a/solution.py
+++ b/solution.py
@@ -29,63 +29,78 @@
 
 def bin_sums(ids, residual, footprint):
     rows = N_GX * BINS
+    most = BINS - 8
 
     def body(tile_ref, step_ref, block_ref, res_ref, fp_ref, first_ref, *refs):
-        sel_ref = refs[-1]
-        c = pl.program_id(0)
-
-        @pl.when(c == 0)
-        def _():
-            tile = tile_ref[...].reshape(1, SND)
-            block = block_ref[...].reshape(1, SND)
-            local = (block >> 1) * 8 + step_ref[...].reshape(1, SND) * 2 + (block & 1)
-            away = (tile // N_GX - lax.axis_index("gy")) & (N_GY - 1)
-            bins = ((away * N_GX + (tile & (N_GX - 1))) * BINS + local).astype(jnp.int16)
-            weight = jnp.broadcast_to(res_ref[...].reshape(1, SND).astype(BF16), (16, SND))
-            number = lax.broadcasted_iota(jnp.int32, (16, SND), 0).astype(jnp.int16)
-            above = bins - number
-
-            @pl.loop(0, TILES * BINS // 16, unroll=4)
-            def _(m):
-                hit = above == (m * 16).astype(jnp.int16)
-                sel_ref[pl.ds(pl.multiple_of(m * 16, 16), 16), :] = jnp.where(
-                    hit, weight, jnp.zeros((16, SND), BF16)
-                )
-
-        def sums(k):
-            return jnp.dot(
-                sel_ref[k * rows : (k + 1) * rows, :],
-                fp_ref[...],
-                preferred_element_type=F32,
+        fp_buf, sel_ref, first_buf, second_buf, in_sems, first_sems, second_sems = refs[N_GY:]
+        loads = [
+            pltpu.make_async_copy(
+                fp_ref.at[:, pl.ds(h * HALF, HALF)], fp_buf.at[h], in_sems.at[h]
             )
-
-        @pl.when(c == 0)
-        def _():
-            for k in range(N_GY):
-                out = sums(k).astype(BF16)
-                for q in range(N_GX):
-                    at = (q * N_GY + k) * BINS
-                    first_ref[at : at + BINS, :] = out[q * BINS : (q + 1) * BINS]
-
-        @pl.when(c == 1)
-        def _():
-            for k in range(N_GY):
-                out = sums(k)
-                refs[k][:rows, :] = out.astype(BF16)
-                last = [out[(q + 1) * BINS - 8 : (q + 1) * BINS] for q in range(N_GX)]
-                refs[(k + 1) % N_GY][rows:, :] = jnp.concatenate(last, axis=0).astype(BF16)
-
-    one = pl.BlockSpec((SND,), lambda c: (0,))
-    each = rows + N_GX * 8
+            for h in range(2)
+        ]
+        for load in loads:
+            load.start()
+        tile = tile_ref[...].reshape(1, SND)
+        block = block_ref[...].reshape(1, SND)
+        local = (block >> 1) * 8 + step_ref[...].reshape(1, SND) * 2 + (block & 1)
+        away = (tile // N_GX - lax.axis_index("gy")) & (N_GY - 1)
+        bins = ((away * N_GX + (tile & (N_GX - 1))) * BINS + local).astype(jnp.int16)
+        weight = jnp.broadcast_to(res_ref[...].reshape(1, SND).astype(BF16), (16, SND))
+        above = bins - lax.broadcasted_iota(jnp.int32, (16, SND), 0).astype(jnp.int16)
+
+        @pl.loop(0, TILES * BINS // 16, unroll=4)
+        def _(m):
+            hit = above == (m * 16).astype(jnp.int16)
+            sel_ref[pl.ds(pl.multiple_of(m * 16, 16), 16), :] = jnp.where(
+                hit, weight, jnp.zeros((16, SND), BF16)
+            )
+
+        for load in loads:
+            load.wait()
+        stores = []
+        for k in range(N_GY):
+            halves = [
+                jnp.dot(
+                    sel_ref[k * rows : (k + 1) * rows, :],
+                    fp_buf[h],
+                    preferred_element_type=F32,
+                ).reshape(N_GX, BINS, HALF)
+                for h in range(2)
+            ]
+            for h, buf in enumerate((first_buf, second_buf)):
+                both = [halves[h][:, :most], halves[1 - h][:, most:]]
+                buf[k] = jnp.concatenate(both, axis=1).astype(BF16)
+            stores += [
+                pltpu.make_async_copy(
+                    first_buf.at[k],
+                    first_ref.at[:, pl.ds(k * BINS, BINS), :],
+                    first_sems.at[k],
+                ),
+                pltpu.make_async_copy(second_buf.at[k], refs[k], second_sems.at[k]),
+            ]
+            stores[-2].start()
+            stores[-1].start()
+        for store in stores:
+            store.wait()
+
+    one = pl.BlockSpec((SND,), lambda: (0,))
+    far = pl.BlockSpec(memory_space=pl.ANY)
     outs = pl.pallas_call(
         body,
-        grid=(2,),
-        in_specs=[one] * 4 + [pl.BlockSpec((SND, HALF), lambda c: (0, c))],
-        out_specs=[pl.BlockSpec((TILES * BINS, HALF), lambda c: (0, 0))]
-        + [pl.BlockSpec((each, HALF), lambda c: (0, 0))] * N_GY,
-        out_shape=[jax.ShapeDtypeStruct((TILES * BINS, HALF), BF16)]
-        + [jax.ShapeDtypeStruct((each, HALF), BF16)] * N_GY,
-        scratch_shapes=[pltpu.VMEM((TILES * BINS, SND), BF16)],
+        in_specs=[one] * 4 + [far],
+        out_specs=[far] * (1 + N_GY),
+        out_shape=[jax.ShapeDtypeStruct((N_GX, N_GY * BINS, HALF), BF16)]
+        + [jax.ShapeDtypeStruct((N_GX, BINS, HALF), BF16)] * N_GY,
+        scratch_shapes=[
+            pltpu.VMEM((2, SND, HALF), BF16),
+            pltpu.VMEM((TILES * BINS, SND), BF16),
+            pltpu.VMEM((N_GY, N_GX, BINS, HALF), BF16),
+            pltpu.VMEM((N_GY, N_GX, BINS, HALF), BF16),
+            pltpu.SemaphoreType.DMA((2,)),
+            pltpu.SemaphoreType.DMA((N_GY,)),
+            pltpu.SemaphoreType.DMA((N_GY,)),
+        ],
         compiler_params=pltpu.CompilerParams(vmem_limit_bytes=58 * MIB),
         cost_estimate=pl.CostEstimate(
             flops=2 * TILES * BINS * SND * FP, bytes_accessed=8 * MIB, transcendentals=0
@@ -106,10 +121,10 @@
             for s in range(1, count):
                 total = total + got_ref[s, at].astype(F32)
             totals.append(total)
-        none = jnp.zeros((8, cols), F32)
         for k, out_ref in enumerate(out_refs):
             below = totals[(k + 1) % N_GY][:8]
-            out_ref[...] = jnp.concatenate([totals[k], below, none], axis=0).astype(BF16)
+            over = totals[(k - 1) % N_GY][BINS - 8 :]
+            out_ref[...] = jnp.concatenate([totals[k], below, over], axis=0).astype(BF16)
 
     return pl.pallas_call(
         body,
@@ -120,25 +135,16 @@
 
 
 def sum_arrays(arrays):
-    cols = arrays[0].shape[1]
-
-    def body(*refs):
-        def total(at):
-            out = refs[0][at].astype(F32)
+    def body(*refs):
+        for q in range(N_GX):
+            total = refs[0][q].astype(F32)
             for ref in refs[1:-1]:
-                out = out + ref[at].astype(F32)
-            return out
-
-        above = total(pl.ds(N_GX * BINS, N_GX * 8))
-        none = jnp.zeros((8, cols), F32)
-        for q in range(N_GX):
-            halo = jnp.concatenate([above[q * 8 : q * 8 + 8], none], axis=0)
-            refs[-1][q, :BINS] = total(pl.ds(q * BINS, BINS)).astype(BF16)
-            refs[-1][q, BINS:] = halo.astype(BF16)
-
-    return pl.pallas_call(
-        body,
-        out_shape=jax.ShapeDtypeStruct((N_GX, ROWS, cols), BF16),
+                total = total + ref[q].astype(F32)
+            refs[-1][q] = total.astype(BF16)
+
+    return pl.pallas_call(
+        body,
+        out_shape=jax.ShapeDtypeStruct(arrays[0].shape, BF16),
         compiler_params=pltpu.CompilerParams(vmem_limit_bytes=12 * MIB),
         name="sum_arrays",
     )(*arrays)
@@ -163,11 +169,13 @@
             ]
 
         for i in range(4):
-            for br in range(8):
+            for br in range(7):
                 put(8 + br * 8 + i, first, br * 8, i)
                 put(8 + br * 8 + 4 + i, last, br * 8, i)
-            put(4 + i, last, BINS, i)
+            put(LAT + i, last, BINS - 8, i)
+            put(LAT + 4 + i, first, BINS - 8, i)
             put(8 + LAT + i, first, BINS, i)
+            put(4 + i, first, BINS + 8, i)
         for t in range(TS_DEV):
             for bc in range(2):
                 at = (t * 2 + bc) * PAD_LAT
@@ -342,7 +350,7 @@
     later, sooner = steps("ta", False)
     ids = (tile_id[:, 0], step_id, block_id)
     first_gx, first_gy = bin_sums(ids, residual, footprint)
-    got_gx = along_gx(first_gx.reshape(N_GX, N_GY * BINS, HALF))
+    got_gx = along_gx(first_gx)
     came_gy = along_gy(first_gy)
 
     fixed = (sigma, diffusivity[None])

time: 95.2 us -> 89.5 us (0.940)
  waiting for transfers between devices: 34.8 us -> 29.5 us
  Pallas kernels: 22.8 us -> 21.6 us
    ppermute x1, waiting for transfers between devices: 18.1 us -> 15.3 us  [per_device(): up = lax.ppermute(to_down, 'gy', south)]
    all_to_all x2, waiting for transfers between devices: 5.88 us -> 3.85 us  [along_gx(): return lax.all_to_all(rows, 'gx', 0, 0, tiled=True)]
    pallas_call x2, Pallas kernels: 15.1 us -> 13.9 us  [the longest x1 12.8 us: bin_sums(): pl.pallas_call(body, in_specs=[one] * 4 + [far], out_specs=[far] * (1 + N...]
where the time goes in v8:
time: 89.5 us; the launch traced here: 88.9 us
  starting transfers between devices  37.6 us (42%)
  waiting for transfers between devices  29.5 us (33%)
  Pallas kernels  21.6 us (24%)
    ppermute x1, waiting for transfers between devices, per_device(): up = lax.ppermute(to_down, 'gy', south)  15.3 us
    pallas_call x1, Pallas kernels, bin_sums(): pl.pallas_call(body, in_specs=[one] * 4 + [far], out_specs=[far] * (1 + N...  12.8 us
    all_to_all x2, starting transfers between devices, along_gx(): return lax.all_to_all(rows, 'gx', 0, 0, tiled=True)  10.8 us
    ppermute x6, starting transfers between devices, along_gy(): lax.ppermute(parts[k], 'gy', [(i, (i + k) % N_GY) for i in range(N_GY)])  8.18 us
    ppermute x1, starting transfers between devices, per_device(): before = lax.ppermute(high, 'ta', later)  7.74 us
    pallas_call x1, Pallas kernels, diffuse(): pl.pallas_call(body, grid=(TRACERS,), in_specs=[pl.BlockSpec(memory_space...  6.84 us
    ppermute x1, waiting for transfers between devices, per_device(): after = lax.ppermute(low, 'ta', sooner)  6.77 us
    all_to_all x2, waiting for transfers between devices, along_gx(): return lax.all_to_all(rows, 'gx', 0, 0, tiled=True)  3.85 us
  transfers between devices with their start and end apart: 14, of which 5 were waited for; matrix products, arithmetic and copies ran while one was open for 0% of the time, Pallas kernels for 2%

profile of v8, /device:TPU:67, one launch (start us, length us, event | category | flops | bytes accessed | tf_op | source)
XLA Modules:
  0.0 88.9 jit_solution(15385355700343624587)
XLA Ops:
  0.0 12.8 %bin_sums.1 = (bf16[8,256,512]{2,1,0:T(8,128)(2,1)}, bf16[8,64,512]{2,1,0:T(8,128)(2,1)}, bf16[8,64,512]{2,1,0:T(8,128)(2,1)}, bf16[8,64,512]{2,1,0:T(8,128)(2,1)}, bf16[8,64,512]{2,1,0:T(8,128)(2,1)}) custom-call(s32[2048]{0:T(1024)} %bitcast.4, s32[2048]{0:T(1024)} %step_ref.1, s32[2048]{0:T(1024)} %block_ref.1, bf16[2048]{0:T(1024)(128)(2,1)} %res_ref.1, ...), custom_call_target="tpu_custom_call" | custom-call | flops 8589934592 | bytes 8388608 | tf_op jit(solution)/shard_map/bin_sums/pallas_call | solution.py:89
  12.9 0.0 copy-start
  12.9 0.0 copy-start.2
  12.9 0.0 copy-start.1
  12.9 5.7 %all-to-all-start = ((bf16[8,256,512]{2,1,0:T(8,128)(2,1)}), bf16[8,256,512]{2,1,0:T(8,128)(2,1)S(1)}, u32[]{:S(2)}, u32[]{:S(2)}) async-start(bf16[8,256,512]{2,1,0:T(8,128)(2,1)} %get-tuple-element.29), calls=%async_computation | async-start | bytes 4194304 | tf_op jit(solution)/shard_map/all_to_all | solution.py:344
  18.6 1.2 %collective-permute-start.3 = (bf16[8,64,512]{2,1,0:T(8,128)(2,1)}, bf16[8,64,512]{2,1,0:T(8,128)(2,1)S(1)}, u32[]{:S(2)}, u32[]{:S(2)}) collective-permute-start(bf16[8,64,512]{2,1,0:T(8,128)(2,1)} %get-tuple-element.35), channel_id=1, source_target_pairs={{0,8},{8,16},{16,24},{24,0},{1,9},{9,17},{17,25},{25,1},{2,10},{10... | collective-permute-start | bytes 1572872 | tf_op jit(solution)/shard_map/ppermute | solution.py:338
  19.8 0.8 collective-permute-start.4
  20.6 1.9 %collective-permute-start.5 = (bf16[8,64,512]{2,1,0:T(8,128)(2,1)S(1)}, bf16[8,64,512]{2,1,0:T(8,128)(2,1)S(1)}, u32[]{:S(2)}, u32[]{:S(2)}) collective-permute-start(bf16[8,64,512]{2,1,0:T(8,128)(2,1)S(1)} %copy-done.4), channel_id=1, source_target_pairs={{0,24},{8,0},{16,8},{24,16},{1,25},{9,1},{17,9},{25,17},{2,26},{10... | collective-permute-start | bytes 1572872 | tf_op jit(solution)/shard_map/ppermute | solution.py:338
  22.5 1.9 %collective-permute-start.6 = (f32[20,256]{1,0:T(8,128)S(1)}, f32[20,256]{1,0:T(8,128)S(1)}, u32[]{:S(2)}, u32[]{:S(2)}) collective-permute-start(f32[20,256]{1,0:T(8,128)S(1)} %get-tuple-element.40), channel_id=1, source_target_pairs={{0,8},{8,16},{16,24},{1,9},{9,17},{17,25},{2,10},{10,18},{18,26},{... | collective-permute-start | bytes 61448 | tf_op jit(solution)/shard_map/ppermute | solution.py:359
  24.5 3.4 %collective-permute-start.7 = (f32[20,256]{1,0:T(8,128)S(1)}, f32[20,256]{1,0:T(8,128)S(1)}, u32[]{:S(2)}, u32[]{:S(2)}) collective-permute-start(f32[20,256]{1,0:T(8,128)S(1)} %get-tuple-element.41), channel_id=1, source_target_pairs={{8,0},{16,8},{24,16},{9,1},{17,9},{25,17},{10,2},{18,10},{26,18},{... | collective-permute-start | bytes 61448 | tf_op jit(solution)/shard_map/ppermute | solution.py:360
  27.8 15.3 %collective-permute-done.6.refs_2_ = f32[20,256]{1,0:T(8,128)S(1)} collective-permute-done((f32[20,256]{1,0:T(8,128)S(1)}, f32[20,256]{1,0:T(8,128)S(1)}, u32[]{:S(2)}, u32[]{:S(2)}) %collective-permute-start.6) | collective-permute-done | bytes 20512 | tf_op jit(solution)/shard_map/ppermute | solution.py:359
  43.1 2.2 %collective-permute-done.7.refs_3_ = f32[20,256]{1,0:T(8,128)S(1)} collective-permute-done((f32[20,256]{1,0:T(8,128)S(1)}, f32[20,256]{1,0:T(8,128)S(1)}, u32[]{:S(2)}, u32[]{:S(2)}) %collective-permute-start.7) | collective-permute-done | bytes 20512 | tf_op jit(solution)/shard_map/ppermute | solution.py:360
  45.3 0.0 collective-permute-done.3.refs_1_
  45.3 0.0 collective-permute-done.4.refs_2_
  45.3 0.0 collective-permute-done.5.refs_3_
  45.3 1.1 %sum_arrays.1 = bf16[8,64,512]{2,1,0:T(8,128)(2,1)} custom-call(bf16[8,64,512]{2,1,0:T(8,128)(2,1)S(1)} %copy-done.1, bf16[8,64,512]{2,1,0:T(8,128)(2,1)S(1)} %collective-permute-done.3.refs_1_, bf16[8,64,512]{2,1,0:T(8,128)(2,1)S(1)} %collective-permute-done.4.refs_2_, bf16[8,64,512]{2,1,0:T(8,128)(2,1)S(1)} %collective-permute-done.5.refs_3_), custom_call_target="tpu_custom_call" | custom-call | tf_op jit(solution)/shard_map/sum_arrays/pallas_call | solution.py:145
  46.4 5.1 %all-to-all-start.1 = ((bf16[8,64,512]{2,1,0:T(8,128)(2,1)}), bf16[8,64,512]{2,1,0:T(8,128)(2,1)S(1)}, u32[]{:S(2)}, u32[]{:S(2)}) async-start(bf16[8,64,512]{2,1,0:T(8,128)(2,1)} %sum_arrays.1), calls=%async_computation.1 | async-start | bytes 1048576 | tf_op jit(solution)/shard_map/all_to_all | solution.py:344
  51.5 0.3 sum_first.1
  51.8 0.3 collective-permute-start
  52.1 2.0 %collective-permute-start.1 = (bf16[80,512]{1,0:T(8,128)(2,1)S(1)}, bf16[80,512]{1,0:T(8,128)(2,1)S(1)}, u32[]{:S(2)}, u32[]{:S(2)}) collective-permute-start(bf16[80,512]{1,0:T(8,128)(2,1)S(1)} %get-tuple-element.32), channel_id=1, source_target_pairs={{0,16},{8,24},{16,0},{24,8},{1,17},{9,25},{17,1},{25,9},{2,18},{10... | collective-permute-start | bytes 245768 | tf_op jit(solution)/shard_map/ppermute | solution.py:338
  54.1 2.0 %collective-permute-start.2 = (bf16[80,512]{1,0:T(8,128)(2,1)S(1)}, bf16[80,512]{1,0:T(8,128)(2,1)S(1)}, u32[]{:S(2)}, u32[]{:S(2)}) collective-permute-start(bf16[80,512]{1,0:T(8,128)(2,1)S(1)} %get-tuple-element.33), channel_id=1, source_target_pairs={{0,24},{8,0},{16,8},{24,16},{1,25},{9,1},{17,9},{25,17},{2,26},{10... | collective-permute-start | bytes 245768 | tf_op jit(solution)/shard_map/ppermute | solution.py:338
  56.1 3.9 %all-to-all-done.1.refs_4_ = bf16[8,64,512]{2,1,0:T(8,128)(2,1)S(1)} async-done(((bf16[8,64,512]{2,1,0:T(8,128)(2,1)}), bf16[8,64,512]{2,1,0:T(8,128)(2,1)S(1)}, u32[]{:S(2)}, u32[]{:S(2)}) %all-to-all-start.1) | async-done | bytes 524320 | tf_op jit(solution)/shard_map/all_to_all | solution.py:344
  59.9 0.3 tile_sum.1
  60.2 7.7 %collective-permute-start.8 = (bf16[2,80,256]{2,1,0:T(8,128)(2,1)S(1)}, bf16[2,80,256]{2,1,0:T(8,128)(2,1)S(1)}, u32[]{:S(2)}, u32[]{:S(2)}) collective-permute-start(bf16[2,80,256]{2,1,0:T(8,128)(2,1)S(1)} %get-tuple-element.46), channel_id=1, source_target_pairs={{0,32},{32,64},{64,96},{96,128},{128,160},{160,192},{192,224},{1,3... | collective-permute-start | bytes 245768 | tf_op jit(solution)/shard_map/ppermute | solution.py:367
  67.9 1.9 %collective-permute-start.9 = (bf16[2,80,256]{2,1,0:T(8,128)(2,1)S(1)}, bf16[2,80,256]{2,1,0:T(8,128)(2,1)S(1)}, u32[]{:S(2)}, u32[]{:S(2)}) collective-permute-start(bf16[2,80,256]{2,1,0:T(8,128)(2,1)S(1)} %get-tuple-element.48), channel_id=1, source_target_pairs={{32,0},{64,32},{96,64},{128,96},{160,128},{192,160},{224,192},{33,... | collective-permute-start | bytes 245768 | tf_op jit(solution)/shard_map/ppermute | solution.py:368
  69.9 0.0 collective-permute-done.8.refs_0_
  69.9 6.8 %collective-permute-done.9.refs_2_ = bf16[2,80,256]{2,1,0:T(8,128)(2,1)S(1)} collective-permute-done((bf16[2,80,256]{2,1,0:T(8,128)(2,1)S(1)}, bf16[2,80,256]{2,1,0:T(8,128)(2,1)S(1)}, u32[]{:S(2)}, u32[]{:S(2)}) %collective-permute-start.9) | collective-permute-done | bytes 81952 | tf_op jit(solution)/shard_map/ppermute | solution.py:368
  76.7 0.3 halo_lon.1
  77.0 0.3 collective-permute-start.10
  77.3 3.3 %collective-permute-start.11 = (f32[80,128]{1,0:T(8,128)S(1)}, f32[80,128]{1,0:T(8,128)S(1)}, u32[]{:S(2)}, u32[]{:S(2)}) collective-permute-start(f32[80,128]{1,0:T(8,128)S(1)} %get-tuple-element.52), channel_id=1, source_target_pairs={{1,0},{2,1},{3,2},{4,3},{5,4},{6,5},{7,6},{0,7},{9,8},{10,9},{11,1... | collective-permute-start | bytes 122888 | tf_op jit(solution)/shard_map/ppermute | solution.py:372
  80.6 1.4 %collective-permute-done.10.refs_4_ = f32[80,128]{1,0:T(8,128)S(1)} collective-permute-done((f32[80,128]{1,0:T(8,128)S(1)}, f32[80,128]{1,0:T(8,128)S(1)}, u32[]{:S(2)}, u32[]{:S(2)}) %collective-permute-start.10) | collective-permute-done | bytes 40992 | tf_op jit(solution)/shard_map/ppermute | solution.py:371
  82.0 6.8 %diffuse.1 = f32[4,4,64,256]{3,2,1,0:T(8,128)} custom-call(f32[4,5]{1,0:T(4,128)S(1)} %copy-done.3, bf16[2,80,256]{2,1,0:T(8,128)(2,1)S(1)} %collective-permute-done.8.refs_0_, f32[4,80,256]{2,1,0:T(8,128)S(1)} %get-tuple-element.47.refs_1_, bf16[2,80,256]{2,1,0:T(8,128)(2,1)S(1)} %collective-permute-done.9.refs_2_, f32[5,80,256]{2,1,0:T(8,128)S(1)} %static_planes.1.refs_3_, ...), custom_call_target="tpu_custom_call" | custom-call | tf_op jit(solution)/shard_map/diffuse/pallas_call | solution.py:316
  (14 shorter events, 0.1 us)
Async XLA Ops:
  12.9 7.8 %copy-start.4 = (bf16[8,64,512]{2,1,0:T(8,128)(2,1)S(1)}, bf16[8,64,512]{2,1,0:T(8,128)(2,1)}, u32[]{:S(2)}) copy-start(bf16[8,64,512]{2,1,0:T(8,128)(2,1)} %get-tuple-element.37) | copy-start | bytes 1572868
  12.9 9.6 %copy-start = (f32[4,64,256]{2,1,0:T(8,128)S(1)}, f32[4,64,256]{2,1,0:T(8,128)}, u32[]{:S(2)}) copy-start(f32[4,64,256]{2,1,0:T(8,128)} %refs_0_.1) | copy-start | bytes 786436
  12.9 9.6 %copy-start.2 = (f32[64,256]{1,0:T(8,128)S(1)}, f32[64,256]{1,0:T(8,128)}, u32[]{:S(2)}) copy-start(f32[64,256]{1,0:T(8,128)} %param.15) | copy-start | bytes 196612
  12.9 32.4 %copy-start.1 = (bf16[8,64,512]{2,1,0:T(8,128)(2,1)S(1)}, bf16[8,64,512]{2,1,0:T(8,128)(2,1)}, u32[]{:S(2)}) copy-start(bf16[8,64,512]{2,1,0:T(8,128)(2,1)} %get-tuple-element.42.refs_0_) | copy-start | bytes 1572868
  12.9 33.5 %all-to-all-start = ((bf16[8,256,512]{2,1,0:T(8,128)(2,1)}), bf16[8,256,512]{2,1,0:T(8,128)(2,1)S(1)}, u32[]{:S(2)}, u32[]{:S(2)}) async-start(bf16[8,256,512]{2,1,0:T(8,128)(2,1)} %get-tuple-element.29), calls=%async_computation | async-start | bytes 4194304 | tf_op jit(solution)/shard_map/all_to_all | solution.py:344
  18.6 26.7 %collective-permute-start.3 = (bf16[8,64,512]{2,1,0:T(8,128)(2,1)}, bf16[8,64,512]{2,1,0:T(8,128)(2,1)S(1)}, u32[]{:S(2)}, u32[]{:S(2)}) collective-permute-start(bf16[8,64,512]{2,1,0:T(8,128)(2,1)} %get-tuple-element.35), channel_id=1, source_target_pairs={{0,8},{8,16},{16,24},{24,0},{1,9},{9,17},{17,25},{25,1},{2,10},{10... | collective-permute-start | bytes 1572872 | tf_op jit(solution)/shard_map/ppermute | solution.py:338
  19.8 25.5 %collective-permute-start.4 = (bf16[8,64,512]{2,1,0:T(8,128)(2,1)}, bf16[8,64,512]{2,1,0:T(8,128)(2,1)S(1)}, u32[]{:S(2)}, u32[]{:S(2)}) collective-permute-start(bf16[8,64,512]{2,1,0:T(8,128)(2,1)} %get-tuple-element.36), channel_id=1, source_target_pairs={{0,16},{8,24},{16,0},{24,8},{1,17},{9,25},{17,1},{25,9},{2,18},{10... | collective-permute-start | bytes 1572872 | tf_op jit(solution)/shard_map/ppermute | solution.py:338
  20.6 24.7 %collective-permute-start.5 = (bf16[8,64,512]{2,1,0:T(8,128)(2,1)S(1)}, bf16[8,64,512]{2,1,0:T(8,128)(2,1)S(1)}, u32[]{:S(2)}, u32[]{:S(2)}) collective-permute-start(bf16[8,64,512]{2,1,0:T(8,128)(2,1)S(1)} %copy-done.4), channel_id=1, source_target_pairs={{0,24},{8,0},{16,8},{24,16},{1,25},{9,1},{17,9},{25,17},{2,26},{10... | collective-permute-start | bytes 1572872 | tf_op jit(solution)/shard_map/ppermute | solution.py:338
  22.5 20.6 %collective-permute-start.6 = (f32[20,256]{1,0:T(8,128)S(1)}, f32[20,256]{1,0:T(8,128)S(1)}, u32[]{:S(2)}, u32[]{:S(2)}) collective-permute-start(f32[20,256]{1,0:T(8,128)S(1)} %get-tuple-element.40), channel_id=1, source_target_pairs={{0,8},{8,16},{16,24},{1,9},{9,17},{17,25},{2,10},{10,18},{18,26},{... | collective-permute-start | bytes 61448 | tf_op jit(solution)/shard_map/ppermute | solution.py:359
  24.5 20.8 %collective-permute-start.7 = (f32[20,256]{1,0:T(8,128)S(1)}, f32[20,256]{1,0:T(8,128)S(1)}, u32[]{:S(2)}, u32[]{:S(2)}) collective-permute-start(f32[20,256]{1,0:T(8,128)S(1)} %get-tuple-element.41), channel_id=1, source_target_pairs={{8,0},{16,8},{24,16},{9,1},{17,9},{25,17},{10,2},{18,10},{26,18},{... | collective-permute-start | bytes 61448 | tf_op jit(solution)/shard_map/ppermute | solution.py:360
  46.4 13.5 %all-to-all-start.1 = ((bf16[8,64,512]{2,1,0:T(8,128)(2,1)}), bf16[8,64,512]{2,1,0:T(8,128)(2,1)S(1)}, u32[]{:S(2)}, u32[]{:S(2)}) async-start(bf16[8,64,512]{2,1,0:T(8,128)(2,1)} %sum_arrays.1), calls=%async_computation.1 | async-start | bytes 1048576 | tf_op jit(solution)/shard_map/all_to_all | solution.py:344
  51.5 30.5 %copy-start.3 = (f32[4,5]{1,0:T(4,128)S(1)}, f32[4,5]{1,0:T(4,128)}, u32[]{:S(2)}) copy-start(f32[4,5]{1,0:T(4,128)} %taps_ref.1) | copy-start | bytes 244
  51.8 8.1 %collective-permute-start = (bf16[80,512]{1,0:T(8,128)(2,1)S(1)}, bf16[80,512]{1,0:T(8,128)(2,1)S(1)}, u32[]{:S(2)}, u32[]{:S(2)}) collective-permute-start(bf16[80,512]{1,0:T(8,128)(2,1)S(1)} %get-tuple-element.31), channel_id=1, source_target_pairs={{0,8},{8,16},{16,24},{24,0},{1,9},{9,17},{17,25},{25,1},{2,10},{10... | collective-permute-start | bytes 245768 | tf_op jit(solution)/shard_map/ppermute | solution.py:338
  52.1 7.8 %collective-permute-start.1 = (bf16[80,512]{1,0:T(8,128)(2,1)S(1)}, bf16[80,512]{1,0:T(8,128)(2,1)S(1)}, u32[]{:S(2)}, u32[]{:S(2)}) collective-permute-start(bf16[80,512]{1,0:T(8,128)(2,1)S(1)} %get-tuple-element.32), channel_id=1, source_target_pairs={{0,16},{8,24},{16,0},{24,8},{1,17},{9,25},{17,1},{25,9},{2,18},{10... | collective-permute-start | bytes 245768 | tf_op jit(solution)/shard_map/ppermute | solution.py:338
  54.1 5.8 %collective-permute-start.2 = (bf16[80,512]{1,0:T(8,128)(2,1)S(1)}, bf16[80,512]{1,0:T(8,128)(2,1)S(1)}, u32[]{:S(2)}, u32[]{:S(2)}) collective-permute-start(bf16[80,512]{1,0:T(8,128)(2,1)S(1)} %get-tuple-element.33), channel_id=1, source_target_pairs={{0,24},{8,0},{16,8},{24,16},{1,25},{9,1},{17,9},{25,17},{2,26},{10... | collective-permute-start | bytes 245768 | tf_op jit(solution)/shard_map/ppermute | solution.py:338
  60.2 9.7 %collective-permute-start.8 = (bf16[2,80,256]{2,1,0:T(8,128)(2,1)S(1)}, bf16[2,80,256]{2,1,0:T(8,128)(2,1)S(1)}, u32[]{:S(2)}, u32[]{:S(2)}) collective-permute-start(bf16[2,80,256]{2,1,0:T(8,128)(2,1)S(1)} %get-tuple-element.46), channel_id=1, source_target_pairs={{0,32},{32,64},{64,96},{96,128},{128,160},{160,192},{192,224},{1,3... | collective-permute-start | bytes 245768 | tf_op jit(solution)/shard_map/ppermute | solution.py:367
  67.9 8.7 %collective-permute-start.9 = (bf16[2,80,256]{2,1,0:T(8,128)(2,1)S(1)}, bf16[2,80,256]{2,1,0:T(8,128)(2,1)S(1)}, u32[]{:S(2)}, u32[]{:S(2)}) collective-permute-start(bf16[2,80,256]{2,1,0:T(8,128)(2,1)S(1)} %get-tuple-element.48), channel_id=1, source_target_pairs={{32,0},{64,32},{96,64},{128,96},{160,128},{192,160},{224,192},{33,... | collective-permute-start | bytes 245768 | tf_op jit(solution)/shard_map/ppermute | solution.py:368
  77.0 5.0 %collective-permute-start.10 = (f32[80,128]{1,0:T(8,128)S(1)}, f32[80,128]{1,0:T(8,128)S(1)}, u32[]{:S(2)}, u32[]{:S(2)}) collective-permute-start(f32[80,128]{1,0:T(8,128)S(1)} %get-tuple-element.51), channel_id=1, source_target_pairs={{0,1},{1,2},{2,3},{3,4},{4,5},{5,6},{6,7},{7,0},{8,9},{9,10},{10,1... | collective-permute-start | bytes 122888 | tf_op jit(solution)/shard_map/ppermute | solution.py:371
  77.3 4.7 %collective-permute-start.11 = (f32[80,128]{1,0:T(8,128)S(1)}, f32[80,128]{1,0:T(8,128)S(1)}, u32[]{:S(2)}, u32[]{:S(2)}) collective-permute-start(f32[80,128]{1,0:T(8,128)S(1)} %get-tuple-element.52), channel_id=1, source_target_pairs={{1,0},{2,1},{3,2},{4,3},{5,4},{6,5},{7,6},{0,7},{9,8},{10,9},{11,1... | collective-permute-start | bytes 122888 | tf_op jit(solution)/shard_map/ppermute | solution.py:372

commit v9 on v8

--- a/solution.py
+++ b/solution.py
@@ -267,60 +267,134 @@
     )(*arrays, up, down)
 
 
-def beside_lon(k, plane, left, right):
+def side_of(k, left, right):
     lane = lax.broadcasted_iota(jnp.int32, right.shape, 1)
     to_right = (-HALO * k) % 128
     to_left = (128 - HALO - HALO * k) % 128
     right = pltpu.roll(right, to_right, 1) if to_right else right
     left = pltpu.roll(left, to_left, 1) if to_left else left
-    side = jnp.where(lane < HALO, right, jnp.where(lane >= 128 - HALO, left, 0.0))
-    return jnp.concatenate([plane, side], axis=1)
+    return jnp.where(lane < HALO, right, jnp.where(lane >= 128 - HALO, left, 0.0))
+
+
+def strips_of(plane):
+    return [plane[8 * r : 8 * r + 8] for r in range(PAD_LAT // 8)]
+
+
+def up_and_down(field):
+    row = lax.broadcasted_iota(jnp.int32, field[0].shape, 0)
+    before = [pltpu.roll(f, 1, 0) for f in field]
+    after = [pltpu.roll(f, 7, 0) for f in field]
+    last = len(field) - 1
+    return [
+        jnp.where(row == 0, before[max(r - 1, 0)], before[r])
+        + jnp.where(row == 7, after[min(r + 1, last)], after[r])
+        for r in range(len(field))
+    ]
+
+
+def band(c, t, taps_ref, planes, scale):
+    out = []
+    for r, strip in enumerate(scale):
+        total = taps_ref[c, 0] * planes[t][r]
+        for k in range(1, 2 * HB + 1):
+            total = total + taps_ref[c, k] * planes[t + k][r]
+        out.append(strip * total)
+    return out
 
 
 def planes_of(refs):
     return [ref[k].astype(F32) for ref in refs for k in range(ref.shape[0])]
 
 
-def diffuse(arrays, left, right, taps):
+def begin(arrays, taps):
     n = TS_DEV + 2 * HB
 
     def body(taps_ref, *refs):
-        l_ref, r_ref, out_ref, pad_ref = refs[-4:]
-        c = pl.program_id(0)
-
-        @pl.when(c == 0)
-        def _():
-            for k, plane in enumerate(planes_of(refs[:-4])):
-                pad_ref[k] = beside_lon(k, plane, l_ref[...], r_ref[...])
-
-        banded = taps_ref[c, 0] * pad_ref[0:TS_DEV]
-        for k in range(1, 2 * HB + 1):
-            banded = banded + taps_ref[c, k] * pad_ref[k : k + TS_DEV]
-        field = pad_ref[n + c][None] * banded
-        rate = pad_ref[n + TRACERS][None]
-        for _ in range(KSTEPS):
-            beside = (
-                pltpu.roll(field, 1, 2)
-                + pltpu.roll(field, PAD_LON - 1, 2)
-                + pltpu.roll(field, 1, 1)
-                + pltpu.roll(field, PAD_LAT - 1, 1)
-            )
-            field = field + rate * (beside - 4.0 * field)
-        scale = pad_ref[n + c, 8 : 8 + LAT, :LON]
-        out_ref[0] = scale[None] * field[:, 8 : 8 + LAT, :LON]
-
-    def whole(a):
-        return pl.BlockSpec(a.shape, lambda c: (0,) * a.ndim)
-
-    operands = (*arrays, left, right)
-    return pl.pallas_call(
-        body,
-        grid=(TRACERS,),
-        in_specs=[pl.BlockSpec(memory_space=pltpu.SMEM)] + [whole(a) for a in operands],
-        out_specs=pl.BlockSpec((1, TS_DEV, LAT, LON), lambda c: (c, 0, 0, 0)),
+        start_ref, part_ref = refs[-2:]
+        planes = [strips_of(p) for p in planes_of(refs[:-2])]
+        for c in range(TRACERS):
+            for t in range(TS_DEV):
+                field = band(c, t, taps_ref, planes, planes[n + c])
+                for r, beside in enumerate(up_and_down(field)):
+                    at = pl.ds(8 * r, 8)
+                    start_ref[c, t, at] = field[r]
+                    rate = planes[n + TRACERS][r]
+                    part_ref[c, t, at] = field[r] + rate * (beside - 4.0 * field[r])
+
+    return pl.pallas_call(
+        body,
+        in_specs=[pl.BlockSpec(memory_space=pltpu.SMEM)]
+        + [pl.BlockSpec(memory_space=pltpu.VMEM)] * len(arrays),
+        out_specs=[pl.BlockSpec(memory_space=pltpu.VMEM)] * 2,
+        out_shape=[jax.ShapeDtypeStruct((TRACERS, TS_DEV, PAD_LAT, LON), F32)] * 2,
+        compiler_params=pltpu.CompilerParams(vmem_limit_bytes=8 * MIB),
+        cost_estimate=pl.CostEstimate(
+            flops=32 * MIB, bytes_accessed=4 * MIB, transcendentals=0
+        ),
+        name="begin",
+    )(taps, *arrays)
+
+
+def diffuse(started, static, left, right, taps):
+    n = TS_DEV + 2 * HB
+    last = PAD_LAT // 8 - 1
+
+    def body(taps_ref, start_ref, part_ref, st_ref, l_ref, r_ref, out_ref, side_ref, done_ref, sems):
+        for k in range(n + TRACERS + 1):
+            side_ref[k] = side_of(k, l_ref[...], r_ref[...])
+        sides = [strips_of(side_ref[k]) for k in range(n + TRACERS + 1)]
+        stores = [
+            pltpu.make_async_copy(done_ref.at[c], out_ref.at[c], sems.at[c])
+            for c in range(TRACERS)
+        ]
+
+        def wide(main, side):
+            return jnp.concatenate([main, side], axis=1)
+
+        def rate(r):
+            return wide(st_ref[TRACERS, 8 * r : 8 * r + 8], sides[n + TRACERS][r])
+
+        def along(f):
+            return pltpu.roll(f, 1, 1) + pltpu.roll(f, PAD_LON - 1, 1)
+
+        for c in range(TRACERS):
+            for t in range(TS_DEV):
+                side = band(c, t, taps_ref, sides, sides[n + c])
+                field = []
+                for r, beside in enumerate(up_and_down(side)):
+                    at = pl.ds(8 * r, 8)
+                    part = side[r] + sides[n + TRACERS][r] * (beside - 4.0 * side[r])
+                    both = along(wide(start_ref[c, t, at], side[r]))
+                    field.append(wide(part_ref[c, t, at], part) + rate(r) * both)
+                for step in range(1, KSTEPS):
+                    beside = up_and_down(field)
+                    stepped = list(field)
+                    end = step == KSTEPS - 1
+                    for r in range(end, last + 1 - end):
+                        total = along(field[r]) + beside[r]
+                        stepped[r] = field[r] + rate(r) * (total - 4.0 * field[r])
+                    field = stepped
+                for r in range(1, last):
+                    done_ref[c, t, 8 * r - 8 : 8 * r, :] = (
+                        st_ref[c, 8 * r : 8 * r + 8] * field[r][:, :LON]
+                    )
+            stores[c].start()
+        for store in stores:
+            store.wait()
+
+    operands = (*started, static, left, right)
+    return pl.pallas_call(
+        body,
+        in_specs=[pl.BlockSpec(memory_space=pltpu.SMEM)]
+        + [pl.BlockSpec(memory_space=pltpu.VMEM)] * len(operands),
+        out_specs=pl.BlockSpec(memory_space=pl.ANY),
         out_shape=jax.ShapeDtypeStruct((TRACERS, TS_DEV, LAT, LON), F32),
-        scratch_shapes=[pltpu.VMEM((n + TRACERS + 1, PAD_LAT, PAD_LON), F32)],
-        compiler_params=pltpu.CompilerParams(vmem_limit_bytes=20 * MIB),
+        scratch_shapes=[
+            pltpu.VMEM((n + TRACERS + 1, PAD_LAT, 128), F32),
+            pltpu.VMEM((TRACERS, TS_DEV, LAT, LON), F32),
+            pltpu.SemaphoreType.DMA((TRACERS,)),
+        ],
+        compiler_params=pltpu.CompilerParams(vmem_limit_bytes=12 * MIB),
         name="diffuse",
     )(taps, *operands)
 
@@ -370,7 +444,7 @@
     to_left, to_right = pack_lon(arrays, F32, "halo_lon")
     left = lax.ppermute(to_right, "gx", east)
     right = lax.ppermute(to_left, "gx", west)
-    return diffuse(arrays, left, right, taps)
+    return diffuse(begin(arrays, taps), static, left, right, taps)
 
 
 def solution(mesh):

time: 89.5 us -> 89.1 us (level)
  waiting for transfers between devices: 29.5 us -> 28.1 us
    ppermute x1, waiting for transfers between devices: 1.39 us -> 0.01 us  [per_device(): left = lax.ppermute(to_right, 'gx', east)]
    pallas_call x1 -> x2, Pallas kernels: 6.84 us -> 7.66 us  [the longest x1 6.24 us: diffuse(): pl.pallas_call(body, in_specs=[pl.BlockSpec(memory_space=pltpu.SMEM)] + [...]
  transfers between devices with their start and end apart: 14 -> 14, of which waited for: 5 -> 4; matrix products, arithmetic and copies ran while one was open for 0% -> 0% of each run, Pallas kernels for 2% -> 3%
where the time goes in v9:
time: 89.1 us; the launch traced here: 88.5 us
  starting transfers between devices  37.6 us (42%)
  waiting for transfers between devices  28.1 us (32%)
  Pallas kernels  22.4 us (25%)
    ppermute x1, waiting for transfers between devices, per_device(): up = lax.ppermute(to_down, 'gy', south)  15.3 us
    pallas_call x1, Pallas kernels, bin_sums(): pl.pallas_call(body, in_specs=[one] * 4 + [far], out_specs=[far] * (1 + N...  12.9 us
    all_to_all x2, starting transfers between devices, along_gx(): return lax.all_to_all(rows, 'gx', 0, 0, tiled=True)  10.8 us
    ppermute x6, starting transfers between devices, along_gy(): lax.ppermute(parts[k], 'gy', [(i, (i + k) % N_GY) for i in range(N_GY)])  8.18 us
    ppermute x1, starting transfers between devices, per_device(): before = lax.ppermute(high, 'ta', later)  7.74 us
    ppermute x1, waiting for transfers between devices, per_device(): after = lax.ppermute(low, 'ta', sooner)  6.77 us
    pallas_call x1, Pallas kernels, diffuse(): pl.pallas_call(body, in_specs=[pl.BlockSpec(memory_space=pltpu.SMEM)] + [...  6.24 us
    all_to_all x2, waiting for transfers between devices, along_gx(): return lax.all_to_all(rows, 'gx', 0, 0, tiled=True)  3.85 us
  transfers between devices with their start and end apart: 14, of which 4 were waited for; matrix products, arithmetic and copies ran while one was open for 0% of the time, Pallas kernels for 3%

profile of v9, /device:TPU:67, one launch (start us, length us, event | category | flops | bytes accessed | tf_op | source)
XLA Modules:
  0.0 88.5 jit_solution(17938855731386323091)
XLA Ops:
  0.0 12.9 %bin_sums.1 = (bf16[8,256,512]{2,1,0:T(8,128)(2,1)}, bf16[8,64,512]{2,1,0:T(8,128)(2,1)}, bf16[8,64,512]{2,1,0:T(8,128)(2,1)}, bf16[8,64,512]{2,1,0:T(8,128)(2,1)}, bf16[8,64,512]{2,1,0:T(8,128)(2,1)}) custom-call(s32[2048]{0:T(1024)} %bitcast.4, s32[2048]{0:T(1024)} %step_ref.1, s32[2048]{0:T(1024)} %block_ref.1, bf16[2048]{0:T(1024)(128)(2,1)} %res_ref.1, ...), custom_call_target="tpu_custom_call" | custom-call | flops 8589934592 | bytes 8388608 | tf_op jit(solution)/shard_map/bin_sums/pallas_call | solution.py:89
  12.9 0.0 copy-start
  12.9 0.0 copy-start.2
  12.9 0.0 copy-start.1
  12.9 5.7 %all-to-all-start = ((bf16[8,256,512]{2,1,0:T(8,128)(2,1)}), bf16[8,256,512]{2,1,0:T(8,128)(2,1)S(1)}, u32[]{:S(2)}, u32[]{:S(2)}) async-start(bf16[8,256,512]{2,1,0:T(8,128)(2,1)} %get-tuple-element.31), calls=%async_computation | async-start | bytes 4194304 | tf_op jit(solution)/shard_map/all_to_all | solution.py:418
  18.6 1.2 %collective-permute-start.3 = (bf16[8,64,512]{2,1,0:T(8,128)(2,1)}, bf16[8,64,512]{2,1,0:T(8,128)(2,1)S(1)}, u32[]{:S(2)}, u32[]{:S(2)}) collective-permute-start(bf16[8,64,512]{2,1,0:T(8,128)(2,1)} %get-tuple-element.37), channel_id=1, source_target_pairs={{0,8},{8,16},{16,24},{24,0},{1,9},{9,17},{17,25},{25,1},{2,10},{10... | collective-permute-start | bytes 1572872 | tf_op jit(solution)/shard_map/ppermute | solution.py:412
  19.8 0.8 collective-permute-start.4
  20.6 1.9 %collective-permute-start.5 = (bf16[8,64,512]{2,1,0:T(8,128)(2,1)S(1)}, bf16[8,64,512]{2,1,0:T(8,128)(2,1)S(1)}, u32[]{:S(2)}, u32[]{:S(2)}) collective-permute-start(bf16[8,64,512]{2,1,0:T(8,128)(2,1)S(1)} %copy-done.4), channel_id=1, source_target_pairs={{0,24},{8,0},{16,8},{24,16},{1,25},{9,1},{17,9},{25,17},{2,26},{10... | collective-permute-start | bytes 1572872 | tf_op jit(solution)/shard_map/ppermute | solution.py:412
  22.5 1.9 %collective-permute-start.6 = (f32[20,256]{1,0:T(8,128)S(1)}, f32[20,256]{1,0:T(8,128)S(1)}, u32[]{:S(2)}, u32[]{:S(2)}) collective-permute-start(f32[20,256]{1,0:T(8,128)S(1)} %get-tuple-element.42), channel_id=1, source_target_pairs={{0,8},{8,16},{16,24},{1,9},{9,17},{17,25},{2,10},{10,18},{18,26},{... | collective-permute-start | bytes 61448 | tf_op jit(solution)/shard_map/ppermute | solution.py:433
  24.5 3.4 %collective-permute-start.7 = (f32[20,256]{1,0:T(8,128)S(1)}, f32[20,256]{1,0:T(8,128)S(1)}, u32[]{:S(2)}, u32[]{:S(2)}) collective-permute-start(f32[20,256]{1,0:T(8,128)S(1)} %get-tuple-element.43), channel_id=1, source_target_pairs={{8,0},{16,8},{24,16},{9,1},{17,9},{25,17},{10,2},{18,10},{26,18},{... | collective-permute-start | bytes 61448 | tf_op jit(solution)/shard_map/ppermute | solution.py:434
  27.8 15.3 %collective-permute-done.6.refs_2_ = f32[20,256]{1,0:T(8,128)S(1)} collective-permute-done((f32[20,256]{1,0:T(8,128)S(1)}, f32[20,256]{1,0:T(8,128)S(1)}, u32[]{:S(2)}, u32[]{:S(2)}) %collective-permute-start.6) | collective-permute-done | bytes 20512 | tf_op jit(solution)/shard_map/ppermute | solution.py:433
  43.1 2.2 %collective-permute-done.7.refs_3_ = f32[20,256]{1,0:T(8,128)S(1)} collective-permute-done((f32[20,256]{1,0:T(8,128)S(1)}, f32[20,256]{1,0:T(8,128)S(1)}, u32[]{:S(2)}, u32[]{:S(2)}) %collective-permute-start.7) | collective-permute-done | bytes 20512 | tf_op jit(solution)/shard_map/ppermute | solution.py:434
  45.3 0.0 collective-permute-done.3.refs_1_
  45.3 0.0 collective-permute-done.4.refs_2_
  45.3 0.0 collective-permute-done.5.refs_3_
  45.3 1.1 %sum_arrays.1 = bf16[8,64,512]{2,1,0:T(8,128)(2,1)} custom-call(bf16[8,64,512]{2,1,0:T(8,128)(2,1)S(1)} %copy-done.1, bf16[8,64,512]{2,1,0:T(8,128)(2,1)S(1)} %collective-permute-done.3.refs_1_, bf16[8,64,512]{2,1,0:T(8,128)(2,1)S(1)} %collective-permute-done.4.refs_2_, bf16[8,64,512]{2,1,0:T(8,128)(2,1)S(1)} %collective-permute-done.5.refs_3_), custom_call_target="tpu_custom_call" | custom-call | tf_op jit(solution)/shard_map/sum_arrays/pallas_call | solution.py:145
  46.4 5.1 %all-to-all-start.1 = ((bf16[8,64,512]{2,1,0:T(8,128)(2,1)}), bf16[8,64,512]{2,1,0:T(8,128)(2,1)S(1)}, u32[]{:S(2)}, u32[]{:S(2)}) async-start(bf16[8,64,512]{2,1,0:T(8,128)(2,1)} %sum_arrays.1), calls=%async_computation.1 | async-start | bytes 1048576 | tf_op jit(solution)/shard_map/all_to_all | solution.py:418
  51.5 0.3 sum_first.1
  51.8 0.3 collective-permute-start
  52.1 2.0 %collective-permute-start.1 = (bf16[80,512]{1,0:T(8,128)(2,1)S(1)}, bf16[80,512]{1,0:T(8,128)(2,1)S(1)}, u32[]{:S(2)}, u32[]{:S(2)}) collective-permute-start(bf16[80,512]{1,0:T(8,128)(2,1)S(1)} %get-tuple-element.34), channel_id=1, source_target_pairs={{0,16},{8,24},{16,0},{24,8},{1,17},{9,25},{17,1},{25,9},{2,18},{10... | collective-permute-start | bytes 245768 | tf_op jit(solution)/shard_map/ppermute | solution.py:412
  54.1 2.0 %collective-permute-start.2 = (bf16[80,512]{1,0:T(8,128)(2,1)S(1)}, bf16[80,512]{1,0:T(8,128)(2,1)S(1)}, u32[]{:S(2)}, u32[]{:S(2)}) collective-permute-start(bf16[80,512]{1,0:T(8,128)(2,1)S(1)} %get-tuple-element.35), channel_id=1, source_target_pairs={{0,24},{8,0},{16,8},{24,16},{1,25},{9,1},{17,9},{25,17},{2,26},{10... | collective-permute-start | bytes 245768 | tf_op jit(solution)/shard_map/ppermute | solution.py:412
  56.1 3.9 %all-to-all-done.1.refs_4_ = bf16[8,64,512]{2,1,0:T(8,128)(2,1)S(1)} async-done(((bf16[8,64,512]{2,1,0:T(8,128)(2,1)}), bf16[8,64,512]{2,1,0:T(8,128)(2,1)S(1)}, u32[]{:S(2)}, u32[]{:S(2)}) %all-to-all-start.1) | async-done | bytes 524320 | tf_op jit(solution)/shard_map/all_to_all | solution.py:418
  59.9 0.3 tile_sum.1
  60.2 7.7 %collective-permute-start.8 = (bf16[2,80,256]{2,1,0:T(8,128)(2,1)S(1)}, bf16[2,80,256]{2,1,0:T(8,128)(2,1)S(1)}, u32[]{:S(2)}, u32[]{:S(2)}) collective-permute-start(bf16[2,80,256]{2,1,0:T(8,128)(2,1)S(1)} %get-tuple-element.48), channel_id=1, source_target_pairs={{0,32},{32,64},{64,96},{96,128},{128,160},{160,192},{192,224},{1,3... | collective-permute-start | bytes 245768 | tf_op jit(solution)/shard_map/ppermute | solution.py:441
  68.0 1.9 %collective-permute-start.9 = (bf16[2,80,256]{2,1,0:T(8,128)(2,1)S(1)}, bf16[2,80,256]{2,1,0:T(8,128)(2,1)S(1)}, u32[]{:S(2)}, u32[]{:S(2)}) collective-permute-start(bf16[2,80,256]{2,1,0:T(8,128)(2,1)S(1)} %get-tuple-element.50), channel_id=1, source_target_pairs={{32,0},{64,32},{96,64},{128,96},{160,128},{192,160},{224,192},{33,... | collective-permute-start | bytes 245768 | tf_op jit(solution)/shard_map/ppermute | solution.py:442
  69.9 0.0 collective-permute-done.8.refs_0_
  69.9 6.8 %collective-permute-done.9.refs_2_ = bf16[2,80,256]{2,1,0:T(8,128)(2,1)S(1)} collective-permute-done((bf16[2,80,256]{2,1,0:T(8,128)(2,1)S(1)}, bf16[2,80,256]{2,1,0:T(8,128)(2,1)S(1)}, u32[]{:S(2)}, u32[]{:S(2)}) %collective-permute-start.9) | collective-permute-done | bytes 81952 | tf_op jit(solution)/shard_map/ppermute | solution.py:442
  76.7 0.3 halo_lon.1
  77.0 0.3 collective-permute-start.10
  77.3 3.3 %collective-permute-start.11 = (f32[80,128]{1,0:T(8,128)S(1)}, f32[80,128]{1,0:T(8,128)S(1)}, u32[]{:S(2)}, u32[]{:S(2)}) collective-permute-start(f32[80,128]{1,0:T(8,128)S(1)} %get-tuple-element.56), channel_id=1, source_target_pairs={{1,0},{2,1},{3,2},{4,3},{5,4},{6,5},{7,6},{0,7},{9,8},{10,9},{11,1... | collective-permute-start | bytes 122888 | tf_op jit(solution)/shard_map/ppermute | solution.py:446
  80.7 1.4 %begin.1 = (f32[4,4,80,256]{3,2,1,0:T(8,128)S(1)}, f32[4,4,80,256]{3,2,1,0:T(8,128)S(1)}) custom-call(f32[4,5]{1,0:T(4,128)S(1)} %copy-done.3, bf16[2,80,256]{2,1,0:T(8,128)(2,1)S(1)} %collective-permute-done.8.refs_0_, f32[4,80,256]{2,1,0:T(8,128)S(1)} %get-tuple-element.49.refs_1_, bf16[2,80,256]{2,1,0:T(8,128)(2,1)S(1)} %collective-permute-done.9.refs_2_, ...), custom_call_target="tpu_custom_call" | custom-call | flops 33554432 | bytes 4194304 | tf_op jit(solution)/shard_map/begin/pallas_call | solution.py:324
  82.1 6.2 %diffuse.1 = f32[4,4,64,256]{3,2,1,0:T(8,128)} custom-call(f32[4,5]{1,0:T(4,128)S(1)} %copy-done.3, f32[4,4,80,256]{3,2,1,0:T(8,128)S(1)} %get-tuple-element.53.start_ref, f32[4,4,80,256]{3,2,1,0:T(8,128)S(1)} %get-tuple-element.54.part_ref, f32[5,80,256]{2,1,0:T(8,128)S(1)} %static_planes.1.refs_3_.st_ref, f32[80,128]{1,0:T(8,128)S(1)} %collective-permute-done.10.l_ref, ...), custom_call_target="tpu_custom_call" | custom-call | tf_op jit(solution)/shard_map/diffuse/pallas_call | solution.py:386
  (15 shorter events, 0.1 us)
Async XLA Ops:
  12.9 7.8 %copy-start.4 = (bf16[8,64,512]{2,1,0:T(8,128)(2,1)S(1)}, bf16[8,64,512]{2,1,0:T(8,128)(2,1)}, u32[]{:S(2)}) copy-start(bf16[8,64,512]{2,1,0:T(8,128)(2,1)} %get-tuple-element.39) | copy-start | bytes 1572868
  12.9 9.6 %copy-start = (f32[4,64,256]{2,1,0:T(8,128)S(1)}, f32[4,64,256]{2,1,0:T(8,128)}, u32[]{:S(2)}) copy-start(f32[4,64,256]{2,1,0:T(8,128)} %refs_0_.1) | copy-start | bytes 786436
  12.9 9.6 %copy-start.2 = (f32[64,256]{1,0:T(8,128)S(1)}, f32[64,256]{1,0:T(8,128)}, u32[]{:S(2)}) copy-start(f32[64,256]{1,0:T(8,128)} %param.15) | copy-start | bytes 196612
  12.9 32.4 %copy-start.1 = (bf16[8,64,512]{2,1,0:T(8,128)(2,1)S(1)}, bf16[8,64,512]{2,1,0:T(8,128)(2,1)}, u32[]{:S(2)}) copy-start(bf16[8,64,512]{2,1,0:T(8,128)(2,1)} %get-tuple-element.44.refs_0_) | copy-start | bytes 1572868
  12.9 33.5 %all-to-all-start = ((bf16[8,256,512]{2,1,0:T(8,128)(2,1)}), bf16[8,256,512]{2,1,0:T(8,128)(2,1)S(1)}, u32[]{:S(2)}, u32[]{:S(2)}) async-start(bf16[8,256,512]{2,1,0:T(8,128)(2,1)} %get-tuple-element.31), calls=%async_computation | async-start | bytes 4194304 | tf_op jit(solution)/shard_map/all_to_all | solution.py:418
  18.6 26.7 %collective-permute-start.3 = (bf16[8,64,512]{2,1,0:T(8,128)(2,1)}, bf16[8,64,512]{2,1,0:T(8,128)(2,1)S(1)}, u32[]{:S(2)}, u32[]{:S(2)}) collective-permute-start(bf16[8,64,512]{2,1,0:T(8,128)(2,1)} %get-tuple-element.37), channel_id=1, source_target_pairs={{0,8},{8,16},{16,24},{24,0},{1,9},{9,17},{17,25},{25,1},{2,10},{10... | collective-permute-start | bytes 1572872 | tf_op jit(solution)/shard_map/ppermute | solution.py:412
  19.8 25.5 %collective-permute-start.4 = (bf16[8,64,512]{2,1,0:T(8,128)(2,1)}, bf16[8,64,512]{2,1,0:T(8,128)(2,1)S(1)}, u32[]{:S(2)}, u32[]{:S(2)}) collective-permute-start(bf16[8,64,512]{2,1,0:T(8,128)(2,1)} %get-tuple-element.38), channel_id=1, source_target_pairs={{0,16},{8,24},{16,0},{24,8},{1,17},{9,25},{17,1},{25,9},{2,18},{10... | collective-permute-start | bytes 1572872 | tf_op jit(solution)/shard_map/ppermute | solution.py:412
  20.6 24.7 %collective-permute-start.5 = (bf16[8,64,512]{2,1,0:T(8,128)(2,1)S(1)}, bf16[8,64,512]{2,1,0:T(8,128)(2,1)S(1)}, u32[]{:S(2)}, u32[]{:S(2)}) collective-permute-start(bf16[8,64,512]{2,1,0:T(8,128)(2,1)S(1)} %copy-done.4), channel_id=1, source_target_pairs={{0,24},{8,0},{16,8},{24,16},{1,25},{9,1},{17,9},{25,17},{2,26},{10... | collective-permute-start | bytes 1572872 | tf_op jit(solution)/shard_map/ppermute | solution.py:412
  22.5 20.6 %collective-permute-start.6 = (f32[20,256]{1,0:T(8,128)S(1)}, f32[20,256]{1,0:T(8,128)S(1)}, u32[]{:S(2)}, u32[]{:S(2)}) collective-permute-start(f32[20,256]{1,0:T(8,128)S(1)} %get-tuple-element.42), channel_id=1, source_target_pairs={{0,8},{8,16},{16,24},{1,9},{9,17},{17,25},{2,10},{10,18},{18,26},{... | collective-permute-start | bytes 61448 | tf_op jit(solution)/shard_map/ppermute | solution.py:433
  24.5 20.8 %collective-permute-start.7 = (f32[20,256]{1,0:T(8,128)S(1)}, f32[20,256]{1,0:T(8,128)S(1)}, u32[]{:S(2)}, u32[]{:S(2)}) collective-permute-start(f32[20,256]{1,0:T(8,128)S(1)} %get-tuple-element.43), channel_id=1, source_target_pairs={{8,0},{16,8},{24,16},{9,1},{17,9},{25,17},{10,2},{18,10},{26,18},{... | collective-permute-start | bytes 61448 | tf_op jit(solution)/shard_map/ppermute | solution.py:434
  46.4 13.5 %all-to-all-start.1 = ((bf16[8,64,512]{2,1,0:T(8,128)(2,1)}), bf16[8,64,512]{2,1,0:T(8,128)(2,1)S(1)}, u32[]{:S(2)}, u32[]{:S(2)}) async-start(bf16[8,64,512]{2,1,0:T(8,128)(2,1)} %sum_arrays.1), calls=%async_computation.1 | async-start | bytes 1048576 | tf_op jit(solution)/shard_map/all_to_all | solution.py:418
  51.5 29.1 %copy-start.3 = (f32[4,5]{1,0:T(4,128)S(1)}, f32[4,5]{1,0:T(4,128)}, u32[]{:S(2)}) copy-start(f32[4,5]{1,0:T(4,128)} %taps_ref.3) | copy-start | bytes 244
  51.8 8.1 %collective-permute-start = (bf16[80,512]{1,0:T(8,128)(2,1)S(1)}, bf16[80,512]{1,0:T(8,128)(2,1)S(1)}, u32[]{:S(2)}, u32[]{:S(2)}) collective-permute-start(bf16[80,512]{1,0:T(8,128)(2,1)S(1)} %get-tuple-element.33), channel_id=1, source_target_pairs={{0,8},{8,16},{16,24},{24,0},{1,9},{9,17},{17,25},{25,1},{2,10},{10... | collective-permute-start | bytes 245768 | tf_op jit(solution)/shard_map/ppermute | solution.py:412
  52.1 7.8 %collective-permute-start.1 = (bf16[80,512]{1,0:T(8,128)(2,1)S(1)}, bf16[80,512]{1,0:T(8,128)(2,1)S(1)}, u32[]{:S(2)}, u32[]{:S(2)}) collective-permute-start(bf16[80,512]{1,0:T(8,128)(2,1)S(1)} %get-tuple-element.34), channel_id=1, source_target_pairs={{0,16},{8,24},{16,0},{24,8},{1,17},{9,25},{17,1},{25,9},{2,18},{10... | collective-permute-start | bytes 245768 | tf_op jit(solution)/shard_map/ppermute | solution.py:412
  54.1 5.8 %collective-permute-start.2 = (bf16[80,512]{1,0:T(8,128)(2,1)S(1)}, bf16[80,512]{1,0:T(8,128)(2,1)S(1)}, u32[]{:S(2)}, u32[]{:S(2)}) collective-permute-start(bf16[80,512]{1,0:T(8,128)(2,1)S(1)} %get-tuple-element.35), channel_id=1, source_target_pairs={{0,24},{8,0},{16,8},{24,16},{1,25},{9,1},{17,9},{25,17},{2,26},{10... | collective-permute-start | bytes 245768 | tf_op jit(solution)/shard_map/ppermute | solution.py:412
  60.2 9.7 %collective-permute-start.8 = (bf16[2,80,256]{2,1,0:T(8,128)(2,1)S(1)}, bf16[2,80,256]{2,1,0:T(8,128)(2,1)S(1)}, u32[]{:S(2)}, u32[]{:S(2)}) collective-permute-start(bf16[2,80,256]{2,1,0:T(8,128)(2,1)S(1)} %get-tuple-element.48), channel_id=1, source_target_pairs={{0,32},{32,64},{64,96},{96,128},{128,160},{160,192},{192,224},{1,3... | collective-permute-start | bytes 245768 | tf_op jit(solution)/shard_map/ppermute | solution.py:441
  68.0 8.7 %collective-permute-start.9 = (bf16[2,80,256]{2,1,0:T(8,128)(2,1)S(1)}, bf16[2,80,256]{2,1,0:T(8,128)(2,1)S(1)}, u32[]{:S(2)}, u32[]{:S(2)}) collective-permute-start(bf16[2,80,256]{2,1,0:T(8,128)(2,1)S(1)} %get-tuple-element.50), channel_id=1, source_target_pairs={{32,0},{64,32},{96,64},{128,96},{160,128},{192,160},{224,192},{33,... | collective-permute-start | bytes 245768 | tf_op jit(solution)/shard_map/ppermute | solution.py:442
  77.0 5.1 %collective-permute-start.10 = (f32[80,128]{1,0:T(8,128)S(1)}, f32[80,128]{1,0:T(8,128)S(1)}, u32[]{:S(2)}, u32[]{:S(2)}) collective-permute-start(f32[80,128]{1,0:T(8,128)S(1)} %get-tuple-element.55), channel_id=1, source_target_pairs={{0,1},{1,2},{2,3},{3,4},{4,5},{5,6},{6,7},{7,0},{8,9},{9,10},{10,1... | collective-permute-start | bytes 122888 | tf_op jit(solution)/shard_map/ppermute | solution.py:445
  77.3 4.8 %collective-permute-start.11 = (f32[80,128]{1,0:T(8,128)S(1)}, f32[80,128]{1,0:T(8,128)S(1)}, u32[]{:S(2)}, u32[]{:S(2)}) collective-permute-start(f32[80,128]{1,0:T(8,128)S(1)} %get-tuple-element.56), channel_id=1, source_target_pairs={{1,0},{2,1},{3,2},{4,3},{5,4},{6,5},{7,6},{0,7},{9,8},{10,9},{11,1... | collective-permute-start | bytes 122888 | tf_op jit(solution)/shard_map/ppermute | solution.py:446

commit v10 on v9

--- a/solution.py
+++ b/solution.py
@@ -408,10 +408,11 @@
 
 
 def along_gy(parts):
-    return [parts[0]] + [
-        lax.ppermute(parts[k], "gy", [(i, (i + k) % N_GY) for i in range(N_GY)])
-        for k in range(1, N_GY)
-    ]
+    came = [parts[0]]
+    for k in (2, 1, 3):
+        ring = [(i, (i + k) % N_GY) for i in range(N_GY)]
+        came.append(lax.ppermute(parts[k], "gy", ring))
+    return came
 
 
 def along_gx(rows):

time: 89.1 us -> 89.5 us (level)
  waiting for transfers between devices: 28.1 us -> 31.4 us
  starting transfers between devices: 37.6 us -> 35 us
    all_to_all x2, waiting for transfers between devices: 3.85 us -> 6.15 us  [along_gx(): return lax.all_to_all(rows, 'gx', 0, 0, tiled=True)]
    ppermute x6, starting transfers between devices: 8.18 us -> 6.16 us  [along_gy(): came.append(lax.ppermute(parts[k], 'gy', ring))]
    ppermute x1, waiting for transfers between devices: 15.3 us -> 17.2 us  [per_device(): up = lax.ppermute(to_down, 'gy', south)]
    ppermute x1, waiting for transfers between devices: 2.21 us -> 1.25 us  [per_device(): down = lax.ppermute(to_up, 'gy', north)]
where the time goes in v10:
time: 89.5 us; the launch traced here: 89.1 us
  starting transfers between devices  35 us (39%)
  waiting for transfers between devices  31.4 us (35%)
  Pallas kernels  22.4 us (25%)
    ppermute x1, waiting for transfers between devices, per_device(): up = lax.ppermute(to_down, 'gy', south)  17.2 us
    pallas_call x1, Pallas kernels, bin_sums(): pl.pallas_call(body, in_specs=[one] * 4 + [far], out_specs=[far] * (1 + N...  12.9 us
    all_to_all x2, starting transfers between devices, along_gx(): return lax.all_to_all(rows, 'gx', 0, 0, tiled=True)  10.8 us
    ppermute x1, starting transfers between devices, per_device(): before = lax.ppermute(high, 'ta', later)  6.86 us
    ppermute x1, waiting for transfers between devices, per_device(): after = lax.ppermute(low, 'ta', sooner)  6.77 us
    pallas_call x1, Pallas kernels, diffuse(): pl.pallas_call(body, in_specs=[pl.BlockSpec(memory_space=pltpu.SMEM)] + [...  6.24 us
    ppermute x6, starting transfers between devices, along_gy(): came.append(lax.ppermute(parts[k], 'gy', ring))  6.16 us
    all_to_all x2, waiting for transfers between devices, along_gx(): return lax.all_to_all(rows, 'gx', 0, 0, tiled=True)  6.15 us
  transfers between devices with their start and end apart: 14, of which 4 were waited for; matrix products, arithmetic and copies ran while one was open for 0% of the time, Pallas kernels for 3%

profile of v10, /device:TPU:67, one launch (start us, length us, event | category | flops | bytes accessed | tf_op | source)
XLA Modules:
  0.0 89.1 jit_solution(11983032736173404507)
XLA Ops:
  0.0 12.9 %bin_sums.1 = (bf16[8,256,512]{2,1,0:T(8,128)(2,1)}, bf16[8,64,512]{2,1,0:T(8,128)(2,1)}, bf16[8,64,512]{2,1,0:T(8,128)(2,1)}, bf16[8,64,512]{2,1,0:T(8,128)(2,1)}, bf16[8,64,512]{2,1,0:T(8,128)(2,1)}) custom-call(s32[2048]{0:T(1024)} %bitcast.4, s32[2048]{0:T(1024)} %step_ref.1, s32[2048]{0:T(1024)} %block_ref.1, bf16[2048]{0:T(1024)(128)(2,1)} %res_ref.1, ...), custom_call_target="tpu_custom_call" | custom-call | flops 8589934592 | bytes 8388608 | tf_op jit(solution)/shard_map/bin_sums/pallas_call | solution.py:89
  12.9 0.0 copy-start
  12.9 0.0 copy-start.2
  12.9 0.0 copy-start.1
  12.9 5.7 %all-to-all-start = ((bf16[8,256,512]{2,1,0:T(8,128)(2,1)}), bf16[8,256,512]{2,1,0:T(8,128)(2,1)S(1)}, u32[]{:S(2)}, u32[]{:S(2)}) async-start(bf16[8,256,512]{2,1,0:T(8,128)(2,1)} %get-tuple-element.31), calls=%async_computation | async-start | bytes 4194304 | tf_op jit(solution)/shard_map/all_to_all | solution.py:419
  18.6 1.8 %collective-permute-start.3 = (bf16[8,64,512]{2,1,0:T(8,128)(2,1)}, bf16[8,64,512]{2,1,0:T(8,128)(2,1)S(1)}, u32[]{:S(2)}, u32[]{:S(2)}) collective-permute-start(bf16[8,64,512]{2,1,0:T(8,128)(2,1)} %get-tuple-element.37), channel_id=1, source_target_pairs={{0,16},{8,24},{16,0},{24,8},{1,17},{9,25},{17,1},{25,9},{2,18},{10... | collective-permute-start | bytes 1572872 | tf_op jit(solution)/shard_map/ppermute | solution.py:414
  20.4 0.0 collective-permute-start.4
  20.5 1.5 %collective-permute-start.5 = (bf16[8,64,512]{2,1,0:T(8,128)(2,1)S(1)}, bf16[8,64,512]{2,1,0:T(8,128)(2,1)S(1)}, u32[]{:S(2)}, u32[]{:S(2)}) collective-permute-start(bf16[8,64,512]{2,1,0:T(8,128)(2,1)S(1)} %copy-done.4), channel_id=1, source_target_pairs={{0,24},{8,0},{16,8},{24,16},{1,25},{9,1},{17,9},{25,17},{2,26},{10... | collective-permute-start | bytes 1572872 | tf_op jit(solution)/shard_map/ppermute | solution.py:414
  21.9 1.9 %collective-permute-start.6 = (f32[20,256]{1,0:T(8,128)S(1)}, f32[20,256]{1,0:T(8,128)S(1)}, u32[]{:S(2)}, u32[]{:S(2)}) collective-permute-start(f32[20,256]{1,0:T(8,128)S(1)} %get-tuple-element.42), channel_id=1, source_target_pairs={{0,8},{8,16},{16,24},{1,9},{9,17},{17,25},{2,10},{10,18},{18,26},{... | collective-permute-start | bytes 61448 | tf_op jit(solution)/shard_map/ppermute | solution.py:434
  23.9 3.6 %collective-permute-start.7 = (f32[20,256]{1,0:T(8,128)S(1)}, f32[20,256]{1,0:T(8,128)S(1)}, u32[]{:S(2)}, u32[]{:S(2)}) collective-permute-start(f32[20,256]{1,0:T(8,128)S(1)} %get-tuple-element.43), channel_id=1, source_target_pairs={{8,0},{16,8},{24,16},{9,1},{17,9},{25,17},{10,2},{18,10},{26,18},{... | collective-permute-start | bytes 61448 | tf_op jit(solution)/shard_map/ppermute | solution.py:435
  27.5 17.2 %collective-permute-done.6.refs_2_ = f32[20,256]{1,0:T(8,128)S(1)} collective-permute-done((f32[20,256]{1,0:T(8,128)S(1)}, f32[20,256]{1,0:T(8,128)S(1)}, u32[]{:S(2)}, u32[]{:S(2)}) %collective-permute-start.6) | collective-permute-done | bytes 20512 | tf_op jit(solution)/shard_map/ppermute | solution.py:434
  44.7 1.3 %collective-permute-done.7.refs_3_ = f32[20,256]{1,0:T(8,128)S(1)} collective-permute-done((f32[20,256]{1,0:T(8,128)S(1)}, f32[20,256]{1,0:T(8,128)S(1)}, u32[]{:S(2)}, u32[]{:S(2)}) %collective-permute-start.7) | collective-permute-done | bytes 20512 | tf_op jit(solution)/shard_map/ppermute | solution.py:435
  45.9 1.1 %sum_arrays.1 = bf16[8,64,512]{2,1,0:T(8,128)(2,1)} custom-call(bf16[8,64,512]{2,1,0:T(8,128)(2,1)S(1)} %copy-done.1, bf16[8,64,512]{2,1,0:T(8,128)(2,1)S(1)} %collective-permute-done.3.refs_1_, bf16[8,64,512]{2,1,0:T(8,128)(2,1)S(1)} %collective-permute-done.4.refs_2_, bf16[8,64,512]{2,1,0:T(8,128)(2,1)S(1)} %collective-permute-done.5.refs_3_), custom_call_target="tpu_custom_call" | custom-call | tf_op jit(solution)/shard_map/sum_arrays/pallas_call | solution.py:145
  47.0 0.0 all-to-all-done.got_ref
  47.0 5.1 %all-to-all-start.1 = ((bf16[8,64,512]{2,1,0:T(8,128)(2,1)}), bf16[8,64,512]{2,1,0:T(8,128)(2,1)S(1)}, u32[]{:S(2)}, u32[]{:S(2)}) async-start(bf16[8,64,512]{2,1,0:T(8,128)(2,1)} %sum_arrays.1), calls=%async_computation.1 | async-start | bytes 1048576 | tf_op jit(solution)/shard_map/all_to_all | solution.py:419
  52.1 0.3 sum_first.1
  52.4 1.4 %collective-permute-start = (bf16[80,512]{1,0:T(8,128)(2,1)S(1)}, bf16[80,512]{1,0:T(8,128)(2,1)S(1)}, u32[]{:S(2)}, u32[]{:S(2)}) collective-permute-start(bf16[80,512]{1,0:T(8,128)(2,1)S(1)} %get-tuple-element.33), channel_id=1, source_target_pairs={{0,16},{8,24},{16,0},{24,8},{1,17},{9,25},{17,1},{25,9},{2,18},{10... | collective-permute-start | bytes 245768 | tf_op jit(solution)/shard_map/ppermute | solution.py:414
  53.8 0.0 collective-permute-start.1
  53.8 1.5 %collective-permute-start.2 = (bf16[80,512]{1,0:T(8,128)(2,1)S(1)}, bf16[80,512]{1,0:T(8,128)(2,1)S(1)}, u32[]{:S(2)}, u32[]{:S(2)}) collective-permute-start(bf16[80,512]{1,0:T(8,128)(2,1)S(1)} %get-tuple-element.35), channel_id=1, source_target_pairs={{0,24},{8,0},{16,8},{24,16},{1,25},{9,1},{17,9},{25,17},{2,26},{10... | collective-permute-start | bytes 245768 | tf_op jit(solution)/shard_map/ppermute | solution.py:414
  55.3 6.1 %all-to-all-done.1.refs_4_ = bf16[8,64,512]{2,1,0:T(8,128)(2,1)S(1)} async-done(((bf16[8,64,512]{2,1,0:T(8,128)(2,1)}), bf16[8,64,512]{2,1,0:T(8,128)(2,1)S(1)}, u32[]{:S(2)}, u32[]{:S(2)}) %all-to-all-start.1) | async-done | bytes 524320 | tf_op jit(solution)/shard_map/all_to_all | solution.py:419
  61.4 0.0 collective-permute-done.refs_1_
  61.4 0.0 collective-permute-done.1.refs_2_
  61.4 0.0 collective-permute-done.2.refs_3_
  61.4 0.3 tile_sum.1
  61.7 6.9 %collective-permute-start.8 = (bf16[2,80,256]{2,1,0:T(8,128)(2,1)S(1)}, bf16[2,80,256]{2,1,0:T(8,128)(2,1)S(1)}, u32[]{:S(2)}, u32[]{:S(2)}) collective-permute-start(bf16[2,80,256]{2,1,0:T(8,128)(2,1)S(1)} %get-tuple-element.48), channel_id=1, source_target_pairs={{0,32},{32,64},{64,96},{96,128},{128,160},{160,192},{192,224},{1,3... | collective-permute-start | bytes 245768 | tf_op jit(solution)/shard_map/ppermute | solution.py:442
  68.6 1.9 %collective-permute-start.9 = (bf16[2,80,256]{2,1,0:T(8,128)(2,1)S(1)}, bf16[2,80,256]{2,1,0:T(8,128)(2,1)S(1)}, u32[]{:S(2)}, u32[]{:S(2)}) collective-permute-start(bf16[2,80,256]{2,1,0:T(8,128)(2,1)S(1)} %get-tuple-element.50), channel_id=1, source_target_pairs={{32,0},{64,32},{96,64},{128,96},{160,128},{192,160},{224,192},{33,... | collective-permute-start | bytes 245768 | tf_op jit(solution)/shard_map/ppermute | solution.py:443
  70.5 6.8 %collective-permute-done.9.refs_2_ = bf16[2,80,256]{2,1,0:T(8,128)(2,1)S(1)} collective-permute-done((bf16[2,80,256]{2,1,0:T(8,128)(2,1)S(1)}, bf16[2,80,256]{2,1,0:T(8,128)(2,1)S(1)}, u32[]{:S(2)}, u32[]{:S(2)}) %collective-permute-start.9) | collective-permute-done | bytes 81952 | tf_op jit(solution)/shard_map/ppermute | solution.py:443
  77.3 0.3 halo_lon.1
  77.6 0.2 collective-permute-start.10
  77.8 3.4 %collective-permute-start.11 = (f32[80,128]{1,0:T(8,128)S(1)}, f32[80,128]{1,0:T(8,128)S(1)}, u32[]{:S(2)}, u32[]{:S(2)}) collective-permute-start(f32[80,128]{1,0:T(8,128)S(1)} %get-tuple-element.56), channel_id=1, source_target_pairs={{1,0},{2,1},{3,2},{4,3},{5,4},{6,5},{7,6},{0,7},{9,8},{10,9},{11,1... | collective-permute-start | bytes 122888 | tf_op jit(solution)/shard_map/ppermute | solution.py:447
  81.3 1.4 %begin.1 = (f32[4,4,80,256]{3,2,1,0:T(8,128)S(1)}, f32[4,4,80,256]{3,2,1,0:T(8,128)S(1)}) custom-call(f32[4,5]{1,0:T(4,128)S(1)} %copy-done.3, bf16[2,80,256]{2,1,0:T(8,128)(2,1)S(1)} %collective-permute-done.8.refs_0_, f32[4,80,256]{2,1,0:T(8,128)S(1)} %get-tuple-element.49.refs_1_, bf16[2,80,256]{2,1,0:T(8,128)(2,1)S(1)} %collective-permute-done.9.refs_2_, ...), custom_call_target="tpu_custom_call" | custom-call | flops 33554432 | bytes 4194304 | tf_op jit(solution)/shard_map/begin/pallas_call | solution.py:324
  82.7 6.2 %diffuse.1 = f32[4,4,64,256]{3,2,1,0:T(8,128)} custom-call(f32[4,5]{1,0:T(4,128)S(1)} %copy-done.3, f32[4,4,80,256]{3,2,1,0:T(8,128)S(1)} %get-tuple-element.53.start_ref, f32[4,4,80,256]{3,2,1,0:T(8,128)S(1)} %get-tuple-element.54.part_ref, f32[5,80,256]{2,1,0:T(8,128)S(1)} %static_planes.1.refs_3_.st_ref, f32[80,128]{1,0:T(8,128)S(1)} %collective-permute-done.10.l_ref, ...), custom_call_target="tpu_custom_call" | custom-call | tf_op jit(solution)/shard_map/diffuse/pallas_call | solution.py:386
  (15 shorter events, 0.1 us)
Async XLA Ops:
  12.9 7.6 %copy-start.4 = (bf16[8,64,512]{2,1,0:T(8,128)(2,1)S(1)}, bf16[8,64,512]{2,1,0:T(8,128)(2,1)}, u32[]{:S(2)}) copy-start(bf16[8,64,512]{2,1,0:T(8,128)(2,1)} %get-tuple-element.39) | copy-start | bytes 1572868
  12.9 9.0 %copy-start = (f32[4,64,256]{2,1,0:T(8,128)S(1)}, f32[4,64,256]{2,1,0:T(8,128)}, u32[]{:S(2)}) copy-start(f32[4,64,256]{2,1,0:T(8,128)} %refs_0_.1) | copy-start | bytes 786436
  12.9 9.0 %copy-start.2 = (f32[64,256]{1,0:T(8,128)S(1)}, f32[64,256]{1,0:T(8,128)}, u32[]{:S(2)}) copy-start(f32[64,256]{1,0:T(8,128)} %param.15) | copy-start | bytes 196612
  12.9 33.0 %copy-start.1 = (bf16[8,64,512]{2,1,0:T(8,128)(2,1)S(1)}, bf16[8,64,512]{2,1,0:T(8,128)(2,1)}, u32[]{:S(2)}) copy-start(bf16[8,64,512]{2,1,0:T(8,128)(2,1)} %get-tuple-element.44.refs_0_) | copy-start | bytes 1572868
  12.9 34.1 %all-to-all-start = ((bf16[8,256,512]{2,1,0:T(8,128)(2,1)}), bf16[8,256,512]{2,1,0:T(8,128)(2,1)S(1)}, u32[]{:S(2)}, u32[]{:S(2)}) async-start(bf16[8,256,512]{2,1,0:T(8,128)(2,1)} %get-tuple-element.31), calls=%async_computation | async-start | bytes 4194304 | tf_op jit(solution)/shard_map/all_to_all | solution.py:419
  18.6 27.3 %collective-permute-start.3 = (bf16[8,64,512]{2,1,0:T(8,128)(2,1)}, bf16[8,64,512]{2,1,0:T(8,128)(2,1)S(1)}, u32[]{:S(2)}, u32[]{:S(2)}) collective-permute-start(bf16[8,64,512]{2,1,0:T(8,128)(2,1)} %get-tuple-element.37), channel_id=1, source_target_pairs={{0,16},{8,24},{16,0},{24,8},{1,17},{9,25},{17,1},{25,9},{2,18},{10... | collective-permute-start | bytes 1572872 | tf_op jit(solution)/shard_map/ppermute | solution.py:414
  20.4 25.5 %collective-permute-start.4 = (bf16[8,64,512]{2,1,0:T(8,128)(2,1)}, bf16[8,64,512]{2,1,0:T(8,128)(2,1)S(1)}, u32[]{:S(2)}, u32[]{:S(2)}) collective-permute-start(bf16[8,64,512]{2,1,0:T(8,128)(2,1)} %get-tuple-element.38), channel_id=1, source_target_pairs={{0,8},{8,16},{16,24},{24,0},{1,9},{9,17},{17,25},{25,1},{2,10},{10... | collective-permute-start | bytes 1572872 | tf_op jit(solution)/shard_map/ppermute | solution.py:414
  20.5 25.5 %collective-permute-start.5 = (bf16[8,64,512]{2,1,0:T(8,128)(2,1)S(1)}, bf16[8,64,512]{2,1,0:T(8,128)(2,1)S(1)}, u32[]{:S(2)}, u32[]{:S(2)}) collective-permute-start(bf16[8,64,512]{2,1,0:T(8,128)(2,1)S(1)} %copy-done.4), channel_id=1, source_target_pairs={{0,24},{8,0},{16,8},{24,16},{1,25},{9,1},{17,9},{25,17},{2,26},{10... | collective-permute-start | bytes 1572872 | tf_op jit(solution)/shard_map/ppermute | solution.py:414
  21.9 22.7 %collective-permute-start.6 = (f32[20,256]{1,0:T(8,128)S(1)}, f32[20,256]{1,0:T(8,128)S(1)}, u32[]{:S(2)}, u32[]{:S(2)}) collective-permute-start(f32[20,256]{1,0:T(8,128)S(1)} %get-tuple-element.42), channel_id=1, source_target_pairs={{0,8},{8,16},{16,24},{1,9},{9,17},{17,25},{2,10},{10,18},{18,26},{... | collective-permute-start | bytes 61448 | tf_op jit(solution)/shard_map/ppermute | solution.py:434
  23.9 22.1 %collective-permute-start.7 = (f32[20,256]{1,0:T(8,128)S(1)}, f32[20,256]{1,0:T(8,128)S(1)}, u32[]{:S(2)}, u32[]{:S(2)}) collective-permute-start(f32[20,256]{1,0:T(8,128)S(1)} %get-tuple-element.43), channel_id=1, source_target_pairs={{8,0},{16,8},{24,16},{9,1},{17,9},{25,17},{10,2},{18,10},{26,18},{... | collective-permute-start | bytes 61448 | tf_op jit(solution)/shard_map/ppermute | solution.py:435
  47.0 14.4 %all-to-all-start.1 = ((bf16[8,64,512]{2,1,0:T(8,128)(2,1)}), bf16[8,64,512]{2,1,0:T(8,128)(2,1)S(1)}, u32[]{:S(2)}, u32[]{:S(2)}) async-start(bf16[8,64,512]{2,1,0:T(8,128)(2,1)} %sum_arrays.1), calls=%async_computation.1 | async-start | bytes 1048576 | tf_op jit(solution)/shard_map/all_to_all | solution.py:419
  52.1 29.1 %copy-start.3 = (f32[4,5]{1,0:T(4,128)S(1)}, f32[4,5]{1,0:T(4,128)}, u32[]{:S(2)}) copy-start(f32[4,5]{1,0:T(4,128)} %taps_ref.3) | copy-start | bytes 244
  52.4 9.0 %collective-permute-start = (bf16[80,512]{1,0:T(8,128)(2,1)S(1)}, bf16[80,512]{1,0:T(8,128)(2,1)S(1)}, u32[]{:S(2)}, u32[]{:S(2)}) collective-permute-start(bf16[80,512]{1,0:T(8,128)(2,1)S(1)} %get-tuple-element.33), channel_id=1, source_target_pairs={{0,16},{8,24},{16,0},{24,8},{1,17},{9,25},{17,1},{25,9},{2,18},{10... | collective-permute-start | bytes 245768 | tf_op jit(solution)/shard_map/ppermute | solution.py:414
  53.8 7.6 %collective-permute-start.1 = (bf16[80,512]{1,0:T(8,128)(2,1)S(1)}, bf16[80,512]{1,0:T(8,128)(2,1)S(1)}, u32[]{:S(2)}, u32[]{:S(2)}) collective-permute-start(bf16[80,512]{1,0:T(8,128)(2,1)S(1)} %get-tuple-element.34), channel_id=1, source_target_pairs={{0,8},{8,16},{16,24},{24,0},{1,9},{9,17},{17,25},{25,1},{2,10},{10... | collective-permute-start | bytes 245768 | tf_op jit(solution)/shard_map/ppermute | solution.py:414
  53.8 7.6 %collective-permute-start.2 = (bf16[80,512]{1,0:T(8,128)(2,1)S(1)}, bf16[80,512]{1,0:T(8,128)(2,1)S(1)}, u32[]{:S(2)}, u32[]{:S(2)}) collective-permute-start(bf16[80,512]{1,0:T(8,128)(2,1)S(1)} %get-tuple-element.35), channel_id=1, source_target_pairs={{0,24},{8,0},{16,8},{24,16},{1,25},{9,1},{17,9},{25,17},{2,26},{10... | collective-permute-start | bytes 245768 | tf_op jit(solution)/shard_map/ppermute | solution.py:414
  61.7 8.8 %collective-permute-start.8 = (bf16[2,80,256]{2,1,0:T(8,128)(2,1)S(1)}, bf16[2,80,256]{2,1,0:T(8,128)(2,1)S(1)}, u32[]{:S(2)}, u32[]{:S(2)}) collective-permute-start(bf16[2,80,256]{2,1,0:T(8,128)(2,1)S(1)} %get-tuple-element.48), channel_id=1, source_target_pairs={{0,32},{32,64},{64,96},{96,128},{128,160},{160,192},{192,224},{1,3... | collective-permute-start | bytes 245768 | tf_op jit(solution)/shard_map/ppermute | solution.py:442
  68.6 8.7 %collective-permute-start.9 = (bf16[2,80,256]{2,1,0:T(8,128)(2,1)S(1)}, bf16[2,80,256]{2,1,0:T(8,128)(2,1)S(1)}, u32[]{:S(2)}, u32[]{:S(2)}) collective-permute-start(bf16[2,80,256]{2,1,0:T(8,128)(2,1)S(1)} %get-tuple-element.50), channel_id=1, source_target_pairs={{32,0},{64,32},{96,64},{128,96},{160,128},{192,160},{224,192},{33,... | collective-permute-start | bytes 245768 | tf_op jit(solution)/shard_map/ppermute | solution.py:443
  77.6 5.1 %collective-permute-start.10 = (f32[80,128]{1,0:T(8,128)S(1)}, f32[80,128]{1,0:T(8,128)S(1)}, u32[]{:S(2)}, u32[]{:S(2)}) collective-permute-start(f32[80,128]{1,0:T(8,128)S(1)} %get-tuple-element.55), channel_id=1, source_target_pairs={{0,1},{1,2},{2,3},{3,4},{4,5},{5,6},{6,7},{7,0},{8,9},{9,10},{10,1... | collective-permute-start | bytes 122888 | tf_op jit(solution)/shard_map/ppermute | solution.py:446
  77.8 4.9 %collective-permute-start.11 = (f32[80,128]{1,0:T(8,128)S(1)}, f32[80,128]{1,0:T(8,128)S(1)}, u32[]{:S(2)}, u32[]{:S(2)}) collective-permute-start(f32[80,128]{1,0:T(8,128)S(1)} %get-tuple-element.56), channel_id=1, source_target_pairs={{1,0},{2,1},{3,2},{4,3},{5,4},{6,5},{7,6},{0,7},{9,8},{10,9},{11,1... | collective-permute-start | bytes 122888 | tf_op jit(solution)/shard_map/ppermute | solution.py:447
